TPU v7x, 32 devices: a whole 2x2x4 slice. The times are simulated.
32 devices in a mesh: dp: 8 (over z, y), tensor: 4 (over x, core).
Axes of the slice: x: 2, y: 2, z: 4, core: 2. Of those that a mesh axis runs over, the one named last changes fastest.
Arguments:
- tokens: bfloat16 [4096, 2048], P(('dp', 'tensor')), may hold values from -6 to 6
- norm_gain: bfloat16 [2048], P('dp'), may hold values from 0.5 to 1.5
- q_weight: bfloat16 [2048, 2048], P('dp', 'tensor'), may hold values from -0.5 to 0.5
- key_matrix: bfloat16 [2048, 512], P('dp', 'tensor'), may hold values from -0.5 to 0.5
- value_matrix: bfloat16 [2048, 512], P('dp', 'tensor'), may hold values from -0.125 to 0.125
- o_weight: bfloat16 [2048, 2048], P('tensor', 'dp'), may hold values from -3 to 3
- mlp_gain: bfloat16 [2048], P('dp'), may hold values from 0.5 to 1.5
- gate_weight: bfloat16 [2048, 8192], P('dp', 'tensor'), may hold values from -0.125 to 0.125
- up_weight: bfloat16 [2048, 8192], P('dp', 'tensor'), may hold values from -0.125 to 0.125
- down_weight: bfloat16 [8192, 2048], P('tensor', 'dp'), may hold values from -0.25 to 0.25
- parents: int32 [16], replicated, may hold values from 0 to 15, as said below
- out_grad: bfloat16 [4096, 2048], P(('dp', 'tensor')), may hold values from -6 to 6
Outputs:
- mixed: bfloat16 [4096, 2048], P(('dp', 'tensor'))
- grad_tokens: bfloat16 [4096, 2048], P(('dp', 'tensor'))
- grad_norm_gain: float32 [2048], P('dp')
- grad_q_weight: float32 [2048, 2048], P('dp', 'tensor')
- grad_k_weight: float32 [2048, 512], P('dp', 'tensor')
- grad_v_weight: float32 [2048, 512], P('dp', 'tensor')
- grad_o_weight: float32 [2048, 2048], P('tensor', 'dp')
- grad_mlp_gain: float32 [2048], P('dp')
- grad_gate_weight: float32 [2048, 8192], P('dp', 'tensor')
- grad_up_weight: float32 [2048, 8192], P('dp', 'tensor')
- grad_down_weight: float32 [8192, 2048], P('tensor', 'dp')
Inputs may be any that keep to these rules, and one draw needn't show every extreme that they name: parents[s] is the segment that segment s continues; a root names itself. Segments of 256 tokens form trees: a chain of up to 8 trunk segments, up to 4 branch segments continuing the trunk's last, and up to 2 leaf segments on each branch; from any segment the root is reached in at most 9 steps. Trees are filled in that order and the last one may be cut.
All inputs are finite; a program needn't handle non-finite values.
Results may differ from a plain program's by a relative error of at most 0.025.
Values may be sent and summed in bfloat16 or wider, within the bound.
No kernel may reach another device: no remote copies, remote signals or barrier semaphores. Data moves between devices by JAX's collectives and lax.ppermute only.
A program may use at most 192 MiB of HBM per device.

v0:
```python
import jax
import jax.numpy as jnp
from jax import lax
from jax.sharding import PartitionSpec as P

HEAD_SIZE = 64
SEG = 256


attn_scale = 0.015625
branch_scale = 0.22
norm_eps = 1e-05
rope_base = 10000000.0
masked_score = -1e30


def ancestry(parents):
    seg_total = parents.shape[0]
    seg_ids = jnp.arange(seg_total, dtype=jnp.int32)
    current = seg_ids
    lineage = current[:, None] == seg_ids[None, :]
    for repeat in range(9):
        current = parents[current]
        lineage = lineage | (current[:, None] == seg_ids[None, :])
    depth = jnp.sum(lineage.astype(jnp.int32), axis=1) - 1
    return (lineage, depth)


def rope_tables(position, head_dim):
    half_dim = head_dim // 2
    exponent = jnp.arange(half_dim, dtype=jnp.float32) * (2.0 / head_dim)
    inverse = jnp.power(rope_base, -exponent)
    angles = position.astype(jnp.float32)[:, None] * inverse[None, :]
    return (jnp.cos(angles), jnp.sin(angles))


def rotary_apply(value_rows, cosine_table, sine_table, direction):
    half_dim = value_rows.shape[-1] // 2
    first_half = value_rows[..., :half_dim]
    second = value_rows[..., half_dim:]
    cos_part = cosine_table[:, None, :]
    sin_part = sine_table[:, None, :] * direction
    return jnp.concatenate(
        [first_half * cos_part - second * sin_part, second * cos_part + first_half * sin_part],
        axis=-1,
    )


def unchanged(inner_state):
    return inner_state


def local(
    tokens,
    norm_gain,
    q_weight,
    key_matrix,
    value_matrix,
    o_weight,
    mlp_gain,
    gate_weight,
    up_weight,
    down_weight,
    parents,
    out_grad,
):
    tensor_size = lax.axis_size("tensor")
    dp_size = lax.axis_size("dp")
    local_rows = tokens.shape[0]
    group_rows = local_rows * tensor_size
    total_rows = group_rows * dp_size
    q_local = q_weight.shape[1] // HEAD_SIZE
    kv_local = key_matrix.shape[1] // HEAD_SIZE
    per_group = q_local // kv_local
    kv_cols = kv_local * HEAD_SIZE
    lineage, depth = ancestry(parents)
    group_start = lax.axis_index("dp") * group_rows
    query_index = group_start + jnp.arange(group_rows, dtype=jnp.int32)
    query_seg = query_index // SEG
    position = depth[query_seg] * SEG + query_index % SEG
    cosine_table, sine_table = rope_tables(position, HEAD_SIZE)
    seg_count = group_rows // SEG
    query_lineage = lax.dynamic_slice_in_dim(lineage, group_start // SEG, seg_count, 0)
    key_block = group_rows * min(dp_size, max(1, 1024 // group_rows))
    block_count = total_rows // key_block
    block_segs = key_block // SEG

    def block_mask(key_start):
        seg_allowed = lax.dynamic_slice_in_dim(query_lineage, key_start // SEG, block_segs, 1)
        widened = jnp.broadcast_to(
            seg_allowed[:, None, :, None], (seg_count, SEG, block_segs, SEG)
        ).reshape(group_rows, key_block)
        key_index = key_start + jnp.arange(key_block, dtype=jnp.int32)
        causal = (query_seg[:, None] != (key_index // SEG)[None, :]) | (
            key_index[None, :] <= query_index[:, None]
        )
        return (widened & causal, jnp.any(seg_allowed))

    def block_scores(query_heads, key_slab, allowed):
        raw_scores = jnp.einsum(
            "qhgd,khd->hgqk", query_heads, key_slab, preferred_element_type=jnp.float32
        )
        return jnp.where(allowed[None, None], raw_scores * attn_scale, masked_score)

    weights = (
        lax.all_gather(norm_gain, "dp", axis=0, tiled=True),
        lax.all_gather(q_weight, "dp", axis=0, tiled=True),
        lax.all_gather(key_matrix, "dp", axis=0, tiled=True),
        lax.all_gather(value_matrix, "dp", axis=0, tiled=True),
        lax.all_gather(o_weight, "dp", axis=1, tiled=True),
        lax.all_gather(mlp_gain, "dp", axis=0, tiled=True),
        lax.all_gather(gate_weight, "dp", axis=0, tiled=True),
        lax.all_gather(up_weight, "dp", axis=0, tiled=True),
        lax.all_gather(down_weight, "dp", axis=1, tiled=True),
    )
    gain_one, q_full, k_full, v_full, o_full, gain_two, gate_full, up_full, down_full = weights
    inputs = tokens.astype(jnp.float32)
    inv_one = lax.rsqrt(jnp.mean(inputs * inputs, axis=-1, keepdims=True) + norm_eps)
    normed_one = inputs * inv_one
    hidden_one = (normed_one * gain_one.astype(jnp.float32)).astype(jnp.bfloat16)
    rows_one = lax.all_gather(hidden_one, "tensor", axis=0, tiled=True)
    query_proj = jnp.dot(rows_one, q_full, preferred_element_type=jnp.float32)
    key_projected = jnp.dot(rows_one, k_full, preferred_element_type=jnp.float32)
    value_proj = jnp.dot(rows_one, v_full, preferred_element_type=jnp.float32)
    query_rows = rotary_apply(
        query_proj.reshape(group_rows, q_local, HEAD_SIZE), cosine_table, sine_table, 1.0
    ).astype(jnp.bfloat16)
    key_rows = (
        rotary_apply(
            key_projected.reshape(group_rows, kv_local, HEAD_SIZE), cosine_table, sine_table, 1.0
        )
        .astype(jnp.bfloat16)
        .reshape(group_rows, kv_cols)
    )
    value_rows = value_proj.astype(jnp.bfloat16)
    all_keys, all_values = (
        lax.all_gather(key_rows, "dp", axis=0, tiled=True),
        lax.all_gather(value_rows, "dp", axis=0, tiled=True),
    )
    query_heads = query_rows.reshape(group_rows, kv_local, per_group, HEAD_SIZE)

    def lse_turn(block_id, loop_state):
        key_start = block_id * key_block
        allowed, visited = block_mask(key_start)

        def lse_visit_block(inner_state):
            row_max, row_total = inner_state
            key_slab = lax.dynamic_slice_in_dim(all_keys, key_start, key_block, 0).reshape(
                key_block, kv_local, HEAD_SIZE
            )
            scores = block_scores(query_heads, key_slab, allowed)
            new_max = jnp.maximum(row_max, jnp.max(scores, axis=-1))
            exp_terms = jnp.where(allowed[None, None], jnp.exp(scores - new_max[..., None]), 0.0)
            return (new_max, row_total * jnp.exp(row_max - new_max) + jnp.sum(exp_terms, axis=-1))

        return lax.cond(visited, lse_visit_block, unchanged, loop_state)

    stat_shape = (kv_local, per_group, group_rows)
    row_max, row_total = lax.fori_loop(
        0,
        block_count,
        lse_turn,
        (jnp.full(stat_shape, masked_score, jnp.float32), jnp.zeros(stat_shape, jnp.float32)),
    )
    log_total = row_max + jnp.log(row_total)

    def out_turn(block_id, loop_state):
        key_start = block_id * key_block
        allowed, visited = block_mask(key_start)

        def out_visit_block(inner_state):
            key_slab = lax.dynamic_slice_in_dim(all_keys, key_start, key_block, 0).reshape(
                key_block, kv_local, HEAD_SIZE
            )
            value_slab = lax.dynamic_slice_in_dim(all_values, key_start, key_block, 0).reshape(
                key_block, kv_local, HEAD_SIZE
            )
            scores = block_scores(query_heads, key_slab, allowed)
            probabilities = jnp.where(
                allowed[None, None], jnp.exp(scores - log_total[..., None]), 0.0
            ).astype(jnp.bfloat16)
            return inner_state + jnp.einsum(
                "hgqk,khd->hgqd", probabilities, value_slab, preferred_element_type=jnp.float32
            )

        return lax.cond(visited, out_visit_block, unchanged, loop_state)

    attended = lax.fori_loop(
        0,
        block_count,
        out_turn,
        jnp.zeros((kv_local, per_group, group_rows, HEAD_SIZE), jnp.float32),
    )
    attn_low = (
        attended.transpose(2, 0, 1, 3).reshape(group_rows, q_local * HEAD_SIZE).astype(jnp.bfloat16)
    )
    attn_part = jnp.dot(attn_low, o_full, preferred_element_type=jnp.float32)
    attn_mine = lax.psum_scatter(
        attn_part.astype(jnp.bfloat16), "tensor", scatter_dimension=0, tiled=True
    ).astype(jnp.float32)
    middle = inputs + branch_scale * attn_mine
    inv_two = lax.rsqrt(jnp.mean(middle * middle, axis=-1, keepdims=True) + norm_eps)
    normed_two = middle * inv_two
    hidden_two = (normed_two * gain_two.astype(jnp.float32)).astype(jnp.bfloat16)
    rows_two = lax.all_gather(hidden_two, "tensor", axis=0, tiled=True)
    gate_pre = jnp.dot(rows_two, gate_full, preferred_element_type=jnp.float32)
    up_pre = jnp.dot(rows_two, up_full, preferred_element_type=jnp.float32)
    gate_sigmoid = jax.nn.sigmoid(gate_pre)
    activated = (gate_pre * gate_sigmoid * up_pre).astype(jnp.bfloat16)
    mlp_part = jnp.dot(activated, down_full, preferred_element_type=jnp.float32)
    mlp_mine = lax.psum_scatter(
        mlp_part.astype(jnp.bfloat16), "tensor", scatter_dimension=0, tiled=True
    ).astype(jnp.float32)
    mixed = (middle + branch_scale * mlp_mine).astype(jnp.bfloat16)
    again = (
        lax.all_gather(norm_gain, "dp", axis=0, tiled=True),
        lax.all_gather(q_weight, "dp", axis=0, tiled=True),
        lax.all_gather(key_matrix, "dp", axis=0, tiled=True),
        lax.all_gather(value_matrix, "dp", axis=0, tiled=True),
        lax.all_gather(o_weight, "dp", axis=1, tiled=True),
        lax.all_gather(mlp_gain, "dp", axis=0, tiled=True),
        lax.all_gather(gate_weight, "dp", axis=0, tiled=True),
        lax.all_gather(up_weight, "dp", axis=0, tiled=True),
        lax.all_gather(down_weight, "dp", axis=1, tiled=True),
        lax.all_gather(key_rows, "dp", axis=0, tiled=True),
        lax.all_gather(value_rows, "dp", axis=0, tiled=True),
    )
    (
        gain_one,
        q_full,
        k_full,
        v_full,
        o_full,
        gain_two,
        gate_full,
        up_full,
        down_full,
        all_keys,
        all_values,
    ) = again
    grad_out = out_grad.astype(jnp.float32)
    grad_mlp = (branch_scale * grad_out).astype(jnp.bfloat16)
    grad_mlp_rows = lax.all_gather(grad_mlp, "tensor", axis=0, tiled=True)
    grad_hidden = jnp.einsum(
        "td,fd->tf", grad_mlp_rows, down_full, preferred_element_type=jnp.float32
    )
    grad_down = jnp.einsum(
        "tf,td->fd", activated, grad_mlp_rows, preferred_element_type=jnp.float32
    )
    grad_gate_act = (
        grad_hidden * up_pre * gate_sigmoid * (1.0 + gate_pre * (1.0 - gate_sigmoid))
    ).astype(jnp.bfloat16)
    grad_up_act = (grad_hidden * gate_pre * gate_sigmoid).astype(jnp.bfloat16)
    grad_gate = jnp.einsum("td,tf->df", rows_two, grad_gate_act, preferred_element_type=jnp.float32)
    grad_up = jnp.einsum("td,tf->df", rows_two, grad_up_act, preferred_element_type=jnp.float32)
    input_part = jnp.einsum(
        "tf,df->td", grad_gate_act, gate_full, preferred_element_type=jnp.float32
    ) + jnp.einsum("tf,df->td", grad_up_act, up_full, preferred_element_type=jnp.float32)
    grad_rows_two = lax.psum_scatter(
        input_part.astype(jnp.bfloat16), "tensor", scatter_dimension=0, tiled=True
    ).astype(jnp.float32)
    gain_two_part = jnp.sum(grad_rows_two * normed_two, axis=0)
    grad_normed_two = grad_rows_two * gain_two.astype(jnp.float32)
    grad_middle = grad_out + inv_two * (
        grad_normed_two
        - normed_two * jnp.mean(grad_normed_two * normed_two, axis=-1, keepdims=True)
    )
    grad_attn = (branch_scale * grad_middle).astype(jnp.bfloat16)
    grad_attn_rows = lax.all_gather(grad_attn, "tensor", axis=0, tiled=True)
    grad_o = jnp.einsum("tc,td->cd", attn_low, grad_attn_rows, preferred_element_type=jnp.float32)
    grad_heads = (
        jnp.einsum("td,cd->tc", grad_attn_rows, o_full, preferred_element_type=jnp.float32)
        .astype(jnp.bfloat16)
        .reshape(group_rows, kv_local, per_group, HEAD_SIZE)
    )
    delta_rows = jnp.einsum("qhgd,hgqd->hgq", grad_heads.astype(jnp.float32), attended)

    def back_turn(block_id, loop_state):
        key_start = block_id * key_block
        allowed, visited = block_mask(key_start)

        def back_visit_block(inner_state):
            grad_query, grad_kv = inner_state
            key_slab = lax.dynamic_slice_in_dim(all_keys, key_start, key_block, 0).reshape(
                key_block, kv_local, HEAD_SIZE
            )
            value_slab = lax.dynamic_slice_in_dim(all_values, key_start, key_block, 0).reshape(
                key_block, kv_local, HEAD_SIZE
            )
            scores = block_scores(query_heads, key_slab, allowed)
            probabilities = jnp.where(
                allowed[None, None], jnp.exp(scores - log_total[..., None]), 0.0
            )
            grad_probs = jnp.einsum(
                "qhgd,khd->hgqk", grad_heads, value_slab, preferred_element_type=jnp.float32
            )
            grad_scores = (
                probabilities * (grad_probs - delta_rows[..., None]) * attn_scale
            ).astype(jnp.bfloat16)
            grad_query = grad_query + jnp.einsum(
                "hgqk,khd->hgqd", grad_scores, key_slab, preferred_element_type=jnp.float32
            )
            key_part = jnp.einsum(
                "hgqk,qhgd->khd", grad_scores, query_heads, preferred_element_type=jnp.float32
            ).reshape(key_block, kv_cols)
            value_part = jnp.einsum(
                "hgqk,qhgd->khd",
                probabilities.astype(jnp.bfloat16),
                grad_heads,
                preferred_element_type=jnp.float32,
            ).reshape(key_block, kv_cols)
            current = lax.dynamic_slice_in_dim(grad_kv, key_start, key_block, 0)
            grad_kv = lax.dynamic_update_slice_in_dim(
                grad_kv, current + jnp.concatenate([key_part, value_part], axis=1), key_start, 0
            )
            return (grad_query, grad_kv)

        return lax.cond(visited, back_visit_block, unchanged, loop_state)

    grad_query, grad_kv = lax.fori_loop(
        0,
        block_count,
        back_turn,
        (
            jnp.zeros((kv_local, per_group, group_rows, HEAD_SIZE), jnp.float32),
            jnp.zeros((total_rows, 2 * kv_cols), jnp.float32),
        ),
    )
    grad_kv_mine = lax.psum_scatter(
        grad_kv.astype(jnp.bfloat16), "dp", scatter_dimension=0, tiled=True
    ).astype(jnp.float32)
    grad_keys = (
        rotary_apply(
            grad_kv_mine[:, :kv_cols].reshape(group_rows, kv_local, HEAD_SIZE),
            cosine_table,
            sine_table,
            -1.0,
        )
        .astype(jnp.bfloat16)
        .reshape(group_rows, kv_cols)
    )
    grad_values = grad_kv_mine[:, kv_cols:].astype(jnp.bfloat16)
    grad_queries = (
        rotary_apply(
            grad_query.transpose(2, 0, 1, 3).reshape(group_rows, q_local, HEAD_SIZE),
            cosine_table,
            sine_table,
            -1.0,
        )
        .astype(jnp.bfloat16)
        .reshape(group_rows, q_local * HEAD_SIZE)
    )
    grad_q = jnp.einsum("td,tc->dc", rows_one, grad_queries, preferred_element_type=jnp.float32)
    grad_k = jnp.einsum("td,tc->dc", rows_one, grad_keys, preferred_element_type=jnp.float32)
    grad_v = jnp.einsum("td,tc->dc", rows_one, grad_values, preferred_element_type=jnp.float32)
    input_one = jnp.einsum("tc,dc->td", grad_queries, q_full, preferred_element_type=jnp.float32)
    input_one = input_one + jnp.einsum(
        "tc,dc->td", grad_keys, k_full, preferred_element_type=jnp.float32
    )
    input_one = input_one + jnp.einsum(
        "tc,dc->td", grad_values, v_full, preferred_element_type=jnp.float32
    )
    grad_rows_one = lax.psum_scatter(
        input_one.astype(jnp.bfloat16), "tensor", scatter_dimension=0, tiled=True
    ).astype(jnp.float32)
    gain_one_part = jnp.sum(grad_rows_one * normed_one, axis=0)
    grad_normed_one = grad_rows_one * gain_one.astype(jnp.float32)
    grad_inputs = grad_middle + inv_one * (
        grad_normed_one
        - normed_one * jnp.mean(grad_normed_one * normed_one, axis=-1, keepdims=True)
    )
    summed = (
        lax.psum_scatter(
            gain_one_part.astype(jnp.bfloat16), "dp", scatter_dimension=0, tiled=True
        ).astype(jnp.float32),
        lax.psum_scatter(grad_q.astype(jnp.bfloat16), "dp", scatter_dimension=0, tiled=True).astype(
            jnp.float32
        ),
        lax.psum_scatter(grad_k.astype(jnp.bfloat16), "dp", scatter_dimension=0, tiled=True).astype(
            jnp.float32
        ),
        lax.psum_scatter(grad_v.astype(jnp.bfloat16), "dp", scatter_dimension=0, tiled=True).astype(
            jnp.float32
        ),
        lax.psum_scatter(grad_o.astype(jnp.bfloat16), "dp", scatter_dimension=1, tiled=True).astype(
            jnp.float32
        ),
        lax.psum_scatter(
            gain_two_part.astype(jnp.bfloat16), "dp", scatter_dimension=0, tiled=True
        ).astype(jnp.float32),
        lax.psum_scatter(
            grad_gate.astype(jnp.bfloat16), "dp", scatter_dimension=0, tiled=True
        ).astype(jnp.float32),
        lax.psum_scatter(
            grad_up.astype(jnp.bfloat16), "dp", scatter_dimension=0, tiled=True
        ).astype(jnp.float32),
        lax.psum_scatter(
            grad_down.astype(jnp.bfloat16), "dp", scatter_dimension=1, tiled=True
        ).astype(jnp.float32),
    )
    gain_sums = lax.psum((summed[0], summed[5]), "tensor")
    return (
        mixed,
        grad_inputs.astype(jnp.bfloat16),
        gain_sums[0],
        summed[1],
        summed[2],
        summed[3],
        summed[4],
        gain_sums[1],
        summed[6],
        summed[7],
        summed[8],
    )


def solution(mesh):
    in_specs = (
        P(("dp", "tensor"), None),
        P("dp"),
        P("dp", "tensor"),
        P("dp", "tensor"),
        P("dp", "tensor"),
        P("tensor", "dp"),
        P("dp"),
        P("dp", "tensor"),
        P("dp", "tensor"),
        P("tensor", "dp"),
        P(),
        P(("dp", "tensor"), None),
    )
    out_specs = (
        P(("dp", "tensor"), None),
        P(("dp", "tensor"), None),
        P("dp"),
        P("dp", "tensor"),
        P("dp", "tensor"),
        P("dp", "tensor"),
        P("tensor", "dp"),
        P("dp"),
        P("dp", "tensor"),
        P("dp", "tensor"),
        P("tensor", "dp"),
    )
    return jax.shard_map(local, mesh=mesh, in_specs=in_specs, out_specs=out_specs, check_vma=False)
```

profile of v0, /device:TPU:0, one launch (start us, length us, event | category | flops | bytes accessed | tf_op | source)
XLA Modules:
  0.0 1874.4 jit_solution(6985771121452716310)
XLA Ops:
  41.2 32.0 %all_gather.61 = bf16[2048,128]{1,0:T(8,128)(2,1)S(1)} all-gather(bf16[256,128]{1,0:T(8,128)(2,1)S(1)} %copy-done.26), channel_id=1, replica_groups=mesh['dp'=8,'tensor'=4] {'dp'}, dimensions={0}, use_global_device_ids=true | all-gather | bytes 589824 | tf_op jit(solution)/shard_map/all_gather | solution.py:109
  88.5 32.1 %all_gather.58 = bf16[2048,128]{1,0:T(8,128)(2,1)S(1)} all-gather(bf16[256,128]{1,0:T(8,128)(2,1)S(1)} %copy-done.27), channel_id=1, replica_groups=mesh['dp'=8,'tensor'=4] {'dp'}, dimensions={0}, use_global_device_ids=true | all-gather | bytes 589824 | tf_op jit(solution)/shard_map/all_gather | solution.py:108
  126.8 26.5 %all-gather.20.cloned.1.call-done = bf16[4096,128]{1,0:T(8,128)(2,1)} async-done(((bf16[512,128]{1,0:T(8,128)(2,1)}), bf16[4096,128]{1,0:T(8,128)(2,1)}) %all-gather.20.cloned.1.call-update) | async-done | bytes 1048592 | tf_op jit(solution)/shard_map/all_gather | solution.py:138
  154.8 39.3 %all-gather.16.cloned.1.call-done = bf16[4096,128]{0,1:T(8,128)(2,1)} async-done(((bf16[512,128]{0,1:T(8,128)(2,1)}), bf16[4096,128]{0,1:T(8,128)(2,1)}) %all-gather.16.cloned.1.call-update) | async-done | bytes 1048592 | tf_op jit(solution)/shard_map/all_gather | solution.py:137
  194.1 45.4 %while.61 = (s32[]{:T(128)}, f32[2,4,512]{2,1,0:T(4,128)S(1)}, f32[2,4,512]{2,1,0:T(4,128)S(1)}, pred[2,16]{1,0:T(4,128)(4,1)S(1)}, bf16[4096,128]{0,1:T(8,128)(...) while((s32[]{:T(128)}, f32[2,4,512]{2,1,0:T(4,128)S(1)}, ...), condition=%wide.region_8.9_spmd.clone.clone, body=%wide.region_2.8_spmd.clone.clone.sunk | while | flops 572558336 | bytes 39849584 | solution.py:159
  240.7 50.8 %while.62 = (s32[]{:T(128)}, f32[2,4,512,64]{2,3,1,0:T(8,128)}, pred[2,16]{1,0:T(4,128)(4,1)S(1)}, bf16[4096,128]{0,1:T(8,128)(2,1)}, bf16[512,2,4,64]{0,3,2,1:T...) while((s32[]{:T(128)}, f32[2,4,512,64]{2,3,1,0:T(8,128)}, ...), condition=%wide.region_13.14_spmd.clone.clone, body=%wide.region_9.13_spmd.clone.clone.sunk | while | flops 1097100288 | bytes 8457825 | solution.py:188
  354.3 127.3 %all-gather.28.cloned.1.call-done = bf16[2048,2048]{1,0:T(8,128)(2,1)} async-done(((bf16[256,2048]{1,0:T(8,128)(2,1)}), bf16[2048,2048]{1,0:T(8,128)(2,1)}) %all-gather.28.cloned.1.call-update) | async-done | bytes 8388624 | tf_op jit(solution)/shard_map/all_gather | solution.py:113
  492.1 115.0 %all-gather.26.cloned.1.call-done = bf16[2048,2048]{1,0:T(8,128)(2,1)} async-done(((bf16[256,2048]{1,0:T(8,128)(2,1)}), bf16[2048,2048]{1,0:T(8,128)(2,1)}) %all-gather.26.cloned.1.call-update) | async-done | bytes 8388624 | tf_op jit(solution)/shard_map/all_gather | solution.py:112
  630.0 127.7 %all-gather.30.cloned.1.call-done = bf16[2048,2048]{1,0:T(8,128)(2,1)} async-done(((bf16[2048,256]{1,0:T(8,128)(2,1)}), bf16[2048,2048]{1,0:T(8,128)(2,1)}) %all-gather.30.cloned.1.call-update) | async-done | bytes 8388624 | tf_op jit(solution)/shard_map/all_gather | solution.py:114
  783.6 29.7 %reduce-scatter.17.cloned.1.call-done = bf16[128,2048]{1,0:T(8,128)(2,1)} async-done(((bf16[512,2048]{1,0:T(8,128)(2,1)}), bf16[128,2048]{1,0:T(8,128)(2,1)}) %reduce-scatter.17.cloned.1.call-update) | async-done | bytes 524304 | tf_op jit(solution)/shard_map/reduce_scatter | solution.py:259
  818.0 22.7 %all-gather.34.cloned.1.call-done = bf16[512,2048]{1,0:T(8,128)(2,1)} async-done(((bf16[128,2048]{1,0:T(8,128)(2,1)}), bf16[512,2048]{1,0:T(8,128)(2,1)}) %all-gather.34.cloned.1.call-update) | async-done | bytes 2097168 | tf_op jit(solution)/shard_map/all_gather | solution.py:269
  847.9 150.7 %while.63 = (s32[]{:T(128)}, f32[2,4,512,64]{2,3,1,0:T(8,128)S(1)}, f32[4096,256]{0,1:T(8,128)}, pred[2,16]{1,0:T(4,128)(4,1)S(1)}, bf16[4096,128]{0,1:T(8,128)(...) while((s32[]{:T(128)}, f32[2,4,512,64]{2,3,1,0:T(8,128)S(1)}, ...), condition=%wide.region_23.24_spmd.clone.clone, body=%wide.region_19.23_spmd.clone.clone.sunk | while | flops 2741791744 | bytes 90541744 | solution.py:320
  849.5 36.1 %conditional.14 = ((f32[2,4,512,64]{2,3,1,0:T(8,128)S(1)}, f32[4096,256]{0,1:T(8,128)})) conditional(s32[]{:T(128)} %convert_element_type.408, (f32[2,4,512,64]{2,3,1,0:T(8,128)S(1)}, f32[4096,256]{0,1:T(8,128)}) %tuple.253, (pred[2,4]{1,0:T(4,128)(4,1)S(1)}, s32[512]{0:T(512)S(1)}, s32[]{:T(128)}, s32[1,1024]{1,0:T(1,128)S(1)}, s32[]{:T(128)}, ...), branch_computations={%region_21.21_spmd, %region_22.22_spmd.clone} | conditional | flops 2741784576 | bytes 90528344 | solution.py:318
  887.1 36.2 %conditional.14 = ((f32[2,4,512,64]{2,3,1,0:T(8,128)S(1)}, f32[4096,256]{0,1:T(8,128)})) conditional(s32[]{:T(128)} %convert_element_type.408, (f32[2,4,512,64]{2,3,1,0:T(8,128)S(1)}, f32[4096,256]{0,1:T(8,128)}) %tuple.253, (pred[2,4]{1,0:T(4,128)(4,1)S(1)}, s32[512]{0:T(512)S(1)}, s32[]{:T(128)}, s32[1,1024]{1,0:T(1,128)S(1)}, s32[]{:T(128)}, ...), branch_computations={%region_21.21_spmd, %region_22.22_spmd.clone} | conditional | flops 2741784576 | bytes 90528344 | solution.py:318
  924.7 36.2 %conditional.14 = ((f32[2,4,512,64]{2,3,1,0:T(8,128)S(1)}, f32[4096,256]{0,1:T(8,128)})) conditional(s32[]{:T(128)} %convert_element_type.408, (f32[2,4,512,64]{2,3,1,0:T(8,128)S(1)}, f32[4096,256]{0,1:T(8,128)}) %tuple.253, (pred[2,4]{1,0:T(4,128)(4,1)S(1)}, s32[512]{0:T(512)S(1)}, s32[]{:T(128)}, s32[1,1024]{1,0:T(1,128)S(1)}, s32[]{:T(128)}, ...), branch_computations={%region_21.21_spmd, %region_22.22_spmd.clone} | conditional | flops 2741784576 | bytes 90528344 | solution.py:318
  962.4 36.2 %conditional.14 = ((f32[2,4,512,64]{2,3,1,0:T(8,128)S(1)}, f32[4096,256]{0,1:T(8,128)})) conditional(s32[]{:T(128)} %convert_element_type.408, (f32[2,4,512,64]{2,3,1,0:T(8,128)S(1)}, f32[4096,256]{0,1:T(8,128)}) %tuple.253, (pred[2,4]{1,0:T(4,128)(4,1)S(1)}, s32[512]{0:T(512)S(1)}, s32[]{:T(128)}, s32[1,1024]{1,0:T(1,128)S(1)}, s32[]{:T(128)}, ...), branch_computations={%region_21.21_spmd, %region_22.22_spmd.clone} | conditional | flops 2741784576 | bytes 90528344 | solution.py:318
  1011.5 59.1 %reduce-scatter.19.cloned.1.call-done = bf16[512,256]{0,1:T(8,128)(2,1)} async-done(((bf16[4096,256]{0,1:T(8,128)(2,1)}), bf16[512,256]{0,1:T(8,128)(2,1)}) %reduce-scatter.19.cloned.1.call-update) | async-done | bytes 262160 | tf_op jit(solution)/shard_map/reduce_scatter | solution.py:329
  1142.8 68.3 %reduce-scatter.23.cloned.1.call-done = bf16[256,512]{1,0:T(8,128)(2,1)} async-done(((bf16[2048,512]{1,0:T(8,128)(2,1)}), bf16[256,512]{1,0:T(8,128)(2,1)}) %reduce-scatter.23.cloned.1.call-update) | async-done | bytes 262160 | tf_op jit(solution)/shard_map/reduce_scatter | solution.py:376
  1212.9 62.4 %reduce-scatter.25.cloned.1.call-done = bf16[256,128]{1,0:T(8,128)(2,1)} async-done(((bf16[2048,128]{1,0:T(8,128)(2,1)}), bf16[256,128]{1,0:T(8,128)(2,1)}) %reduce-scatter.25.cloned.1.call-update) | async-done | bytes 65552 | tf_op jit(solution)/shard_map/reduce_scatter | solution.py:379
  1276.8 63.0 %reduce-scatter.27.cloned.1.call-done = bf16[256,128]{1,0:T(8,128)(2,1)} async-done(((bf16[2048,128]{1,0:T(8,128)(2,1)}), bf16[256,128]{1,0:T(8,128)(2,1)}) %reduce-scatter.27.cloned.1.call-update) | async-done | bytes 65552 | tf_op jit(solution)/shard_map/reduce_scatter | solution.py:382
  1341.4 32.1 %reduce-scatter.21.cloned.1.call-done = bf16[128,2048]{1,0:T(8,128)(2,1)} async-done(((bf16[512,2048]{1,0:T(8,128)(2,1)}), bf16[128,2048]{1,0:T(8,128)(2,1)}) %reduce-scatter.21.cloned.1.call-update) | async-done | bytes 524304 | tf_op jit(solution)/shard_map/reduce_scatter | solution.py:363
  1411.3 149.5 %reduce-scatter.33.cloned.1.call-done = bf16[256,2048]{1,0:T(8,128)(2,1)} async-done(((bf16[2048,2048]{1,0:T(8,128)(2,1)}), bf16[256,2048]{1,0:T(8,128)(2,1)}) %reduce-scatter.33.cloned.1.call-update) | async-done | bytes 1048592 | tf_op jit(solution)/shard_map/reduce_scatter | solution.py:394
  1563.6 149.3 %reduce-scatter.31.cloned.1.call-done = bf16[256,2048]{1,0:T(8,128)(2,1)} async-done(((bf16[2048,2048]{1,0:T(8,128)(2,1)}), bf16[256,2048]{1,0:T(8,128)(2,1)}) %reduce-scatter.31.cloned.1.call-update) | async-done | bytes 1048592 | tf_op jit(solution)/shard_map/reduce_scatter | solution.py:391
  1715.7 149.3 %reduce-scatter.35.cloned.1.call-done = bf16[2048,256]{1,0:T(8,128)(2,1)} async-done(((bf16[2048,2048]{1,0:T(8,128)(2,1)}), bf16[2048,256]{1,0:T(8,128)(2,1)}) %reduce-scatter.35.cloned.1.call-update) | async-done | bytes 1048592 | tf_op jit(solution)/shard_map/reduce_scatter | solution.py:397
  (461 shorter events, 647.8 us)
Async XLA Ops:
  7.2 66.0 %all-gather.14.cloned.1.call-start = ((), (), s32[]{:S(2)}) async-start(), calls=%async_computation.12 | async-start | bytes 2621440 | tf_op jit(solution)/shard_map/all_gather | solution.py:121
  34.1 89.6 %all-gather.18.cloned.1.call-start = ((), (), s32[]{:S(2)}) async-start(), calls=%async_computation.14 | async-start | bytes 2359296 | tf_op jit(solution)/shard_map/all_gather | solution.py:107
  34.8 118.5 %all-gather.20.cloned.1.call-start = ((), (), s32[]{:S(2)}) async-start(), calls=%async_computation.15 | async-start | bytes 1179648 | tf_op jit(solution)/shard_map/all_gather | solution.py:138
  76.4 117.6 %all-gather.16.cloned.1.call-start = ((), (), s32[]{:S(2)}) async-start(), calls=%async_computation.13 | async-start | bytes 1179648 | tf_op jit(solution)/shard_map/all_gather | solution.py:137
  123.0 170.2 %all-gather.22.cloned.1.call-start = ((), (), s32[]{:S(2)}) async-start(), calls=%async_computation.16 | async-start | bytes 2359296 | tf_op jit(solution)/shard_map/all_gather | solution.py:110
  123.6 204.5 %reduce-scatter.13.cloned.1.call-start = ((), (), s32[]{:S(2)}) async-start(), calls=%async_computation.17 | async-start | bytes 2621440 | tf_op jit(solution)/shard_map/reduce_scatter | solution.py:198
  297.6 56.7 %all-gather.24.cloned.1.call-start = ((), (), s32[]{:S(2)}) async-start(), calls=%async_computation.18 | async-start | bytes 2621440 | tf_op jit(solution)/shard_map/all_gather | solution.py:205
  316.3 499.2 %copy-start.22 = (f32[8,1,256]{2,1,0:T(1,128)}, f32[8,1,256]{2,1,0:T(1,128)S(1)}, u32[]{:S(2)}) copy-start(f32[8,1,256]{2,1,0:T(1,128)S(1)} %convert_element_type.266) | copy-start | bytes 24580
  331.6 150.1 %all-gather.28.cloned.1.call-start = ((), (), s32[]{:S(2)}) async-start(), calls=%async_computation.20 | async-start | bytes 9437184 | tf_op jit(solution)/shard_map/all_gather | solution.py:113
  332.3 274.8 %all-gather.26.cloned.1.call-start = ((), (), s32[]{:S(2)}) async-start(), calls=%async_computation.19 | async-start | bytes 9437184 | tf_op jit(solution)/shard_map/all_gather | solution.py:112
  333.1 296.9 %all-gather.32.cloned.1.call-start = ((), (), s32[]{:S(2)}) async-start(), calls=%async_computation.23 | async-start | bytes 2621440 | tf_op jit(solution)/shard_map/all_gather | solution.py:243
  334.0 423.6 %all-gather.30.cloned.1.call-start = ((), (), s32[]{:S(2)}) async-start(), calls=%async_computation.21 | async-start | bytes 9437184 | tf_op jit(solution)/shard_map/all_gather | solution.py:114
  334.8 478.6 %reduce-scatter.17.cloned.1.call-start = ((), (), s32[]{:S(2)}) async-start(), calls=%async_computation.24 | async-start | bytes 2621440 | tf_op jit(solution)/shard_map/reduce_scatter | solution.py:259
  783.6 57.1 %all-gather.34.cloned.1.call-start = ((), (), s32[]{:S(2)}) async-start(), calls=%async_computation.25 | async-start | bytes 2621440 | tf_op jit(solution)/shard_map/all_gather | solution.py:269
  817.9 252.7 %reduce-scatter.19.cloned.1.call-start = ((), (), s32[]{:S(2)}) async-start(), calls=%async_computation.26 | async-start | bytes 2359296 | tf_op jit(solution)/shard_map/reduce_scatter | solution.py:329
  1002.5 138.6 %reduce-scatter.29.cloned.1.call-start = ((), (), s32[]{:S(2)}) async-start(), calls=%async_computation.31 | async-start | bytes 2359296 | tf_op jit(solution)/shard_map/reduce_scatter | solution.py:385
  1007.2 203.9 %reduce-scatter.23.cloned.1.call-start = ((), (), s32[]{:S(2)}) async-start(), calls=%async_computation.28 | async-start | bytes 2359296 | tf_op jit(solution)/shard_map/reduce_scatter | solution.py:376
  1011.5 263.8 %reduce-scatter.25.cloned.1.call-start = ((), (), s32[]{:S(2)}) async-start(), calls=%async_computation.29 | async-start | bytes 589824 | tf_op jit(solution)/shard_map/reduce_scatter | solution.py:379
  1073.3 266.6 %reduce-scatter.27.cloned.1.call-start = ((), (), s32[]{:S(2)}) async-start(), calls=%async_computation.30 | async-start | bytes 589824 | tf_op jit(solution)/shard_map/reduce_scatter | solution.py:382
  1075.0 298.5 %reduce-scatter.21.cloned.1.call-start = ((), (), s32[]{:S(2)}) async-start(), calls=%async_computation.27 | async-start | bytes 2621440 | tf_op jit(solution)/shard_map/reduce_scatter | solution.py:363
  1081.1 327.0 %reduce-scatter.15.cloned.1.call-start = ((), (), s32[]{:S(2)}) async-start(), calls=%async_computation.22 | async-start | bytes 2621440 | tf_op jit(solution)/shard_map/reduce_scatter | solution.py:211
  1091.2 469.6 %reduce-scatter.33.cloned.1.call-start = ((), (), s32[]{:S(2)}) async-start(), calls=%async_computation.33 | async-start | bytes 9437184 | tf_op jit(solution)/shard_map/reduce_scatter | solution.py:394
  1099.9 613.0 %reduce-scatter.31.cloned.1.call-start = ((), (), s32[]{:S(2)}) async-start(), calls=%async_computation.32 | async-start | bytes 9437184 | tf_op jit(solution)/shard_map/reduce_scatter | solution.py:391
  1108.4 756.6 %reduce-scatter.35.cloned.1.call-start = ((), (), s32[]{:S(2)}) async-start(), calls=%async_computation.34 | async-start | bytes 9437184 | tf_op jit(solution)/shard_map/reduce_scatter | solution.py:397
  (41 other events, 4226.7 us)
Sparse Core Ops, SparseCore 0:
  34.2 19.8 all-gather.13
  56.2 55.7 all-gather.17
  114.6 38.5 all-gather.19
  155.8 38.2 all-gather.15
  196.0 49.9 all-gather.21
  297.7 30.3 reduce-scatter.12
  331.7 22.5 all-gather.23
  356.7 124.9 all-gather.27
  484.0 123.1 all-gather.25
  609.2 20.7 all-gather.31
  632.2 125.3 all-gather.29
  783.7 29.6 reduce-scatter.16
  818.1 22.5 all-gather.33
  1002.6 67.9 reduce-scatter.18
  1074.0 67.0 reduce-scatter.28
  1144.4 66.6 reduce-scatter.22
  1214.3 60.9 reduce-scatter.24
  1278.9 60.9 reduce-scatter.26
  1343.0 30.4 reduce-scatter.20
  1376.6 31.5 reduce-scatter.14
  1411.8 148.9 reduce-scatter.32
  1564.9 147.9 reduce-scatter.30
  1716.5 148.4 reduce-scatter.34
where the time goes:
time: 1890 us; the launch traced here: 1870 us
  waiting for transfers between devices  1290 us (68%)
  matrix products  279 us (15%)
  blocking collectives  133 us (7%)
  other arithmetic  91.7 us (5%)
  local copies, waits for them, and re-layouts  49.3 us (3%)
    reduce_scatter x1, waiting for transfers between devices, local(): lax.psum_scatter(grad_up.astype(jnp.bfloat16), 'dp', scatter_dimension=0,...  149 us
    reduce_scatter x1, waiting for transfers between devices, local(): lax.psum_scatter(grad_down.astype(jnp.bfloat16), 'dp', scatter_dimension=...  149 us
    reduce_scatter x1, waiting for transfers between devices, local(): lax.psum_scatter(grad_gate.astype(jnp.bfloat16), 'dp', scatter_dimension=...  149 us
    all_gather x1, waiting for transfers between devices, local(): lax.all_gather(down_weight, 'dp', axis=1, tiled=True)  128 us
    all_gather x1, waiting for transfers between devices, local(): lax.all_gather(up_weight, 'dp', axis=0, tiled=True)  127 us
    all_gather x1, waiting for transfers between devices, local(): lax.all_gather(gate_weight, 'dp', axis=0, tiled=True)  115 us
    reduce_scatter x1, waiting for transfers between devices, local(): lax.psum_scatter(grad_q.astype(jnp.bfloat16), 'dp', scatter_dimension=0,...  68.3 us
    reduce_scatter x1, waiting for transfers between devices, local(): lax.psum_scatter(grad_v.astype(jnp.bfloat16), 'dp', scatter_dimension=0,...  63 us
  transfers between devices with their start and end apart: 23, of which 20 were waited for; matrix products, arithmetic and copies ran while one was open for 11% of the time, Pallas kernels for 0%

commit v1 on v0

--- a/solution.py
+++ b/solution.py
@@ -44,6 +44,66 @@
         [first_half * cos_part - second * sin_part, second * cos_part + first_half * sin_part],
         axis=-1,
     )
+
+
+def rotated(value, axis, size, step):
+    return lax.ppermute(value, axis, [(i, (i + step) % size) for i in range(size)])
+
+
+def relative_pieces(value, axis, size):
+    return [value] + [rotated(value, axis, size, k) for k in range(1, size)]
+
+
+def natural_pieces(pieces, axis):
+    size = len(pieces)
+    place = lax.axis_index(axis)
+    return [
+        lax.select_n(place, *[pieces[(i - j) % size] for i in range(size)]) for j in range(size)
+    ]
+
+
+def exchanged(value, axis, size, dim):
+    place = lax.axis_index(axis)
+    width = value.shape[dim] // size
+    pieces = []
+    for k in range(size):
+        target = lax.rem(place + k, size)
+        block = lax.dynamic_slice_in_dim(value, target * width, width, dim)
+        pieces.append(block if k == 0 else rotated(block, axis, size, k))
+    return natural_pieces(pieces, axis)
+
+
+def summed_pieces(pieces, axis):
+    size = len(pieces)
+    total = pieces[0].astype(jnp.float32)
+    for k in range(1, size):
+        sent = rotated(pieces[k].astype(jnp.bfloat16), axis, size, -k)
+        total = total + sent.astype(jnp.float32)
+    return total
+
+
+def relative_columns(value, blocks, axis):
+    size = lax.axis_size(axis)
+    place = lax.axis_index(axis)
+    rows = value.shape[0]
+    split = value.reshape(rows, blocks, size, -1)
+    return jnp.concatenate(
+        [
+            lax.dynamic_index_in_dim(
+                split, lax.rem(place - k + size, size), 2, keepdims=False
+            ).reshape(rows, -1)
+            for k in range(size)
+        ],
+        axis=1,
+    )
+
+
+def natural_columns(value, blocks, axis):
+    size = lax.axis_size(axis)
+    rows = value.shape[0]
+    split = value.reshape(rows, size, blocks, -1)
+    parts = natural_pieces([split[:, k] for k in range(size)], axis)
+    return jnp.stack(parts, axis=2).reshape(rows, -1)
 
 
 def unchanged(inner_state):
@@ -64,8 +124,9 @@
     parents,
     out_grad,
 ):
-    tensor_size = lax.axis_size("tensor")
-    dp_size = lax.axis_size("dp")
+    z_size, y_size, x_size = (lax.axis_size(name) for name in ("z", "y", "x"))
+    tensor_size = x_size * lax.axis_size("c")
+    dp_size = z_size * y_size
     local_rows = tokens.shape[0]
     group_rows = local_rows * tensor_size
     total_rows = group_rows * dp_size
@@ -74,7 +135,7 @@
     per_group = q_local // kv_local
     kv_cols = kv_local * HEAD_SIZE
     lineage, depth = ancestry(parents)
-    group_start = lax.axis_index("dp") * group_rows
+    group_start = lax.axis_index(("z", "y")) * group_rows
     query_index = group_start + jnp.arange(group_rows, dtype=jnp.int32)
     query_seg = query_index // SEG
     position = depth[query_seg] * SEG + query_index % SEG
@@ -102,23 +163,28 @@
         )
         return jnp.where(allowed[None, None], raw_scores * attn_scale, masked_score)
 
-    weights = (
-        lax.all_gather(norm_gain, "dp", axis=0, tiled=True),
-        lax.all_gather(q_weight, "dp", axis=0, tiled=True),
-        lax.all_gather(key_matrix, "dp", axis=0, tiled=True),
-        lax.all_gather(value_matrix, "dp", axis=0, tiled=True),
-        lax.all_gather(o_weight, "dp", axis=1, tiled=True),
-        lax.all_gather(mlp_gain, "dp", axis=0, tiled=True),
-        lax.all_gather(gate_weight, "dp", axis=0, tiled=True),
-        lax.all_gather(up_weight, "dp", axis=0, tiled=True),
-        lax.all_gather(down_weight, "dp", axis=1, tiled=True),
-    )
-    gain_one, q_full, k_full, v_full, o_full, gain_two, gate_full, up_full, down_full = weights
+    gains = jnp.stack([norm_gain, mlp_gain])
+    gain_z = jnp.stack(natural_pieces(relative_pieces(gains, "z", z_size), "z"), 1)
+    gain_zy = jnp.stack(natural_pieces(relative_pieces(gain_z, "y", y_size), "y"), 2)
+    gain_one, gain_two = gain_zy.reshape(2, -1)
+    q_full = lax.all_gather(q_weight, ("z", "y"), axis=0, tiled=True)
+    k_full = lax.all_gather(key_matrix, ("z", "y"), axis=0, tiled=True)
+    v_full = lax.all_gather(value_matrix, ("z", "y"), axis=0, tiled=True)
+    o_full = lax.all_gather(o_weight, ("z", "y"), axis=1, tiled=True)
+
+    def hidden_block(weight, feature_dim):
+        own = jnp.concatenate(exchanged(weight, "z", z_size, 1 - feature_dim), axis=feature_dim)
+        full = jnp.concatenate(relative_pieces(own, "y", y_size), axis=feature_dim)
+        return jnp.concatenate(relative_pieces(full, "x", x_size), axis=1 - feature_dim)
+
+    gate_block = hidden_block(gate_weight, 0)
+    up_block = hidden_block(up_weight, 0)
+    down_block = hidden_block(down_weight, 1)
     inputs = tokens.astype(jnp.float32)
     inv_one = lax.rsqrt(jnp.mean(inputs * inputs, axis=-1, keepdims=True) + norm_eps)
     normed_one = inputs * inv_one
     hidden_one = (normed_one * gain_one.astype(jnp.float32)).astype(jnp.bfloat16)
-    rows_one = lax.all_gather(hidden_one, "tensor", axis=0, tiled=True)
+    rows_one = lax.all_gather(hidden_one, ("x", "c"), axis=0, tiled=True)
     query_proj = jnp.dot(rows_one, q_full, preferred_element_type=jnp.float32)
     key_projected = jnp.dot(rows_one, k_full, preferred_element_type=jnp.float32)
     value_proj = jnp.dot(rows_one, v_full, preferred_element_type=jnp.float32)
@@ -134,8 +200,8 @@
     )
     value_rows = value_proj.astype(jnp.bfloat16)
     all_keys, all_values = (
-        lax.all_gather(key_rows, "dp", axis=0, tiled=True),
-        lax.all_gather(value_rows, "dp", axis=0, tiled=True),
+        lax.all_gather(key_rows, ("z", "y"), axis=0, tiled=True),
+        lax.all_gather(value_rows, ("z", "y"), axis=0, tiled=True),
     )
     query_heads = query_rows.reshape(group_rows, kv_local, per_group, HEAD_SIZE)
 
@@ -196,69 +262,74 @@
     )
     attn_part = jnp.dot(attn_low, o_full, preferred_element_type=jnp.float32)
     attn_mine = lax.psum_scatter(
-        attn_part.astype(jnp.bfloat16), "tensor", scatter_dimension=0, tiled=True
+        attn_part.astype(jnp.bfloat16), ("x", "c"), scatter_dimension=0, tiled=True
     ).astype(jnp.float32)
     middle = inputs + branch_scale * attn_mine
     inv_two = lax.rsqrt(jnp.mean(middle * middle, axis=-1, keepdims=True) + norm_eps)
     normed_two = middle * inv_two
     hidden_two = (normed_two * gain_two.astype(jnp.float32)).astype(jnp.bfloat16)
-    rows_two = lax.all_gather(hidden_two, "tensor", axis=0, tiled=True)
-    gate_pre = jnp.dot(rows_two, gate_full, preferred_element_type=jnp.float32)
-    up_pre = jnp.dot(rows_two, up_full, preferred_element_type=jnp.float32)
+    rows_two = lax.all_gather(
+        relative_columns(hidden_two, z_size, "y"), ("z", "c"), axis=0, tiled=True
+    )
+    grad_out = out_grad.astype(jnp.float32)
+    grad_mlp = (branch_scale * grad_out).astype(jnp.bfloat16)
+    grad_mlp_rows = lax.all_gather(
+        relative_columns(grad_mlp, z_size, "y"), ("z", "c"), axis=0, tiled=True
+    )
+    gate_pre = jnp.dot(rows_two, gate_block, preferred_element_type=jnp.float32)
+    up_pre = jnp.dot(rows_two, up_block, preferred_element_type=jnp.float32)
     gate_sigmoid = jax.nn.sigmoid(gate_pre)
     activated = (gate_pre * gate_sigmoid * up_pre).astype(jnp.bfloat16)
-    mlp_part = jnp.dot(activated, down_full, preferred_element_type=jnp.float32)
-    mlp_mine = lax.psum_scatter(
-        mlp_part.astype(jnp.bfloat16), "tensor", scatter_dimension=0, tiled=True
-    ).astype(jnp.float32)
-    mixed = (middle + branch_scale * mlp_mine).astype(jnp.bfloat16)
-    again = (
-        lax.all_gather(norm_gain, "dp", axis=0, tiled=True),
-        lax.all_gather(q_weight, "dp", axis=0, tiled=True),
-        lax.all_gather(key_matrix, "dp", axis=0, tiled=True),
-        lax.all_gather(value_matrix, "dp", axis=0, tiled=True),
-        lax.all_gather(o_weight, "dp", axis=1, tiled=True),
-        lax.all_gather(mlp_gain, "dp", axis=0, tiled=True),
-        lax.all_gather(gate_weight, "dp", axis=0, tiled=True),
-        lax.all_gather(up_weight, "dp", axis=0, tiled=True),
-        lax.all_gather(down_weight, "dp", axis=1, tiled=True),
-        lax.all_gather(key_rows, "dp", axis=0, tiled=True),
-        lax.all_gather(value_rows, "dp", axis=0, tiled=True),
-    )
-    (
-        gain_one,
-        q_full,
-        k_full,
-        v_full,
-        o_full,
-        gain_two,
-        gate_full,
-        up_full,
-        down_full,
-        all_keys,
-        all_values,
-    ) = again
-    grad_out = out_grad.astype(jnp.float32)
-    grad_mlp = (branch_scale * grad_out).astype(jnp.bfloat16)
-    grad_mlp_rows = lax.all_gather(grad_mlp, "tensor", axis=0, tiled=True)
     grad_hidden = jnp.einsum(
-        "td,fd->tf", grad_mlp_rows, down_full, preferred_element_type=jnp.float32
-    )
-    grad_down = jnp.einsum(
-        "tf,td->fd", activated, grad_mlp_rows, preferred_element_type=jnp.float32
+        "td,fd->tf", grad_mlp_rows, down_block, preferred_element_type=jnp.float32
     )
     grad_gate_act = (
         grad_hidden * up_pre * gate_sigmoid * (1.0 + gate_pre * (1.0 - gate_sigmoid))
     ).astype(jnp.bfloat16)
     grad_up_act = (grad_hidden * gate_pre * gate_sigmoid).astype(jnp.bfloat16)
-    grad_gate = jnp.einsum("td,tf->df", rows_two, grad_gate_act, preferred_element_type=jnp.float32)
-    grad_up = jnp.einsum("td,tf->df", rows_two, grad_up_act, preferred_element_type=jnp.float32)
     input_part = jnp.einsum(
-        "tf,df->td", grad_gate_act, gate_full, preferred_element_type=jnp.float32
-    ) + jnp.einsum("tf,df->td", grad_up_act, up_full, preferred_element_type=jnp.float32)
-    grad_rows_two = lax.psum_scatter(
-        input_part.astype(jnp.bfloat16), "tensor", scatter_dimension=0, tiled=True
+        "tf,df->td", grad_gate_act, gate_block, preferred_element_type=jnp.float32
+    ) + jnp.einsum("tf,df->td", grad_up_act, up_block, preferred_element_type=jnp.float32)
+    grad_rows_two = natural_columns(
+        lax.psum_scatter(
+            input_part.astype(jnp.bfloat16), ("z", "c"), scatter_dimension=0, tiled=True
+        ),
+        z_size,
+        "y",
     ).astype(jnp.float32)
+    mlp_part = jnp.dot(activated, down_block, preferred_element_type=jnp.float32)
+    mlp_mine = natural_columns(
+        lax.psum_scatter(
+            mlp_part.astype(jnp.bfloat16), ("z", "c"), scatter_dimension=0, tiled=True
+        ),
+        z_size,
+        "y",
+    ).astype(jnp.float32)
+    mixed = (middle + branch_scale * mlp_mine).astype(jnp.bfloat16)
+
+    def owned_block(left, right, feature_dim):
+        pieces = []
+        for far in range(y_size):
+            near = [left, right]
+            width = near[feature_dim].shape[1] // y_size
+            near[feature_dim] = near[feature_dim][:, far * width : (far + 1) * width]
+            pieces.append(jnp.einsum("ta,tb->ab", *near, preferred_element_type=jnp.float32))
+        mine = summed_pieces(pieces, "y")
+        width = mine.shape[1 - feature_dim] // x_size
+        mine = summed_pieces(
+            [
+                lax.slice_in_dim(mine, far * width, (far + 1) * width, axis=1 - feature_dim)
+                for far in range(x_size)
+            ],
+            "x",
+        ).astype(jnp.bfloat16)
+        return jnp.concatenate(
+            exchanged(mine, "z", z_size, feature_dim), axis=1 - feature_dim
+        ).astype(jnp.float32)
+
+    grad_down = owned_block(activated, grad_mlp_rows, 1)
+    grad_gate = owned_block(rows_two, grad_gate_act, 0)
+    grad_up = owned_block(rows_two, grad_up_act, 0)
     gain_two_part = jnp.sum(grad_rows_two * normed_two, axis=0)
     grad_normed_two = grad_rows_two * gain_two.astype(jnp.float32)
     grad_middle = grad_out + inv_two * (
@@ -266,7 +337,7 @@
         - normed_two * jnp.mean(grad_normed_two * normed_two, axis=-1, keepdims=True)
     )
     grad_attn = (branch_scale * grad_middle).astype(jnp.bfloat16)
-    grad_attn_rows = lax.all_gather(grad_attn, "tensor", axis=0, tiled=True)
+    grad_attn_rows = lax.all_gather(grad_attn, ("x", "c"), axis=0, tiled=True)
     grad_o = jnp.einsum("tc,td->cd", attn_low, grad_attn_rows, preferred_element_type=jnp.float32)
     grad_heads = (
         jnp.einsum("td,cd->tc", grad_attn_rows, o_full, preferred_element_type=jnp.float32)
@@ -327,7 +398,7 @@
         ),
     )
     grad_kv_mine = lax.psum_scatter(
-        grad_kv.astype(jnp.bfloat16), "dp", scatter_dimension=0, tiled=True
+        grad_kv.astype(jnp.bfloat16), ("z", "y"), scatter_dimension=0, tiled=True
     ).astype(jnp.float32)
     grad_keys = (
         rotary_apply(
@@ -361,7 +432,7 @@
         "tc,dc->td", grad_values, v_full, preferred_element_type=jnp.float32
     )
     grad_rows_one = lax.psum_scatter(
-        input_one.astype(jnp.bfloat16), "tensor", scatter_dimension=0, tiled=True
+        input_one.astype(jnp.bfloat16), ("x", "c"), scatter_dimension=0, tiled=True
     ).astype(jnp.float32)
     gain_one_part = jnp.sum(grad_rows_one * normed_one, axis=0)
     grad_normed_one = grad_rows_one * gain_one.astype(jnp.float32)
@@ -371,75 +442,74 @@
     )
     summed = (
         lax.psum_scatter(
-            gain_one_part.astype(jnp.bfloat16), "dp", scatter_dimension=0, tiled=True
+            jnp.stack([gain_one_part, gain_two_part], 1).astype(jnp.bfloat16),
+            ("z", "y"),
+            scatter_dimension=0,
+            tiled=True,
         ).astype(jnp.float32),
-        lax.psum_scatter(grad_q.astype(jnp.bfloat16), "dp", scatter_dimension=0, tiled=True).astype(
-            jnp.float32
-        ),
-        lax.psum_scatter(grad_k.astype(jnp.bfloat16), "dp", scatter_dimension=0, tiled=True).astype(
-            jnp.float32
-        ),
-        lax.psum_scatter(grad_v.astype(jnp.bfloat16), "dp", scatter_dimension=0, tiled=True).astype(
-            jnp.float32
-        ),
-        lax.psum_scatter(grad_o.astype(jnp.bfloat16), "dp", scatter_dimension=1, tiled=True).astype(
-            jnp.float32
-        ),
-        lax.psum_scatter(
-            gain_two_part.astype(jnp.bfloat16), "dp", scatter_dimension=0, tiled=True
+        lax.psum_scatter(
+            grad_q.astype(jnp.bfloat16), ("z", "y"), scatter_dimension=0, tiled=True
         ).astype(jnp.float32),
         lax.psum_scatter(
-            grad_gate.astype(jnp.bfloat16), "dp", scatter_dimension=0, tiled=True
+            grad_k.astype(jnp.bfloat16), ("z", "y"), scatter_dimension=0, tiled=True
         ).astype(jnp.float32),
         lax.psum_scatter(
-            grad_up.astype(jnp.bfloat16), "dp", scatter_dimension=0, tiled=True
+            grad_v.astype(jnp.bfloat16), ("z", "y"), scatter_dimension=0, tiled=True
         ).astype(jnp.float32),
         lax.psum_scatter(
-            grad_down.astype(jnp.bfloat16), "dp", scatter_dimension=1, tiled=True
+            grad_o.astype(jnp.bfloat16), ("z", "y"), scatter_dimension=1, tiled=True
         ).astype(jnp.float32),
     )
-    gain_sums = lax.psum((summed[0], summed[5]), "tensor")
+    gain_sums = lax.psum(summed[0], ("x", "c"))
     return (
         mixed,
         grad_inputs.astype(jnp.bfloat16),
-        gain_sums[0],
+        gain_sums[:, 0],
         summed[1],
         summed[2],
         summed[3],
         summed[4],
-        gain_sums[1],
-        summed[6],
-        summed[7],
-        summed[8],
+        gain_sums[:, 1],
+        grad_gate,
+        grad_up,
+        grad_down,
     )
 
 
 def solution(mesh):
+    dp_size, tensor_size = mesh.shape["dp"], mesh.shape["tensor"]
+    fine = jax.sharding.Mesh(
+        mesh.devices.reshape(4, dp_size // 4, tensor_size // 2, 2), ("z", "y", "x", "c")
+    )
+    dp, tensor = ("z", "y"), ("x", "c")
+    tokens = P(dp + tensor, None)
+    rows = P(dp, tensor)
+    columns = P(tensor, dp)
     in_specs = (
-        P(("dp", "tensor"), None),
-        P("dp"),
-        P("dp", "tensor"),
-        P("dp", "tensor"),
-        P("dp", "tensor"),
-        P("tensor", "dp"),
-        P("dp"),
-        P("dp", "tensor"),
-        P("dp", "tensor"),
-        P("tensor", "dp"),
+        tokens,
+        P(dp),
+        rows,
+        rows,
+        rows,
+        columns,
+        P(dp),
+        rows,
+        rows,
+        columns,
         P(),
-        P(("dp", "tensor"), None),
+        tokens,
     )
     out_specs = (
-        P(("dp", "tensor"), None),
-        P(("dp", "tensor"), None),
-        P("dp"),
-        P("dp", "tensor"),
-        P("dp", "tensor"),
-        P("dp", "tensor"),
-        P("tensor", "dp"),
-        P("dp"),
-        P("dp", "tensor"),
-        P("dp", "tensor"),
-        P("tensor", "dp"),
-    )
-    return jax.shard_map(local, mesh=mesh, in_specs=in_specs, out_specs=out_specs, check_vma=False)
+        tokens,
+        tokens,
+        P(dp),
+        rows,
+        rows,
+        rows,
+        columns,
+        P(dp),
+        rows,
+        rows,
+        columns,
+    )
+    return jax.shard_map(local, mesh=fine, in_specs=in_specs, out_specs=out_specs, check_vma=False)

time: 1890 us -> 1440 us (0.76)
  waiting for transfers between devices: 1290 us -> 712 us
  starting transfers between devices: 1.51 us -> 141 us
  blocking collectives: 133 us -> 69.8 us
  local copies, waits for them, and re-layouts: 49.3 us -> 92.7 us
    reduce_scatter x12 -> x9, waiting for transfers between devices: 800 us -> 289 us  [the longest x1 62.8 us: local(): lax.psum_scatter(grad_v.astype(jnp.bfloat16), ('z', 'y'), scatter_dimensi...]
    all_gather x11 -> x8, waiting for transfers between devices: 490 us -> 89.5 us  [the longest x1 39.3 us: local(): lax.all_gather(key_rows, ('z', 'y'), axis=0, tiled=True)]
    ppermute x0 -> x34, waiting for transfers between devices: none -> 273 us  [rotated(): lax.ppermute(value, axis, [(i, (i + step) % size) for i in range(size)])]
    ppermute x0 -> x34, starting transfers between devices: none -> 140 us  [rotated(): lax.ppermute(value, axis, [(i, (i + step) % size) for i in range(size)])]
    unnamed x23 -> x19, waiting for transfers between devices: 3.58 us -> 60.8 us
    all_gather x4 -> x2, blocking collectives: 105 us -> 64.1 us  [the longest x1 32.2 us: local(): k_full = lax.all_gather(key_matrix, ('z', 'y'), axis=0, tiled=True)]
    unnamed x1 -> x0, blocking collectives: 21.6 us -> none
    dot_general x9 -> x12, matrix products: 82.2 us -> 84.8 us  [the longest x6 28.1 us: owned_block(): jnp.einsum('ta,tb->ab', *near, preferred_element_type=jnp.float32)]
  transfers between devices with their start and end apart: 23 -> 52, of which waited for: 20 -> 28; matrix products, arithmetic and copies ran while one was open for 11% -> 18% of each run, Pallas kernels for 0% -> 0%
where the time goes in v1:
time: 1440 us; the launch traced here: 1430 us
  waiting for transfers between devices  712 us (49%)
  matrix products  282 us (20%)
  starting transfers between devices  141 us (10%)
  other arithmetic  104 us (7%)
  local copies, waits for them, and re-layouts  92.7 us (6%)
  blocking collectives  69.8 us (5%)
  between operations  17.2 us (1%)
    ppermute x34, waiting for transfers between devices, rotated(): lax.ppermute(value, axis, [(i, (i + step) % size) for i in range(size)])  273 us
    ppermute x34, starting transfers between devices, rotated(): lax.ppermute(value, axis, [(i, (i + step) % size) for i in range(size)])  140 us
    reduce_scatter x1, waiting for transfers between devices, local(): lax.psum_scatter(grad_v.astype(jnp.bfloat16), ('z', 'y'), scatter_dimensi...  62.8 us
    reduce_scatter x1, waiting for transfers between devices, local(): lax.psum_scatter(grad_k.astype(jnp.bfloat16), ('z', 'y'), scatter_dimensi...  62.8 us
    unnamed x19, waiting for transfers between devices  60.8 us
    reduce_scatter x1, waiting for transfers between devices, local(): lax.psum_scatter(input_part.astype(jnp.bfloat16), ('z', 'c'), scatter_dim...  46.6 us
    dot_general x8, matrix products, block_scores(): jnp.einsum('qhgd,khd->hgqk', query_heads, key_slab, preferred_element_typ...  43.8 us
    dot_general x4, matrix products, back_visit_block(): jnp.einsum('qhgd,khd->hgqk', grad_heads, value_slab, preferred_element_ty...  39.8 us
  transfers between devices with their start and end apart: 52, of which 28 were waited for; matrix products, arithmetic and copies ran while one was open for 18% of the time, Pallas kernels for 0%

profile of v1, /device:TPU:0, one launch (start us, length us, event | category | flops | bytes accessed | tf_op | source)
XLA Modules:
  0.0 1428.7 jit_solution(15313511118672521155)
XLA Ops:
  33.9 31.9 %all_gather.34 = bf16[2048,128]{1,0:T(8,128)(2,1)S(1)} all-gather(bf16[256,128]{1,0:T(8,128)(2,1)S(1)} %copy-done.37), channel_id=1, replica_groups=mesh['z'=4,'y'=2,'x'=2,'c'=2] {'z','y'}, dimensions={0}, use_global_device_ids=true | all-gather | bytes 589824 | tf_op jit(solution)/shard_map/all_gather | solution.py:172
  81.1 32.2 %all_gather.31 = bf16[2048,128]{1,0:T(8,128)(2,1)S(1)} all-gather(bf16[256,128]{1,0:T(8,128)(2,1)S(1)} %copy-done.38), channel_id=1, replica_groups=mesh['z'=4,'y'=2,'x'=2,'c'=2] {'z','y'}, dimensions={0}, use_global_device_ids=true | all-gather | bytes 589824 | tf_op jit(solution)/shard_map/all_gather | solution.py:171
  118.8 29.3 %all-gather.15.cloned.1.call-done = bf16[4096,128]{1,0:T(8,128)(2,1)} async-done(((bf16[512,128]{1,0:T(8,128)(2,1)}), bf16[4096,128]{1,0:T(8,128)(2,1)}) %all-gather.15.cloned.1.call-update) | async-done | bytes 1048592 | tf_op jit(solution)/shard_map/all_gather | solution.py:204
  149.6 39.3 %all-gather.11.cloned.1.call-done = bf16[4096,128]{0,1:T(8,128)(2,1)} async-done(((bf16[512,128]{0,1:T(8,128)(2,1)}), bf16[4096,128]{0,1:T(8,128)(2,1)}) %all-gather.11.cloned.1.call-update) | async-done | bytes 1048592 | tf_op jit(solution)/shard_map/all_gather | solution.py:203
  188.9 45.4 %while.61 = (s32[]{:T(128)}, f32[2,4,512]{2,1,0:T(4,128)S(1)}, f32[2,4,512]{2,1,0:T(4,128)S(1)}, pred[2,16]{1,0:T(4,128)(4,1)S(1)}, bf16[4096,128]{0,1:T(8,128)(...) while((s32[]{:T(128)}, f32[2,4,512]{2,1,0:T(4,128)S(1)}, ...), condition=%wide.region_8.9_spmd.clone.clone, body=%wide.region_2.8_spmd.clone.clone.sunk | while | flops 572558336 | bytes 39849584 | solution.py:225
  235.5 51.0 %while.62 = (s32[]{:T(128)}, f32[2,4,512,64]{2,3,1,0:T(8,128)}, pred[2,16]{1,0:T(4,128)(4,1)S(1)}, bf16[4096,128]{0,1:T(8,128)(2,1)}, bf16[512,2,4,64]{0,3,2,1:T...) while((s32[]{:T(128)}, f32[2,4,512,64]{2,3,1,0:T(8,128)}, ...), condition=%wide.region_13.14_spmd.clone.clone, body=%wide.region_9.13_spmd.clone.clone.sunk | while | flops 1097100288 | bytes 8457825 | solution.py:254
  297.1 26.0 %reduce-scatter.13.cloned.1.call-done = bf16[128,2048]{1,0:T(8,128)(2,1)} async-done(((bf16[512,2048]{1,0:T(8,128)(2,1)}), bf16[128,2048]{1,0:T(8,128)(2,1)}) %reduce-scatter.13.cloned.1.call-update) | async-done | bytes 524304 | tf_op jit(solution)/shard_map/reduce_scatter | solution.py:264
  373.3 27.6 %collective-permute-start.9 = (bf16[256,512]{0,1:T(8,128)(2,1)}, bf16[256,512]{0,1:T(8,128)(2,1)S(1)}, u32[]{:S(2)}, u32[]{:S(2)}) collective-permute-start(bf16[256,512]{0,1:T(8,128)(2,1)} %copy.327), channel_id=1, source_target_pairs={{0,8},{8,16},{16,24},{24,0},{1,9},{9,17},{17,25},{25,1},{2,10},{10... | collective-permute-start | bytes 786440 | tf_op jit(solution)/shard_map/ppermute | solution.py:50
  405.8 40.8 %collective-permute-start.4 = (bf16[256,512]{0,1:T(8,128)(2,1)S(1)}, bf16[256,512]{0,1:T(8,128)(2,1)S(1)}, u32[]{:S(2)}, u32[]{:S(2)}) collective-permute-start(bf16[256,512]{0,1:T(8,128)(2,1)S(1)} %copy-done.32), channel_id=1, source_target_pairs={{0,8},{8,16},{16,24},{24,0},{1,9},{9,17},{17,25},{25,1},{2,10},{10... | collective-permute-start | bytes 786440 | tf_op jit(solution)/shard_map/ppermute | solution.py:50
  531.1 33.6 %collective-permute-done.13 = bf16[2048,512]{0,1:T(8,128)(2,1)} collective-permute-done((bf16[2048,512]{0,1:T(8,128)(2,1)}, bf16[2048,512]{0,1:T(8,128)(2,1)}, u32[]{:S(2)}, u32[]{:S(2)}) %collective-permute-start.13) | collective-permute-done | bytes 2097184 | tf_op jit(solution)/shard_map/ppermute | solution.py:50
  574.9 32.1 %collective-permute-done.8 = bf16[2048,512]{0,1:T(8,128)(2,1)} collective-permute-done((bf16[2048,512]{0,1:T(8,128)(2,1)}, bf16[2048,512]{0,1:T(8,128)(2,1)}, u32[]{:S(2)}, u32[]{:S(2)}) %collective-permute-start.8) | collective-permute-done | bytes 2097184 | tf_op jit(solution)/shard_map/ppermute | solution.py:50
  634.9 46.6 %reduce-scatter.17.cloned.1.call-done = bf16[128,2048]{1,0:T(8,128)(2,1)} async-done(((bf16[1024,2048]{1,0:T(8,128)(2,1)}), bf16[128,2048]{1,0:T(8,128)(2,1)}) %reduce-scatter.17.cloned.1.call-update) | async-done | bytes 524304 | tf_op jit(solution)/shard_map/reduce_scatter | solution.py:294
  717.6 151.0 %while.63 = (s32[]{:T(128)}, f32[2,4,512,64]{2,3,1,0:T(8,128)S(1)}, f32[4096,256]{0,1:T(8,128)}, pred[2,16]{1,0:T(4,128)(4,1)S(1)}, bf16[4096,128]{0,1:T(8,128)(...) while((s32[]{:T(128)}, f32[2,4,512,64]{2,3,1,0:T(8,128)S(1)}, ...), condition=%wide.region_23.24_spmd.clone.clone, body=%wide.region_19.23_spmd.clone.clone.sunk | while | flops 2741791744 | bytes 90541744 | solution.py:391
  719.2 36.3 %conditional.14 = ((f32[2,4,512,64]{2,3,1,0:T(8,128)S(1)}, f32[4096,256]{0,1:T(8,128)})) conditional(s32[]{:T(128)} %convert_element_type.453, (f32[2,4,512,64]{2,3,1,0:T(8,128)S(1)}, f32[4096,256]{0,1:T(8,128)}) %tuple.319, (pred[2,4]{1,0:T(4,128)(4,1)S(1)}, s32[512]{0:T(512)S(1)}, s32[]{:T(128)}, s32[1,1024]{1,0:T(1,128)S(1)}, s32[]{:T(128)}, ...), branch_computations={%region_21.21_spmd, %region_22.22_spmd.clone} | conditional | flops 2741784576 | bytes 90528344 | solution.py:389
  757.0 36.3 %conditional.14 = ((f32[2,4,512,64]{2,3,1,0:T(8,128)S(1)}, f32[4096,256]{0,1:T(8,128)})) conditional(s32[]{:T(128)} %convert_element_type.453, (f32[2,4,512,64]{2,3,1,0:T(8,128)S(1)}, f32[4096,256]{0,1:T(8,128)}) %tuple.319, (pred[2,4]{1,0:T(4,128)(4,1)S(1)}, s32[512]{0:T(512)S(1)}, s32[]{:T(128)}, s32[1,1024]{1,0:T(1,128)S(1)}, s32[]{:T(128)}, ...), branch_computations={%region_21.21_spmd, %region_22.22_spmd.clone} | conditional | flops 2741784576 | bytes 90528344 | solution.py:389
  794.7 36.2 %conditional.14 = ((f32[2,4,512,64]{2,3,1,0:T(8,128)S(1)}, f32[4096,256]{0,1:T(8,128)})) conditional(s32[]{:T(128)} %convert_element_type.453, (f32[2,4,512,64]{2,3,1,0:T(8,128)S(1)}, f32[4096,256]{0,1:T(8,128)}) %tuple.319, (pred[2,4]{1,0:T(4,128)(4,1)S(1)}, s32[512]{0:T(512)S(1)}, s32[]{:T(128)}, s32[1,1024]{1,0:T(1,128)S(1)}, s32[]{:T(128)}, ...), branch_computations={%region_21.21_spmd, %region_22.22_spmd.clone} | conditional | flops 2741784576 | bytes 90528344 | solution.py:389
  832.4 36.2 %conditional.14 = ((f32[2,4,512,64]{2,3,1,0:T(8,128)S(1)}, f32[4096,256]{0,1:T(8,128)})) conditional(s32[]{:T(128)} %convert_element_type.453, (f32[2,4,512,64]{2,3,1,0:T(8,128)S(1)}, f32[4096,256]{0,1:T(8,128)}) %tuple.319, (pred[2,4]{1,0:T(4,128)(4,1)S(1)}, s32[512]{0:T(512)S(1)}, s32[]{:T(128)}, s32[1,1024]{1,0:T(1,128)S(1)}, s32[]{:T(128)}, ...), branch_computations={%region_21.21_spmd, %region_22.22_spmd.clone} | conditional | flops 2741784576 | bytes 90528344 | solution.py:389
  908.3 39.3 %reduce-scatter.19.cloned.1.call-done = bf16[512,256]{0,1:T(8,128)(2,1)} async-done(((bf16[4096,256]{0,1:T(8,128)(2,1)}), bf16[512,256]{0,1:T(8,128)(2,1)}) %reduce-scatter.19.cloned.1.call-update) | async-done | bytes 262160 | tf_op jit(solution)/shard_map/reduce_scatter | solution.py:400
  963.5 36.9 %collective-permute-done.29 = bf16[1024,1024]{1,0:T(8,128)(2,1)} collective-permute-done((bf16[1024,1024]{1,0:T(8,128)(2,1)}, bf16[1024,1024]{1,0:T(8,128)(2,1)}, u32[]{:S(2)}, u32[]{:S(2)}) %collective-permute-start.29) | collective-permute-done | bytes 2097184 | tf_op jit(solution)/shard_map/ppermute | solution.py:50
  1016.2 40.1 %collective-permute-done.19 = bf16[1024,1024]{0,1:T(8,128)(2,1)} collective-permute-done((bf16[1024,1024]{0,1:T(8,128)(2,1)}, bf16[1024,1024]{0,1:T(8,128)(2,1)}, u32[]{:S(2)}, u32[]{:S(2)}) %collective-permute-start.19) | collective-permute-done | bytes 2097184 | tf_op jit(solution)/shard_map/ppermute | solution.py:50
  1188.7 62.8 %reduce-scatter.25.cloned.1.call-done = bf16[256,128]{1,0:T(8,128)(2,1)} async-done(((bf16[2048,128]{1,0:T(8,128)(2,1)}), bf16[256,128]{1,0:T(8,128)(2,1)}) %reduce-scatter.25.cloned.1.call-update) | async-done | bytes 65552 | tf_op jit(solution)/shard_map/reduce_scatter | solution.py:453
  1253.0 62.8 %reduce-scatter.27.cloned.1.call-done = bf16[256,128]{1,0:T(8,128)(2,1)} async-done(((bf16[2048,128]{1,0:T(8,128)(2,1)}), bf16[256,128]{1,0:T(8,128)(2,1)}) %reduce-scatter.27.cloned.1.call-update) | async-done | bytes 65552 | tf_op jit(solution)/shard_map/reduce_scatter | solution.py:456
  1317.3 31.6 %reduce-scatter.21.cloned.1.call-done = bf16[128,2048]{1,0:T(8,128)(2,1)} async-done(((bf16[512,2048]{1,0:T(8,128)(2,1)}), bf16[128,2048]{1,0:T(8,128)(2,1)}) %reduce-scatter.21.cloned.1.call-update) | async-done | bytes 524304 | tf_op jit(solution)/shard_map/reduce_scatter | solution.py:434
  1354.7 59.3 %reduce-scatter.31.cloned.1.call-done = bf16[256,2]{1,0:T(8,128)(2,1)} async-done(((bf16[2048,2]{1,0:T(8,128)(2,1)}), bf16[256,2]{1,0:T(8,128)(2,1)}) %reduce-scatter.31.cloned.1.call-update) | async-done | bytes 1040
  (625 shorter events, 814.2 us)
Async XLA Ops:
  26.7 88.9 %all-gather.13.cloned.1.call-start = ((), (), s32[]{:S(2)}) async-start(), calls=%async_computation.12 | async-start | bytes 2359296 | tf_op jit(solution)/shard_map/all_gather | solution.py:170
  27.5 120.6 %all-gather.15.cloned.1.call-start = ((), (), s32[]{:S(2)}) async-start(), calls=%async_computation.13 | async-start | bytes 1179648 | tf_op jit(solution)/shard_map/all_gather | solution.py:204
  69.0 119.9 %all-gather.11.cloned.1.call-start = ((), (), s32[]{:S(2)}) async-start(), calls=%async_computation.11 | async-start | bytes 1179648 | tf_op jit(solution)/shard_map/all_gather | solution.py:203
  114.9 173.3 %all-gather.17.cloned.1.call-start = ((), (), s32[]{:S(2)}) async-start(), calls=%async_computation.14 | async-start | bytes 2359296 | tf_op jit(solution)/shard_map/all_gather | solution.py:173
  115.5 207.6 %reduce-scatter.13.cloned.1.call-start = ((), (), s32[]{:S(2)}) async-start(), calls=%async_computation.15 | async-start | bytes 2621440 | tf_op jit(solution)/shard_map/reduce_scatter | solution.py:264
  292.6 228.4 %all-gather.21.cloned.1.call-start = ((), (), s32[]{:S(2)}) async-start(), calls=%async_computation.18 | async-start | bytes 4718592 | tf_op jit(solution)/shard_map/all_gather | solution.py:276
  297.0 267.7 %all-gather.19.cloned.1.call-start = ((), (), s32[]{:S(2)}) async-start(), calls=%async_computation.16 | async-start | bytes 4718592 | tf_op jit(solution)/shard_map/all_gather | solution.py:271
  332.3 349.2 %reduce-scatter.17.cloned.1.call-start = ((), (), s32[]{:S(2)}) async-start(), calls=%async_computation.19 | async-start | bytes 4718592 | tf_op jit(solution)/shard_map/reduce_scatter | solution.py:294
  339.8 110.4 %collective-permute-start.6 = (bf16[256,512]{0,1:T(8,128)(2,1)}, bf16[256,512]{0,1:T(8,128)(2,1)S(1)}, u32[]{:S(2)}, u32[]{:S(2)}) collective-permute-start(bf16[256,512]{0,1:T(8,128)(2,1)} %copy.325), channel_id=1, source_target_pairs={{0,24},{8,0},{16,8},{24,16},{1,25},{9,1},{17,9},{25,17},{2,26},{10... | collective-permute-start | bytes 786440 | tf_op jit(solution)/shard_map/ppermute | solution.py:50
  342.1 108.1 %collective-permute-start.5 = (bf16[256,512]{0,1:T(8,128)(2,1)}, bf16[256,512]{0,1:T(8,128)(2,1)S(1)}, u32[]{:S(2)}, u32[]{:S(2)}) collective-permute-start(bf16[256,512]{0,1:T(8,128)(2,1)} %copy.324), channel_id=1, source_target_pairs={{0,16},{8,24},{16,0},{24,8},{1,17},{9,25},{17,1},{25,9},{2,18},{10... | collective-permute-start | bytes 786440 | tf_op jit(solution)/shard_map/ppermute | solution.py:50
  353.1 93.5 %collective-permute-start.10 = (bf16[256,512]{0,1:T(8,128)(2,1)}, bf16[256,512]{0,1:T(8,128)(2,1)S(1)}, u32[]{:S(2)}, u32[]{:S(2)}) collective-permute-start(bf16[256,512]{0,1:T(8,128)(2,1)} %copy.328), channel_id=1, source_target_pairs={{0,16},{8,24},{16,0},{24,8},{1,17},{9,25},{17,1},{25,9},{2,18},{10... | collective-permute-start | bytes 786440 | tf_op jit(solution)/shard_map/ppermute | solution.py:50
  519.6 87.4 %collective-permute-start.8 = (bf16[2048,512]{0,1:T(8,128)(2,1)}, bf16[2048,512]{0,1:T(8,128)(2,1)}, u32[]{:S(2)}, u32[]{:S(2)}) collective-permute-start(bf16[2048,512]{0,1:T(8,128)(2,1)} %constant_dynamic-update-slice_fusion), channel_id=1, source_target_pairs={{0,2},{2,0},{1,3},{3,1},{4,6},{6,4},{5,7},{7,5},{8,10},{10,8},{9,1... | collective-permute-start | bytes 6291464 | tf_op jit(solution)/shard_map/ppermute | solution.py:50
  689.5 258.1 %reduce-scatter.19.cloned.1.call-start = ((), (), s32[]{:S(2)}) async-start(), calls=%async_computation.21 | async-start | bytes 2359296 | tf_op jit(solution)/shard_map/reduce_scatter | solution.py:400
  872.4 288.0 %reduce-scatter.15.cloned.1.call-start = ((), (), s32[]{:S(2)}) async-start(), calls=%async_computation.17 | async-start | bytes 4718592 | tf_op jit(solution)/shard_map/reduce_scatter | solution.py:302
  882.8 282.3 %reduce-scatter.29.cloned.1.call-start = ((), (), s32[]{:S(2)}) async-start(), calls=%async_computation.26 | async-start | bytes 2359296 | tf_op jit(solution)/shard_map/reduce_scatter | solution.py:459
  888.0 298.8 %reduce-scatter.23.cloned.1.call-start = ((), (), s32[]{:S(2)}) async-start(), calls=%async_computation.23 | async-start | bytes 2359296 | tf_op jit(solution)/shard_map/reduce_scatter | solution.py:450
  892.4 359.0 %reduce-scatter.25.cloned.1.call-start = ((), (), s32[]{:S(2)}) async-start(), calls=%async_computation.24 | async-start | bytes 589824 | tf_op jit(solution)/shard_map/reduce_scatter | solution.py:453
  902.5 97.8 %collective-permute-start.29 = (bf16[1024,1024]{1,0:T(8,128)(2,1)}, bf16[1024,1024]{1,0:T(8,128)(2,1)}, u32[]{:S(2)}, u32[]{:S(2)}) collective-permute-start(bf16[1024,1024]{1,0:T(8,128)(2,1)} %fusion.67), channel_id=1, source_target_pairs={{0,4},{4,0},{1,5},{5,1},{2,6},{6,2},{3,7},{7,3},{8,12},{12,8},{9,1... | collective-permute-start | bytes 6291464 | tf_op jit(solution)/shard_map/ppermute | solution.py:50
  908.3 147.9 %collective-permute-start.19 = (bf16[1024,1024]{0,1:T(8,128)(2,1)}, bf16[1024,1024]{0,1:T(8,128)(2,1)}, u32[]{:S(2)}, u32[]{:S(2)}) collective-permute-start(bf16[1024,1024]{0,1:T(8,128)(2,1)} %convolution_convert_fusion.7), channel_id=1, source_target_pairs={{0,4},{4,0},{1,5},{5,1},{2,6},{6,2},{3,7},{7,3},{8,12},{12,8},{9,1... | collective-permute-start | bytes 6291464 | tf_op jit(solution)/shard_map/ppermute | solution.py:50
  950.2 365.6 %reduce-scatter.27.cloned.1.call-start = ((), (), s32[]{:S(2)}) async-start(), calls=%async_computation.25 | async-start | bytes 589824 | tf_op jit(solution)/shard_map/reduce_scatter | solution.py:456
  962.1 101.5 %collective-permute-start.25 = (bf16[1024,512]{0,1:T(8,128)(2,1)}, bf16[1024,512]{0,1:T(8,128)(2,1)}, u32[]{:S(2)}, u32[]{:S(2)}) collective-permute-start(bf16[1024,512]{0,1:T(8,128)(2,1)} %slice.227), channel_id=1, source_target_pairs={{0,2},{2,0},{1,3},{3,1},{4,6},{6,4},{5,7},{7,5},{8,10},{10,8},{9,1... | collective-permute-start | bytes 3145736 | tf_op jit(solution)/shard_map/ppermute | solution.py:50
  1009.9 338.9 %reduce-scatter.21.cloned.1.call-start = ((), (), s32[]{:S(2)}) async-start(), calls=%async_computation.22 | async-start | bytes 2621440 | tf_op jit(solution)/shard_map/reduce_scatter | solution.py:434
  1016.1 397.9 %reduce-scatter.31.cloned.1.call-start = ((), (), s32[]{:S(2)}) async-start(), calls=%async_computation.27 | async-start | bytes 589824
  1073.9 76.8 %collective-permute-start.32 = (bf16[512,256]{1,0:T(8,128)(2,1)}, bf16[512,256]{1,0:T(8,128)(2,1)S(1)}, u32[]{:S(2)}, u32[]{:S(2)}) collective-permute-start(bf16[512,256]{1,0:T(8,128)(2,1)} %get-tuple-element.1886), channel_id=1, source_target_pairs={{0,16},{8,24},{16,0},{24,8},{1,17},{9,25},{17,1},{25,9},{2,18},{10... | collective-permute-start | bytes 786440 | tf_op jit(solution)/shard_map/ppermute | solution.py:50
  (87 other events, 4251.6 us)
Sparse Core Ops, SparseCore 0:
  26.8 20.7 all-gather.8
  49.8 57.0 all-gather.12
  109.5 38.5 all-gather.14
  150.6 38.2 all-gather.10
  190.8 49.9 all-gather.16
  292.8 30.2 reduce-scatter.12
  689.6 20.7 all-gather.22
  872.6 74.9 reduce-scatter.18
  950.0 48.6 reduce-scatter.14
  1002.5 81.0 reduce-scatter.28
  1087.6 99.2 reduce-scatter.22
  1190.4 60.9 reduce-scatter.24
  1254.8 60.9 reduce-scatter.26
  1318.3 30.4 reduce-scatter.20
  1352.0 61.9 reduce-scatter.30
Sparse Core Ops, SparseCore 1:
  297.1 56.5 all-gather.20
  355.7 83.7 all-gather.18
  634.9 46.5 reduce-scatter.16

commit v2 on v1

v2 whole, which is shorter than its diff:
```python
import jax
import jax.numpy as jnp
from jax import lax
from jax.experimental import pallas as pl
from jax.experimental.pallas import tpu as pltpu
from jax.sharding import PartitionSpec as P

HEAD_SIZE = 64
SEG = 256
MAX_STEPS = 9


attn_scale = 0.015625
branch_scale = 0.22
norm_eps = 1e-05
rope_base = 10000000.0
masked_score = -1e30


def segment_depth(parents):
    seg_total = parents.shape[0]
    seg_ids = jnp.arange(seg_total, dtype=jnp.int32)
    reach = (parents[:, None] == seg_ids[None, :]) | (seg_ids[:, None] == seg_ids[None, :])
    reach = reach.astype(jnp.float32)
    for doubling in range(4):
        reach = jnp.minimum(jnp.dot(reach, reach, preferred_element_type=jnp.float32), 1.0)
    return jnp.sum(reach, axis=1).astype(jnp.int32) - 1


def rope_tables(position, head_dim):
    half_dim = head_dim // 2
    exponent = jnp.arange(half_dim, dtype=jnp.float32) * (2.0 / head_dim)
    inverse = jnp.power(rope_base, -exponent)
    angles = position.astype(jnp.float32)[:, None] * inverse[None, :]
    return (jnp.cos(angles), jnp.sin(angles))


def rotary_apply(value_rows, cosine_table, sine_table, direction):
    half_dim = value_rows.shape[-1] // 2
    first_half = value_rows[..., :half_dim]
    second = value_rows[..., half_dim:]
    cos_part = cosine_table[:, None, :]
    sin_part = sine_table[:, None, :] * direction
    return jnp.concatenate(
        [first_half * cos_part - second * sin_part, second * cos_part + first_half * sin_part],
        axis=-1,
    )


def rotated(value, axis, step):
    size = lax.axis_size(axis)
    return lax.ppermute(value, axis, [(i, (i + step) % size) for i in range(size)])


def relative_pieces(value, axis):
    return [value] + [rotated(value, axis, k) for k in range(1, lax.axis_size(axis))]


def natural_pieces(pieces, axis):
    size = len(pieces)
    place = lax.axis_index(axis)
    return [
        lax.select_n(place, *[pieces[(i - j) % size] for i in range(size)]) for j in range(size)
    ]


def gathered(value, axis):
    size = lax.axis_size(axis)
    copies = jnp.broadcast_to(value[None], (size, *value.shape))
    return lax.all_to_all(copies, axis, 0, 0, tiled=True)


def exchanged(blocks, axis):
    return lax.all_to_all(blocks, axis, 0, 0, tiled=True)


def summed_pieces(pieces, axis):
    sent = [rotated(pieces[k].astype(jnp.bfloat16), axis, -k) for k in range(1, len(pieces))]
    total = pieces[0].astype(jnp.float32)
    for value in sent:
        total = total + value.astype(jnp.float32)
    return total


def summed_blocks(blocks, axis):
    return jnp.sum(exchanged(blocks.astype(jnp.bfloat16), axis).astype(jnp.float32), axis=0)


def column_blocks(value, count):
    return value.reshape(value.shape[0], count, -1).transpose(1, 0, 2)


def joined_columns(blocks):
    return blocks.transpose(1, 0, 2).reshape(blocks.shape[1], -1)


def relative_columns(value):
    size = lax.axis_size("y")
    place = lax.axis_index("y")
    rows = value.shape[0]
    split = value.reshape(rows, lax.axis_size("z"), size, -1)
    flat = [split[:, :, i].reshape(rows, -1) for i in range(size)]
    return jnp.concatenate(
        [
            lax.select_n(place, *[flat[(i - k) % size] for i in range(size)])
            for k in range(size)
        ],
        axis=1,
    )


def natural_columns(value):
    size = lax.axis_size("y")
    rows = value.shape[0]
    split = value.reshape(rows, size, lax.axis_size("z"), -1)
    parts = natural_pieces([split[:, k] for k in range(size)], "y")
    return jnp.stack(parts, axis=2).reshape(rows, -1)


def after(value, *others):
    return lax.optimization_barrier((value, *others))[0]


def ancestor_count(parents, seg):
    def climb(step, state):
        current, count = state
        above = parents[current]
        return above, count + jnp.where(above != current, 1, 0)

    return lax.fori_loop(0, MAX_STEPS, climb, (seg, jnp.int32(1)))[1]


def left_lanes(shape):
    return lax.broadcasted_iota(jnp.int32, shape, 1) < HEAD_SIZE


def stacked_heads(pairs, group):
    left = left_lanes((SEG, 2 * HEAD_SIZE))
    own = left == (group == 0)
    stack = []
    for pair in pairs:
        swapped = pltpu.roll(pair, HEAD_SIZE, 1)
        even = jnp.where(group == 0, pair, swapped)
        odd = jnp.where(group == 0, swapped, pair)
        stack += [jnp.where(own, even, 0.0), jnp.where(own, odd, 0.0)]
    return jnp.concatenate(stack, axis=0)


def unstacked_heads(stack, group):
    left = left_lanes((SEG, 2 * HEAD_SIZE))
    pairs = []
    for first in range(0, stack.shape[0], 2 * SEG):
        even, odd = stack[first : first + SEG], stack[first + SEG : first + 2 * SEG]
        even = jnp.where(group == 0, even, pltpu.roll(even, HEAD_SIZE, 1))
        odd = jnp.where(group == 0, pltpu.roll(odd, HEAD_SIZE, 1), odd)
        pairs.append(jnp.where(left, even, odd))
    return pairs


def turned(value, cosine, sine, direction):
    half = HEAD_SIZE // 2
    lane = lax.broadcasted_iota(jnp.int32, value.shape, 1)
    first = lax.rem(lane, HEAD_SIZE) < half
    ahead = pltpu.roll(value, 2 * HEAD_SIZE - half, 1)
    behind = pltpu.roll(value, half, 1)
    signed = sine * direction
    return value * cosine + jnp.where(first, -ahead * signed, behind * signed)


def nt_dot(left, right):
    return lax.dot_general(
        left, right, (((1,), (1,)), ((), ())), preferred_element_type=jnp.float32
    )


def nn_dot(left, right):
    return lax.dot_general(
        left, right, (((1,), (0,)), ((), ())), preferred_element_type=jnp.float32
    )


def causal_tile(rows):
    query = lax.rem(lax.broadcasted_iota(jnp.int32, (rows, SEG), 0), SEG)
    return lax.broadcasted_iota(jnp.int32, (rows, SEG), 1) <= query


def attend_kernel(
    parents, first_seg, proj, cosine, sine, keys_values, out, out_low, stats, queries, scores
):
    seg = first_seg[0] + pl.program_id(0)
    group = pl.program_id(1)
    count = ancestor_count(parents, seg)
    cos, sin = cosine[...], sine[...]
    lanes = 2 * HEAD_SIZE
    pairs = [
        turned(proj[:, at : at + lanes], cos, sin, 1.0) * attn_scale
        for at in range(0, proj.shape[1], lanes)
    ]
    stack = stacked_heads(pairs, group).astype(jnp.bfloat16)
    queries[0, 0] = stack
    rows = stack.shape[0]

    first = jnp.where(causal_tile(rows), nt_dot(stack, keys_values[seg, :, :lanes]), masked_score)
    scores[0] = first

    def measure(step, state):
        current, top = state
        current = parents[current]
        tile = nt_dot(stack, keys_values[current, :, :lanes])
        scores[step] = tile
        return current, jnp.maximum(top, tile)

    top = lax.fori_loop(1, count, measure, (seg, first))[1]
    row_max = jnp.max(top, axis=1, keepdims=True)

    def gather(step, state):
        current, total, mixed = state
        terms = jnp.exp(scores[step] - row_max)
        mixed = mixed + nn_dot(terms.astype(jnp.bfloat16), keys_values[current, :, lanes:])
        return parents[current], total + terms, mixed

    start = (seg, jnp.zeros((rows, SEG), jnp.float32), jnp.zeros((rows, lanes), jnp.float32))
    total, mixed = lax.fori_loop(0, count, gather, start)[1:]
    total = jnp.sum(total, axis=1, keepdims=True)
    mixed = mixed / total
    stats[0, 0] = row_max + jnp.log(total)
    for place, pair in enumerate(unstacked_heads(mixed, group)):
        out[:, place * lanes : (place + 1) * lanes] = pair
        out_low[:, place * lanes : (place + 1) * lanes] = pair.astype(jnp.bfloat16)


def attend_back_kernel(
    parents, first_seg, queries, grads, attended, stats, cosine, sine, keys_values,
    grad_proj, grad_kv, key_sum, value_sum,
):
    seg = first_seg[0] + pl.program_id(0)
    group = pl.program_id(1)
    count = ancestor_count(parents, seg)
    lanes = 2 * HEAD_SIZE

    @pl.when((pl.program_id(0) == 0) & (group == 0))
    def _():
        key_sum[...] = jnp.zeros_like(key_sum)
        value_sum[...] = jnp.zeros_like(value_sum)

    stack = queries[0, 0]
    rows = stack.shape[0]
    grad_pairs = [
        grads[:, at : at + lanes].astype(jnp.float32) for at in range(0, grads.shape[1], lanes)
    ]
    left = left_lanes((SEG, lanes))
    deltas = []
    for place, pair in enumerate(grad_pairs):
        product = pair * attended[:, place * lanes : (place + 1) * lanes]
        deltas.append(jnp.sum(jnp.where(left, product, 0.0), axis=1, keepdims=True))
        deltas.append(jnp.sum(jnp.where(left, 0.0, product), axis=1, keepdims=True))
    delta = jnp.concatenate(deltas, axis=0)
    grad_wide = stacked_heads(grad_pairs, group)
    grad_stack = grad_wide.astype(jnp.bfloat16)
    grad_turned = grad_wide.T.astype(jnp.bfloat16)
    query_turned = stack.astype(jnp.float32).T.astype(jnp.bfloat16)
    log_total = stats[0, 0]

    def visit(current, total, diagonal):
        tile_keys, tile_values = keys_values[current, :, :lanes], keys_values[current, :, lanes:]
        tile = nt_dot(stack, tile_keys)
        if diagonal:
            tile = jnp.where(causal_tile(rows), tile, masked_score)
        probs = jnp.exp(tile - log_total)
        grad_probs = nt_dot(grad_stack, tile_values)
        grad_tile = (probs * (grad_probs - delta)).astype(jnp.bfloat16)
        key_sum[current] += nn_dot(query_turned, grad_tile)
        value_sum[current] += nn_dot(grad_turned, probs.astype(jnp.bfloat16))
        return total + nn_dot(grad_tile, tile_keys)

    total = visit(seg, jnp.zeros((rows, lanes), jnp.float32), True)

    def climb(step, state):
        current, total = state
        current = parents[current]
        return current, visit(current, total, False)

    total = lax.fori_loop(1, count, climb, (seg, total))[1]
    cos, sin = cosine[...], sine[...]
    for place, pair in enumerate(unstacked_heads(total * attn_scale, group)):
        grad_proj[:, place * lanes : (place + 1) * lanes] = turned(pair, cos, sin, -1.0).astype(
            jnp.bfloat16
        )

    @pl.when((pl.program_id(0) == pl.num_programs(0) - 1) & (group == pl.num_programs(1) - 1))
    def _():
        grad_kv[:, :lanes, :] = key_sum[...].astype(jnp.bfloat16)
        grad_kv[:, lanes:, :] = value_sum[...].astype(jnp.bfloat16)


def attention_specs(group_rows, cols, groups, segs):
    width = cols // groups
    lanes = 2 * HEAD_SIZE
    block = pl.BlockSpec((SEG, width), lambda s, g: (s, g))
    table = pl.BlockSpec((SEG, lanes), lambda s, g: (s, 0))
    whole = pl.BlockSpec((segs, SEG, 2 * lanes), lambda s, g: (0, 0, 0))
    rows = SEG * (width // HEAD_SIZE)
    stack = pl.BlockSpec((1, 1, rows, lanes), lambda s, g: (s, g, 0, 0))
    stat = pl.BlockSpec((1, 1, rows, 1), lambda s, g: (s, g, 0, 0))
    scalar = pl.BlockSpec(memory_space=pltpu.SMEM)
    return block, table, whole, rows, stack, stat, scalar


def attend(parents, first_seg, proj, cosine, sine, keys_values, groups):
    group_rows, cols = proj.shape
    segs = keys_values.shape[0]
    lanes = 2 * HEAD_SIZE
    block, table, whole, rows, stack, stat, scalar = attention_specs(group_rows, cols, groups, segs)
    grid = (group_rows // SEG, groups)
    tiles = grid[0] * grid[1] * 8 * rows * SEG
    return pl.pallas_call(
        attend_kernel,
        grid=grid,
        in_specs=[scalar, scalar, block, table, table, whole],
        out_specs=[block, block, stat, stack],
        out_shape=[
            jax.ShapeDtypeStruct((group_rows, cols), jnp.float32),
            jax.ShapeDtypeStruct((group_rows, cols), jnp.bfloat16),
            jax.ShapeDtypeStruct((*grid, rows, 1), jnp.float32),
            jax.ShapeDtypeStruct((*grid, rows, lanes), jnp.bfloat16),
        ],
        scratch_shapes=[pltpu.VMEM((MAX_STEPS + 1, rows, SEG), jnp.float32)],
        compiler_params=pltpu.CompilerParams(vmem_limit_bytes=56 * 2**20),
        cost_estimate=pl.CostEstimate(
            flops=4 * tiles * lanes, bytes_accessed=8 * 2**20, transcendentals=tiles
        ),
    )(parents, first_seg, proj, cosine, sine, keys_values)


def attend_back(
    parents, first_seg, queries, grads, attended, stats, cosine, sine, keys_values, groups
):
    group_rows, cols = grads.shape
    segs = keys_values.shape[0]
    lanes = 2 * HEAD_SIZE
    block, table, whole, rows, stack, stat, scalar = attention_specs(group_rows, cols, groups, segs)
    grid = (group_rows // SEG, groups)
    tiles = grid[0] * grid[1] * 8 * rows * SEG
    return pl.pallas_call(
        attend_back_kernel,
        grid=grid,
        in_specs=[scalar, scalar, stack, block, block, stat, table, table, whole],
        out_specs=[block, pl.BlockSpec((segs, 2 * lanes, SEG), lambda s, g: (0, 0, 0))],
        out_shape=[
            jax.ShapeDtypeStruct((group_rows, cols), jnp.bfloat16),
            jax.ShapeDtypeStruct((segs, 2 * lanes, SEG), jnp.bfloat16),
        ],
        scratch_shapes=[
            pltpu.VMEM((segs, lanes, SEG), jnp.float32),
            pltpu.VMEM((segs, lanes, SEG), jnp.float32),
        ],
        compiler_params=pltpu.CompilerParams(vmem_limit_bytes=60 * 2**20),
        cost_estimate=pl.CostEstimate(
            flops=10 * tiles * lanes, bytes_accessed=8 * 2**20, transcendentals=tiles
        ),
    )(parents, first_seg, queries, grads, attended, stats, cosine, sine, keys_values)


def row_norm(value):
    inverse = lax.rsqrt(jnp.mean(value * value, axis=-1, keepdims=True) + norm_eps)
    return value * inverse, inverse


def norm_back(grad, normed, inverse, gain):
    scaled = grad * gain
    return inverse * (scaled - normed * jnp.mean(scaled * normed, axis=-1, keepdims=True))


def silu_parts(gate_pre):
    sigmoid = jax.nn.sigmoid(gate_pre)
    return sigmoid, gate_pre * sigmoid


def matmul(left, right):
    return jnp.dot(left, right, preferred_element_type=jnp.float32)


def matmul_turned(left, right):
    return nt_dot(left, right)


def turned_matmul(left, right):
    return lax.dot_general(
        left, right, (((0,), (0,)), ((), ())), preferred_element_type=jnp.float32
    )


def tensor_sum(part, rows):
    x_size, c_size = lax.axis_size("x"), lax.axis_size("c")
    blocks = part.reshape(x_size, c_size, rows, -1)
    c_place, x_place = lax.axis_index("c"), lax.axis_index("x")

    def block(value, place, k, axis):
        size = value.shape[axis]
        return lax.dynamic_index_in_dim(
            value, lax.rem(place - k + size, size), axis, keepdims=False
        )

    mine = summed_pieces([block(blocks, c_place, k, 1) for k in range(c_size)], "c")
    mine = mine.astype(jnp.bfloat16)
    return summed_pieces([block(mine, x_place, k, 0) for k in range(x_size)], "x")


def local(
    tokens,
    norm_gain,
    q_weight,
    key_matrix,
    value_matrix,
    o_weight,
    mlp_gain,
    gate_weight,
    up_weight,
    down_weight,
    parents,
    out_grad,
):
    z_size, y_size, x_size = (lax.axis_size(name) for name in ("z", "y", "x"))
    tensor_size = x_size * lax.axis_size("c")
    low = jnp.bfloat16
    local_rows, width = tokens.shape
    group_rows = local_rows * tensor_size
    kv_cols = key_matrix.shape[1]
    kv_local = kv_cols // HEAD_SIZE
    q_cols = q_weight.shape[1]
    own_width = norm_gain.shape[0]

    own_tokens = relative_columns(tokens)
    own_grad = relative_columns(out_grad).astype(jnp.float32)
    group_tokens = lax.all_gather(own_tokens, ("x", "c"), axis=0, tiled=True)

    both_gains = jnp.concatenate([norm_gain, mlp_gain])
    both_gains = jnp.pad(both_gains, (0, -both_gains.shape[0] % (2 * kv_cols)))
    kv_shard = jnp.concatenate(
        [
            jnp.concatenate([key_matrix, value_matrix], axis=1),
            both_gains.reshape(-1, 2 * kv_cols),
        ],
        axis=0,
    )
    kv_z = gathered(kv_shard, "z")
    kv_zy = jnp.stack(relative_pieces(kv_z, "y"))
    kv_full = kv_zy[:, :, :own_width].reshape(width, 2 * kv_cols)
    gains = kv_zy[:, :, own_width:].reshape(z_size * y_size, -1).astype(jnp.float32)
    gains = gains[:, : 2 * own_width].reshape(-1, 2, own_width)
    gain_one, gain_two = gains[:, 0].reshape(-1), gains[:, 1].reshape(-1)

    q_z = gathered(after(q_weight, kv_z), "z")
    q_full = jnp.stack(relative_pieces(q_z, "y")).reshape(width, q_cols)

    depth = segment_depth(parents)
    dp_place = lax.axis_index(("z", "y"))
    seg_count = group_rows // SEG
    first_seg = (dp_place * seg_count).astype(jnp.int32)
    own_depth = lax.dynamic_slice_in_dim(depth, first_seg, seg_count, 0)
    position = (own_depth[:, None] * SEG + jnp.arange(SEG, dtype=jnp.int32)[None, :]).reshape(-1)
    cosine_table, sine_table = rope_tables(position, HEAD_SIZE)
    cosine_lanes = jnp.tile(cosine_table, (1, 4))
    sine_lanes = jnp.tile(sine_table, (1, 4))
    first_seg = first_seg.reshape(1)

    inputs = own_tokens.astype(jnp.float32)
    normed_one, inv_one = row_norm(inputs)
    group_normed, _ = row_norm(group_tokens.astype(jnp.float32))
    rows_one = (group_normed * gain_one).astype(low)
    kv_proj = matmul(rows_one, kv_full)
    key_rows = rotary_apply(
        kv_proj[:, :kv_cols].reshape(group_rows, kv_local, HEAD_SIZE),
        cosine_table,
        sine_table,
        1.0,
    ).reshape(group_rows, kv_cols)
    kv_rows = jnp.concatenate([key_rows, kv_proj[:, kv_cols:]], axis=1).astype(low)
    all_z = gathered(after(kv_rows, q_z), "z")
    all_kv = jnp.stack(natural_pieces(relative_pieces(all_z, "y"), "y"), axis=1)
    all_kv = all_kv.reshape(-1, SEG, 2 * kv_cols)

    gate_z = exchanged(column_blocks(after(gate_weight, all_z), z_size), "z")
    gate_z = gate_z.reshape(z_size * own_width, -1)
    o_z = joined_columns(gathered(after(o_weight, gate_z), "z"))
    o_full = jnp.concatenate(relative_pieces(o_z, "y"), axis=1)
    up_z = exchanged(column_blocks(after(up_weight, o_z), z_size), "z")
    up_z = up_z.reshape(z_size * own_width, -1)
    down_z = joined_columns(
        exchanged(after(down_weight, up_z).reshape(z_size, -1, own_width), "z")
    )
    gate_block = jnp.concatenate(relative_pieces(gate_z, "y"), axis=0)
    gate_block = jnp.concatenate(relative_pieces(gate_block, "x"), axis=1)
    up_block = jnp.concatenate(relative_pieces(up_z, "x"), axis=1)
    up_block = jnp.concatenate(relative_pieces(up_block, "y"), axis=0)
    down_block = jnp.concatenate(relative_pieces(down_z, "x"), axis=0)
    down_block = jnp.concatenate(relative_pieces(down_block, "y"), axis=1)

    query_proj = matmul(rows_one, q_full)
    attended, attn_low, stats, query_stack = attend(
        parents, first_seg, query_proj, cosine_lanes, sine_lanes, all_kv, kv_local
    )
    attn_part = matmul(attn_low, o_full).astype(low)
    attn_mine = tensor_sum(attn_part, local_rows)
    middle = inputs + branch_scale * attn_mine
    normed_two, inv_two = row_norm(middle)
    hidden_two = (normed_two * gain_two).astype(low)

    rows_two = lax.all_gather(hidden_two, ("z", "c"), axis=0, tiled=True)
    grad_mlp = (branch_scale * own_grad).astype(low)
    grad_mlp_rows = lax.all_gather(grad_mlp, ("z", "c"), axis=0, tiled=True)
    gate_pre = matmul(rows_two, gate_block)
    up_pre = matmul(rows_two, up_block)
    gate_sigmoid, gate_silu = silu_parts(gate_pre)
    activated = (gate_silu * up_pre).astype(low)
    mlp_part = matmul(activated, down_block).astype(low)
    grad_hidden = matmul_turned(grad_mlp_rows, down_block)
    grad_gate_act = (
        grad_hidden * up_pre * gate_sigmoid * (1.0 + gate_pre * (1.0 - gate_sigmoid))
    ).astype(low)
    grad_up_act = (grad_hidden * gate_silu).astype(low)
    input_part = (
        matmul_turned(grad_gate_act, gate_block) + matmul_turned(grad_up_act, up_block)
    ).astype(low)
    grad_rows_two = lax.psum_scatter(
        input_part, ("z", "c"), scatter_dimension=0, tiled=True
    ).astype(jnp.float32)
    mlp_mine = lax.psum_scatter(
        mlp_part, ("z", "c"), scatter_dimension=0, tiled=True
    ).astype(jnp.float32)
    mixed = natural_columns((middle + branch_scale * mlp_mine).astype(low))

    gain_two_part = jnp.sum(grad_rows_two * normed_two, axis=0)
    grad_middle = own_grad + norm_back(grad_rows_two, normed_two, inv_two, gain_two)
    grad_attn = (branch_scale * grad_middle).astype(low)
    grad_attn_rows = lax.all_gather(grad_attn, ("x", "c"), axis=0, tiled=True)

    def halves(value, count):
        part = value.shape[1] // count
        return [value[:, i * part : (i + 1) * part] for i in range(count)]

    down_pieces = [
        summed_pieces(
            [turned_matmul(near, far) for far in halves(grad_mlp_rows, y_size)], "y"
        ).astype(low)
        for near in halves(activated, x_size)
    ]
    grad_down_z = summed_pieces(down_pieces, "x")
    grad_down = exchanged(column_blocks(grad_down_z.astype(low), z_size), "z")
    grad_down = grad_down.reshape(-1, own_width).astype(jnp.float32)

    def gate_grad(first, second, right):
        lefts, rights = halves(rows_two, y_size), halves(right, x_size)
        if first == "y":
            pieces = [
                summed_pieces([turned_matmul(a, b) for a in lefts], "y").astype(low)
                for b in rights
            ]
        else:
            pieces = [
                summed_pieces([turned_matmul(a, b) for b in rights], "x").astype(low)
                for a in lefts
            ]
        mine = summed_pieces(pieces, second).astype(low)
        blocks = exchanged(mine.reshape(z_size, own_width, -1), "z")
        return joined_columns(blocks).astype(jnp.float32)

    grad_gate = gate_grad("y", "x", grad_gate_act)
    grad_up = gate_grad("x", "y", grad_up_act)

    grad_heads = matmul_turned(grad_attn_rows, o_full).astype(low)
    grad_o_part = turned_matmul(attn_low, grad_attn_rows)
    grad_o_y = summed_pieces(halves(grad_o_part, y_size), "y")
    grad_o = summed_blocks(column_blocks(grad_o_y, z_size), "z")
    grad_queries, grad_kv = attend_back(
        parents, first_seg, query_stack, grad_heads, attended, stats, cosine_lanes, sine_lanes,
        all_kv, kv_local,
    )
    kv_split = grad_kv.reshape(z_size, y_size, seg_count, 2 * kv_cols, SEG)
    y_place = lax.axis_index("y")
    kv_pieces = [
        lax.dynamic_index_in_dim(
            kv_split, lax.rem(y_place - k + y_size, y_size), 1, keepdims=False
        )
        for k in range(y_size)
    ]
    kv_mine = summed_blocks(summed_pieces(kv_pieces, "y"), "z")
    kv_mine = kv_mine.transpose(0, 2, 1).reshape(group_rows, 2 * kv_cols)
    grad_keys = rotary_apply(
        kv_mine[:, :kv_cols].reshape(group_rows, kv_local, HEAD_SIZE),
        cosine_table,
        sine_table,
        -1.0,
    ).reshape(group_rows, kv_cols)
    grad_kv_rows = jnp.concatenate([grad_keys, kv_mine[:, kv_cols:]], axis=1).astype(low)

    def owned_rows(part):
        mine = summed_pieces([part[i * width // y_size : (i + 1) * width // y_size] for i in range(y_size)], "y")
        return summed_blocks(mine.reshape(z_size, own_width, -1), "z")

    grad_q = owned_rows(turned_matmul(rows_one, grad_queries))
    grad_kv_weight = owned_rows(turned_matmul(rows_one, grad_kv_rows))
    input_one = matmul_turned(grad_queries, q_full) + matmul_turned(grad_kv_rows, kv_full)
    grad_rows_one = tensor_sum(input_one.astype(low), local_rows)
    gain_one_part = jnp.sum(grad_rows_one * normed_one, axis=0)
    grad_inputs = grad_middle + norm_back(grad_rows_one, normed_one, inv_one, gain_one)
    grad_tokens = natural_columns(grad_inputs.astype(low))

    gain_parts = jnp.stack([gain_one_part, gain_two_part], axis=0)
    gain_parts = natural_columns(gain_parts).reshape(2, z_size * y_size, 1, own_width)
    gain_parts = jnp.broadcast_to(
        gain_parts, (2, z_size * y_size, tensor_size, own_width)
    ).reshape(2, -1, own_width).transpose(1, 0, 2)
    gain_sums = jnp.sum(exchanged(gain_parts, ("z", "y", "x", "c")), axis=0)
    return (
        mixed,
        grad_tokens,
        gain_sums[0],
        grad_q,
        grad_kv_weight[:, :kv_cols],
        grad_kv_weight[:, kv_cols:],
        grad_o,
        gain_sums[1],
        grad_gate,
        grad_up,
        grad_down,
    )


def solution(mesh):
    dp_size, tensor_size = mesh.shape["dp"], mesh.shape["tensor"]
    fine = jax.sharding.Mesh(
        mesh.devices.reshape(4, dp_size // 4, tensor_size // 2, 2), ("z", "y", "x", "c")
    )
    dp, tensor = ("z", "y"), ("x", "c")
    tokens = P(dp + tensor, None)
    rows = P(dp, tensor)
    columns = P(tensor, dp)
    in_specs = (
        tokens,
        P(dp),
        rows,
        rows,
        rows,
        columns,
        P(dp),
        rows,
        rows,
        columns,
        P(),
        tokens,
    )
    out_specs = (
        tokens,
        tokens,
        P(dp),
        rows,
        rows,
        rows,
        columns,
        P(dp),
        rows,
        rows,
        columns,
    )
    return jax.shard_map(local, mesh=fine, in_specs=in_specs, out_specs=out_specs, check_vma=False)
```

time: 1440 us -> 895 us (0.62)
  waiting for transfers between devices: 712 us -> 411 us
  matrix products: 282 us -> 121 us
  other arithmetic: 104 us -> 51.6 us
  local copies, waits for them, and re-layouts: 92.7 us -> 46.3 us
  Pallas kernels: 0 us -> 38.9 us
    reduce_scatter x9 -> x2, waiting for transfers between devices: 289 us -> 0.03 us  [the longest x1 0.03 us: local(): lax.psum_scatter(mlp_part, ('z', 'c'), scatter_dimension=0, tiled=True)]
    dot_general x52 -> x29, matrix products: 282 us -> 121 us  [the longest x6 41.1 us: nt_dot(): lax.dot_general(left, right, (((1,), (1,)), ((), ())), preferred_element_...]
    all_to_all x0 -> x13, waiting for transfers between devices: none -> 158 us  [the longest x10 125 us: exchanged(): return lax.all_to_all(blocks, axis, 0, 0, tiled=True)]
    ppermute x34 -> x27, starting transfers between devices: 140 us -> 44.7 us  [rotated(): lax.ppermute(value, axis, [(i, (i + step) % size) for i in range(size)])]
    all_to_all x0 -> x13, starting transfers between devices: none -> 90.1 us  [the longest x10 75.8 us: exchanged(): return lax.all_to_all(blocks, axis, 0, 0, tiled=True)]
    all_gather x7 -> x3, waiting for transfers between devices: 68.6 us -> 0.02 us  [the longest x1 0.02 us: local(): group_tokens = lax.all_gather(own_tokens, ('x', 'c'), axis=0, tiled=True)]
    all_to_all x0 -> x2, blocking collectives: none -> 66.6 us  [the longest x1 38.2 us: exchanged(): return lax.all_to_all(blocks, axis, 0, 0, tiled=True)]
    all_gather x2 -> x0, blocking collectives: 64.1 us -> none  [the longest x1 32.2 us: local(): k_full = lax.all_gather(key_matrix, ('z', 'y'), axis=0, tiled=True)]
  transfers between devices with their start and end apart: 52 -> 46, of which waited for: 28 -> 25; matrix products, arithmetic and copies ran while one was open for 18% -> 19% of each run, Pallas kernels for 0% -> 4%
where the time goes in v2:
time: 895 us; the launch traced here: 887 us
  waiting for transfers between devices  411 us (46%)
  starting transfers between devices  135 us (15%)
  matrix products  121 us (14%)
  blocking collectives  66.6 us (7%)
  other arithmetic  51.6 us (6%)
  local copies, waits for them, and re-layouts  46.3 us (5%)
  Pallas kernels  38.9 us (4%)
  between operations  17.3 us (2%)
    ppermute x27, waiting for transfers between devices, rotated(): lax.ppermute(value, axis, [(i, (i + step) % size) for i in range(size)])  253 us
    all_to_all x10, waiting for transfers between devices, exchanged(): return lax.all_to_all(blocks, axis, 0, 0, tiled=True)  125 us
    all_to_all x10, starting transfers between devices, exchanged(): return lax.all_to_all(blocks, axis, 0, 0, tiled=True)  75.8 us
    ppermute x27, starting transfers between devices, rotated(): lax.ppermute(value, axis, [(i, (i + step) % size) for i in range(size)])  44.7 us
    dot_general x6, matrix products, nt_dot(): lax.dot_general(left, right, (((1,), (1,)), ((), ())), preferred_element_...  41.1 us
    dot_general x15, matrix products, turned_matmul(): lax.dot_general(left, right, (((0,), (0,)), ((), ())), preferred_element_...  39.8 us
    dot_general x6, matrix products, matmul(): return jnp.dot(left, right, preferred_element_type=jnp.float32)  39.8 us
    all_to_all x1, blocking collectives, exchanged(): return lax.all_to_all(blocks, axis, 0, 0, tiled=True)  38.2 us
  transfers between devices with their start and end apart: 46, of which 25 were waited for; matrix products, arithmetic and copies ran while one was open for 19% of the time, Pallas kernels for 4%

profile of v2, /device:TPU:0, one launch (start us, length us, event | category | flops | bytes accessed | tf_op | source)
XLA Modules:
  0.0 887.4 jit_solution(1219901236830466433)
XLA Ops:
  19.5 14.1 %all-to-all-done = bf16[4,258,256]{2,1,0:T(8,128)(2,1)S(1)} async-done(((bf16[4,258,256]{2,1,0:T(8,128)(2,1)}), bf16[4,258,256]{2,1,0:T(8,128)(2,1)S(1)}, u32[]{:S(2)}, u32[]{:S(2)}) %all-to-all-start) | async-done | bytes 528416 | tf_op jit(solution)/shard_map/all_to_all | solution.py:70
  51.7 14.9 %all-to-all-done.1 = bf16[4,256,512]{2,1,0:T(8,128)(2,1)S(1)} async-done(((bf16[4,256,512]{2,1,0:T(8,128)(2,1)}), bf16[4,256,512]{2,1,0:T(8,128)(2,1)S(1)}, u32[]{:S(2)}, u32[]{:S(2)}) %all-to-all-start.1) | async-done | bytes 1048608 | tf_op jit(solution)/shard_map/all_to_all | solution.py:70
  66.9 28.4 %all_to_all.75 = bf16[4,512,256]{2,1,0:T(8,128)(2,1)} all-to-all(bf16[4,512,256]{2,1,0:T(8,128)(2,1)S(1)} %broadcast_in_dim.14), channel_id=1, replica_groups=mesh['z'=4,'y'=2,'x'=2,'c'=2] {'z'}, dimensions={0} | all-to-all | bytes 2097152 | tf_op jit(solution)/shard_map/all_to_all | solution.py:70
  103.6 40.5 %all-to-all-done.3 = bf16[4,256,512]{1,2,0:T(8,128)(2,1)S(1)} async-done(((bf16[4,256,512]{1,2,0:T(8,128)(2,1)}), bf16[4,256,512]{1,2,0:T(8,128)(2,1)S(1)}, u32[]{:S(2)}, u32[]{:S(2)}) %all-to-all-start.3) | async-done | bytes 1048608 | tf_op jit(solution)/shard_map/all_to_all | solution.py:74
  154.8 22.4 %collective-permute-done.1 = bf16[4,256,512]{2,1,0:T(8,128)(2,1)} collective-permute-done((bf16[4,256,512]{2,1,0:T(8,128)(2,1)S(1)}, bf16[4,256,512]{2,1,0:T(8,128)(2,1)}, u32[]{:S(2)}, u32[]{:S(2)}) %collective-permute-start.1) | collective-permute-done | bytes 1048608 | tf_op jit(solution)/shard_map/ppermute | solution.py:52
  186.7 13.0 %collective-permute-done.2 = bf16[4,512,256]{2,1,0:T(8,128)(2,1)} collective-permute-done((bf16[4,512,256]{2,1,0:T(8,128)(2,1)}, bf16[4,512,256]{2,1,0:T(8,128)(2,1)}, u32[]{:S(2)}, u32[]{:S(2)}) %collective-permute-start.2) | collective-permute-done | bytes 1048608 | tf_op jit(solution)/shard_map/ppermute | solution.py:52
  202.9 19.2 %shard_map.203 = (f32[512,512]{1,0:T(8,128)}, bf16[512,512]{1,0:T(8,128)(2,1)}, f32[2,2,1024,1]{3,2,1,0:T(8,128)}, bf16[2,2,1024,128]{3,2,1,0:T(8,128)(2,1)}) custom-call(s32[16]{0:T(128)} %parents.3, s32[1]{0:T(128)} %bitcast.first_seg, f32[512,512]{1,0:T(8,128)} %fusion.114.proj, f32[512,128]{1,0:T(8,128)} %copy.184.cosine, f32[512,128]{1,0:T(8,128)} %copy.185.sine, ...), custom_call_target="tpu_custom_call" | custom-call | flops 4294967296 | bytes 8388608 | tf_op jit(solution)/shard_map/pallas_call | solution.py:316
  233.7 28.8 %all-to-all-start.5 = ((bf16[4,256,512]{1,2,0:T(8,128)(2,1)}), bf16[4,256,512]{1,2,0:T(8,128)(2,1)S(1)}, u32[]{:S(2)}, u32[]{:S(2)}) async-start(bf16[4,256,512]{1,2,0:T(8,128)(2,1)} %bitcast.31), calls=%async_computation.5 | async-start | bytes 2097152 | tf_op jit(solution)/shard_map/all_to_all | solution.py:74
  265.2 40.1 %all-to-all-done.5 = bf16[4,256,512]{1,2,0:T(8,128)(2,1)S(1)} async-done(((bf16[4,256,512]{1,2,0:T(8,128)(2,1)}), bf16[4,256,512]{1,2,0:T(8,128)(2,1)S(1)}, u32[]{:S(2)}, u32[]{:S(2)}) %all-to-all-start.5) | async-done | bytes 1048608 | tf_op jit(solution)/shard_map/all_to_all | solution.py:74
  306.5 38.2 %all_to_all.76 = bf16[4,512,256]{2,1,0:T(8,128)(2,1)S(1)} all-to-all(bf16[4,512,256]{2,1,0:T(8,128)(2,1)} %bitcast.242), channel_id=1, replica_groups=mesh['z'=4,'y'=2,'x'=2,'c'=2] {'z'}, dimensions={0} | all-to-all | bytes 2097152 | tf_op jit(solution)/shard_map/all_to_all | solution.py:74
  347.4 24.1 %collective-permute-done.10 = bf16[512,1024]{0,1:T(8,128)(2,1)S(1)} collective-permute-done((bf16[512,1024]{0,1:T(8,128)(2,1)S(1)}, bf16[512,1024]{0,1:T(8,128)(2,1)S(1)}, u32[]{:S(2)}, u32[]{:S(2)}) %collective-permute-start.10) | collective-permute-done | bytes 1048608 | tf_op jit(solution)/shard_map/ppermute | solution.py:52
  375.2 16.3 %collective-permute-done.8 = bf16[1024,512]{1,0:T(8,128)(2,1)S(1)} collective-permute-done((bf16[1024,512]{1,0:T(8,128)(2,1)}, bf16[1024,512]{1,0:T(8,128)(2,1)S(1)}, u32[]{:S(2)}, u32[]{:S(2)}) %collective-permute-start.8) | collective-permute-done | bytes 1048608 | tf_op jit(solution)/shard_map/ppermute | solution.py:52
  393.7 50.7 %collective-permute-done.6 = bf16[1024,512]{1,0:T(8,128)(2,1)S(1)} collective-permute-done((bf16[1024,512]{1,0:T(8,128)(2,1)S(1)}, bf16[1024,512]{1,0:T(8,128)(2,1)S(1)}, u32[]{:S(2)}, u32[]{:S(2)}) %collective-permute-start.6) | collective-permute-done | bytes 1048608 | tf_op jit(solution)/shard_map/ppermute | solution.py:52
  456.0 27.7 %collective-permute-done.9 = bf16[1024,1024]{1,0:T(8,128)(2,1)} collective-permute-done((bf16[1024,1024]{1,0:T(8,128)(2,1)}, bf16[1024,1024]{1,0:T(8,128)(2,1)}, u32[]{:S(2)}, u32[]{:S(2)}) %collective-permute-start.9) | collective-permute-done | bytes 2097184 | tf_op jit(solution)/shard_map/ppermute | solution.py:52
  493.7 12.6 %multiply_convert_fusion.1 = (bf16[1024,1024]{1,0:T(8,128)(2,1)S(1)}, bf16[1024,1024]{1,0:T(8,128)(2,1)S(1)}, bf16[1024,1024]{1,0:T(8,128)(2,1)}) fusion(f32[1024,1024]{1,0:T(8,128)S(1)} %copy-done.73, f32[1024,1024]{1,0:T(8,128)} %fusion.19, bf16[1024,2048]{1,0:T(8,128)(2,1)S(1)} %copy-done.59, bf16[2048,512]{1,0:T(8,128)(2,1)} %collective-permute-done.7, ...), kind=kOutput, calls=%fused_computation.11 | convolution fusion | flops 4323278848 | bytes 23068672 | tf_op jit(solution)/shard_map/dot_general | solution.py:380
  506.3 11.0 %fusion.18 = f32[1024,2048]{1,0:T(8,128)} fusion(bf16[1024,1024]{1,0:T(8,128)(2,1)S(1)} %get-tuple-element.42, bf16[1024,1024]{1,0:T(8,128)(2,1)} %collective-permute-done.9, bf16[1024,512]{1,0:T(8,128)(2,1)S(1)} %copy-done.30, bf16[1024,512]{1,0:T(8,128)(2,1)S(1)} %bitcast.225), kind=kOutput, calls=%fused_computation.58 | convolution fusion | flops 4307550208 | bytes 14680064 | tf_op jit(solution)/shard_map/dot_general | solution.py:171
  547.5 33.2 %collective-permute-done.25 = bf16[512,1024]{1,0:T(8,128)(2,1)S(1)} collective-permute-done((bf16[512,1024]{1,0:T(8,128)(2,1)S(1)}, bf16[512,1024]{1,0:T(8,128)(2,1)S(1)}, u32[]{:S(2)}, u32[]{:S(2)}) %collective-permute-start.25) | collective-permute-done | bytes 1048608 | tf_op jit(solution)/shard_map/ppermute | solution.py:52
  597.7 15.7 %collective-permute-done.26 = bf16[512,1024]{1,0:T(8,128)(2,1)S(1)} collective-permute-done((bf16[512,1024]{1,0:T(8,128)(2,1)}, bf16[512,1024]{1,0:T(8,128)(2,1)S(1)}, u32[]{:S(2)}, u32[]{:S(2)}) %collective-permute-start.26) | collective-permute-done | bytes 1048608 | tf_op jit(solution)/shard_map/ppermute | solution.py:52
  653.5 19.7 %shard_map.204 = (bf16[512,512]{1,0:T(8,128)(2,1)}, bf16[16,256,256]{2,1,0:T(8,128)(2,1)}) custom-call(s32[16]{0:T(128)} %parents.3, s32[1]{0:T(128)} %bitcast.first_seg, bf16[2,2,1024,128]{3,2,1,0:T(8,128)(2,1)} %get-tuple-element.30.queries, bf16[512,512]{1,0:T(8,128)(2,1)} %fusion.55.grads, f32[512,512]{1,0:T(8,128)} %get-tuple-element.31.attended, ...), custom_call_target="tpu_custom_call" | custom-call | flops 10737418240 | bytes 8388608 | tf_op jit(solution)/shard_map/pallas_call | solution.py:344
  675.5 20.5 %collective-permute-start.12 = (bf16[4,2,256,256]{3,2,1,0:T(8,128)(2,1)}, bf16[4,2,256,256]{3,2,1,0:T(8,128)(2,1)}, u32[]{:S(2)}, u32[]{:S(2)}) collective-permute-start(bf16[4,2,256,256]{3,2,1,0:T(8,128)(2,1)} %dynamic-slice_bitcast_fusion.1), channel_id=1, source_target_pairs={{0,4},{4,0},{1,5},{5,1},{2,6},{6,2},{3,7},{7,3},{8,12},{12,8},{9,1... | collective-permute-start | bytes 3145736 | tf_op jit(solution)/shard_map/ppermute | solution.py:52
  696.0 12.5 %all-to-all-start.12 = ((bf16[4,256,512]{2,1,0:T(8,128)(2,1)}), bf16[4,256,512]{2,1,0:T(8,128)(2,1)S(1)}, u32[]{:S(2)}, u32[]{:S(2)}) async-start(bf16[4,256,512]{2,1,0:T(8,128)(2,1)} %bitcast.200), calls=%async_computation.14 | async-start | bytes 2097152 | tf_op jit(solution)/shard_map/all_to_all | solution.py:74
  742.0 20.8 %collective-permute-done.17 = bf16[512,1024]{1,0:T(8,128)(2,1)S(1)} collective-permute-done((bf16[512,1024]{1,0:T(8,128)(2,1)S(1)}, bf16[512,1024]{1,0:T(8,128)(2,1)S(1)}, u32[]{:S(2)}, u32[]{:S(2)}) %collective-permute-start.17) | collective-permute-done | bytes 1048608 | tf_op jit(solution)/shard_map/ppermute | solution.py:52
  764.2 10.6 %all-to-all-done.7 = bf16[4,2,256,256]{3,2,1,0:T(8,128)(2,1)} async-done(((bf16[4,2,256,256]{3,2,1,0:T(8,128)(2,1)}), bf16[4,2,256,256]{3,2,1,0:T(8,128)(2,1)}, u32[]{:S(2)}, u32[]{:S(2)}) %all-to-all-start.7) | async-done | bytes 1048608 | tf_op jit(solution)/shard_map/all_to_all | solution.py:74
  793.2 16.5 %all-to-all-done.11 = bf16[4,512,256]{2,1,0:T(8,128)(2,1)} async-done(((bf16[4,512,256]{2,1,0:T(8,128)(2,1)}), bf16[4,512,256]{2,1,0:T(8,128)(2,1)}, u32[]{:S(2)}, u32[]{:S(2)}) %all-to-all-start.11) | async-done | bytes 1048608 | tf_op jit(solution)/shard_map/all_to_all | solution.py:74
  (372 shorter events, 318.7 us)
Async XLA Ops:
  8.0 40.1 %all-gather.5.cloned.1.call-start = ((), (), s32[]{:S(2)}) async-start(), calls=%async_computation.17 | async-start | bytes 2621440 | tf_op jit(solution)/shard_map/all_gather | solution.py:435
  97.6 46.5 %all-to-all-start.3 = ((bf16[4,256,512]{1,2,0:T(8,128)(2,1)}), bf16[4,256,512]{1,2,0:T(8,128)(2,1)S(1)}, u32[]{:S(2)}, u32[]{:S(2)}) async-start(bf16[4,256,512]{1,2,0:T(8,128)(2,1)} %bitcast.18), calls=%async_computation.3 | async-start | bytes 2097152 | tf_op jit(solution)/shard_map/all_to_all | solution.py:74
  101.1 345.2 %all-gather.9.cloned.1.call-start = ((), (), s32[]{:S(2)}) async-start(), calls=%async_computation.20 | async-start | bytes 4718592 | tf_op jit(solution)/shard_map/all_gather | solution.py:511
  151.4 48.4 %collective-permute-start.2 = (bf16[4,512,256]{2,1,0:T(8,128)(2,1)}, bf16[4,512,256]{2,1,0:T(8,128)(2,1)}, u32[]{:S(2)}, u32[]{:S(2)}) collective-permute-start(bf16[4,512,256]{2,1,0:T(8,128)(2,1)} %all_to_all.75), channel_id=1, source_target_pairs={{0,4},{4,0},{1,5},{5,1},{2,6},{6,2},{3,7},{7,3},{8,12},{12,8},{9,1... | collective-permute-start | bytes 3145736 | tf_op jit(solution)/shard_map/ppermute | solution.py:52
  233.7 71.5 %all-to-all-start.5 = ((bf16[4,256,512]{1,2,0:T(8,128)(2,1)}), bf16[4,256,512]{1,2,0:T(8,128)(2,1)S(1)}, u32[]{:S(2)}, u32[]{:S(2)}) async-start(bf16[4,256,512]{1,2,0:T(8,128)(2,1)} %bitcast.31), calls=%async_computation.5 | async-start | bytes 2097152 | tf_op jit(solution)/shard_map/all_to_all | solution.py:74
  262.5 221.1 %all-gather.7.cloned.1.call-start = ((), (), s32[]{:S(2)}) async-start(), calls=%async_computation.18 | async-start | bytes 4718592 | tf_op jit(solution)/shard_map/all_gather | solution.py:509
  265.1 319.1 %reduce-scatter.5.cloned.1.call-start = ((), (), s32[]{:S(2)}) async-start(), calls=%async_computation.21 | async-start | bytes 4718592 | tf_op jit(solution)/shard_map/reduce_scatter | solution.py:525
  345.7 45.8 %collective-permute-start.8 = (bf16[1024,512]{1,0:T(8,128)(2,1)}, bf16[1024,512]{1,0:T(8,128)(2,1)S(1)}, u32[]{:S(2)}, u32[]{:S(2)}) collective-permute-start(bf16[1024,512]{1,0:T(8,128)(2,1)} %bitcast.222), channel_id=1, source_target_pairs={{0,2},{2,0},{1,3},{3,1},{4,6},{6,4},{5,7},{7,5},{8,10},{10,8},{9,1... | collective-permute-start | bytes 3145736 | tf_op jit(solution)/shard_map/ppermute | solution.py:52
  373.2 73.2 %collective-permute-start.11 = (bf16[1024,1024]{0,1:T(8,128)(2,1)}, bf16[1024,1024]{0,1:T(8,128)(2,1)}, u32[]{:S(2)}, u32[]{:S(2)}) collective-permute-start(bf16[1024,1024]{0,1:T(8,128)(2,1)} %pad_maximum_fusion.8), channel_id=1, source_target_pairs={{0,4},{4,0},{1,5},{5,1},{2,6},{6,2},{3,7},{7,3},{8,12},{12,8},{9,1... | collective-permute-start | bytes 6291464 | tf_op jit(solution)/shard_map/ppermute | solution.py:52
  373.2 71.2 %collective-permute-start.6 = (bf16[1024,512]{1,0:T(8,128)(2,1)S(1)}, bf16[1024,512]{1,0:T(8,128)(2,1)S(1)}, u32[]{:S(2)}, u32[]{:S(2)}) collective-permute-start(bf16[1024,512]{1,0:T(8,128)(2,1)S(1)} %bitcast.217), channel_id=1, source_target_pairs={{0,4},{4,0},{1,5},{5,1},{2,6},{6,2},{3,7},{7,3},{8,12},{12,8},{9,1... | collective-permute-start | bytes 3145736 | tf_op jit(solution)/shard_map/ppermute | solution.py:52
  393.2 90.5 %collective-permute-start.9 = (bf16[1024,1024]{1,0:T(8,128)(2,1)}, bf16[1024,1024]{1,0:T(8,128)(2,1)}, u32[]{:S(2)}, u32[]{:S(2)}) collective-permute-start(bf16[1024,1024]{1,0:T(8,128)(2,1)} %pad_maximum_fusion.7), channel_id=1, source_target_pairs={{0,4},{4,0},{1,5},{5,1},{2,6},{6,2},{3,7},{7,3},{8,12},{12,8},{9,1... | collective-permute-start | bytes 6291464 | tf_op jit(solution)/shard_map/ppermute | solution.py:52
  446.1 47.6 %collective-permute-start.7 = (bf16[2048,512]{1,0:T(8,128)(2,1)}, bf16[2048,512]{1,0:T(8,128)(2,1)}, u32[]{:S(2)}, u32[]{:S(2)}) collective-permute-start(bf16[2048,512]{1,0:T(8,128)(2,1)} %pad_maximum_fusion.6), channel_id=1, source_target_pairs={{0,2},{2,0},{1,3},{3,1},{4,6},{6,4},{5,7},{7,5},{8,10},{10,8},{9,1... | collective-permute-start | bytes 6291464 | tf_op jit(solution)/shard_map/ppermute | solution.py:52
  526.4 122.9 %all-gather.11.cloned.1.call-start = ((), (), s32[]{:S(2)}) async-start(), calls=%async_computation.22 | async-start | bytes 2621440 | tf_op jit(solution)/shard_map/all_gather | solution.py:536
  532.0 61.6 %collective-permute-start.24 = (bf16[512,1024]{1,0:T(8,128)(2,1)}, bf16[512,1024]{1,0:T(8,128)(2,1)}, u32[]{:S(2)}, u32[]{:S(2)}) collective-permute-start(bf16[512,1024]{1,0:T(8,128)(2,1)} %fusion.21), channel_id=1, source_target_pairs={{0,4},{4,0},{1,5},{5,1},{2,6},{6,2},{3,7},{7,3},{8,12},{12,8},{9,1... | collective-permute-start | bytes 3145736 | tf_op jit(solution)/shard_map/ppermute | solution.py:52
  534.3 46.4 %collective-permute-start.25 = (bf16[512,1024]{1,0:T(8,128)(2,1)S(1)}, bf16[512,1024]{1,0:T(8,128)(2,1)S(1)}, u32[]{:S(2)}, u32[]{:S(2)}) collective-permute-start(bf16[512,1024]{1,0:T(8,128)(2,1)S(1)} %fusion.24), channel_id=1, source_target_pairs={{0,4},{4,0},{1,5},{5,1},{2,6},{6,2},{3,7},{7,3},{8,12},{12,8},{9,1... | collective-permute-start | bytes 3145736 | tf_op jit(solution)/shard_map/ppermute | solution.py:52
  537.7 93.9 %collective-permute-start.21 = (bf16[1024,512]{1,0:T(8,128)(2,1)}, bf16[1024,512]{1,0:T(8,128)(2,1)}, u32[]{:S(2)}, u32[]{:S(2)}) collective-permute-start(bf16[1024,512]{1,0:T(8,128)(2,1)} %convolution_convert_fusion.3), channel_id=1, source_target_pairs={{0,2},{2,0},{1,3},{3,1},{4,6},{6,4},{5,7},{7,5},{8,10},{10,8},{9,1... | collective-permute-start | bytes 3145736 | tf_op jit(solution)/shard_map/ppermute | solution.py:52
  541.2 47.4 %collective-permute-start.22 = (bf16[1024,512]{1,0:T(8,128)(2,1)}, bf16[1024,512]{1,0:T(8,128)(2,1)}, u32[]{:S(2)}, u32[]{:S(2)}) collective-permute-start(bf16[1024,512]{1,0:T(8,128)(2,1)} %convolution_convert_fusion.2), channel_id=1, source_target_pairs={{0,2},{2,0},{1,3},{3,1},{4,6},{6,4},{5,7},{7,5},{8,10},{10,8},{9,1... | collective-permute-start | bytes 3145736 | tf_op jit(solution)/shard_map/ppermute | solution.py:52
  544.2 89.8 %collective-permute-start.18 = (bf16[1024,512]{1,0:T(8,128)(2,1)}, bf16[1024,512]{1,0:T(8,128)(2,1)}, u32[]{:S(2)}, u32[]{:S(2)}) collective-permute-start(bf16[1024,512]{1,0:T(8,128)(2,1)} %convolution_convert_fusion.5), channel_id=1, source_target_pairs={{0,4},{4,0},{1,5},{5,1},{2,6},{6,2},{3,7},{7,3},{8,12},{12,8},{9,1... | collective-permute-start | bytes 3145736 | tf_op jit(solution)/shard_map/ppermute | solution.py:52
  593.6 48.1 %collective-permute-start.23 = (bf16[1024,512]{1,0:T(8,128)(2,1)}, bf16[1024,512]{1,0:T(8,128)(2,1)S(1)}, u32[]{:S(2)}, u32[]{:S(2)}) collective-permute-start(bf16[1024,512]{1,0:T(8,128)(2,1)} %add_convert_fusion.6), channel_id=1, source_target_pairs={{0,4},{4,0},{1,5},{5,1},{2,6},{6,2},{3,7},{7,3},{8,12},{12,8},{9,1... | collective-permute-start | bytes 3145736 | tf_op jit(solution)/shard_map/ppermute | solution.py:52
  643.0 53.1 %all-to-all-start.13 = ((bf16[4,256,512]{2,1,0:T(8,128)(2,1)}), bf16[4,256,512]{2,1,0:T(8,128)(2,1)S(1)}, u32[]{:S(2)}, u32[]{:S(2)}) async-start(bf16[4,256,512]{2,1,0:T(8,128)(2,1)} %bitcast.201), calls=%async_computation.15 | async-start | bytes 2097152 | tf_op jit(solution)/shard_map/all_to_all | solution.py:74
  675.5 42.4 %collective-permute-start.12 = (bf16[4,2,256,256]{3,2,1,0:T(8,128)(2,1)}, bf16[4,2,256,256]{3,2,1,0:T(8,128)(2,1)}, u32[]{:S(2)}, u32[]{:S(2)}) collective-permute-start(bf16[4,2,256,256]{3,2,1,0:T(8,128)(2,1)} %dynamic-slice_bitcast_fusion.1), channel_id=1, source_target_pairs={{0,4},{4,0},{1,5},{5,1},{2,6},{6,2},{3,7},{7,3},{8,12},{12,8},{9,1... | collective-permute-start | bytes 3145736 | tf_op jit(solution)/shard_map/ppermute | solution.py:52
  708.5 159.4 %reduce-scatter.3.cloned.1.call-start = ((), (), s32[]{:S(2)}) async-start(), calls=%async_computation.19 | async-start | bytes 4718592 | tf_op jit(solution)/shard_map/reduce_scatter | solution.py:528
  728.4 46.4 %all-to-all-start.7 = ((bf16[4,2,256,256]{3,2,1,0:T(8,128)(2,1)}), bf16[4,2,256,256]{3,2,1,0:T(8,128)(2,1)}, u32[]{:S(2)}, u32[]{:S(2)}) async-start(bf16[4,2,256,256]{3,2,1,0:T(8,128)(2,1)} %fusion.7), calls=%async_computation.9 | async-start | bytes 2097152 | tf_op jit(solution)/shard_map/all_to_all | solution.py:74
  740.8 41.9 %collective-permute-start.15 = (bf16[1024,512]{1,0:T(8,128)(2,1)}, bf16[1024,512]{1,0:T(8,128)(2,1)}, u32[]{:S(2)}, u32[]{:S(2)}) collective-permute-start(bf16[1024,512]{1,0:T(8,128)(2,1)} %slice.332), channel_id=1, source_target_pairs={{0,4},{4,0},{1,5},{5,1},{2,6},{6,2},{3,7},{7,3},{8,12},{12,8},{9,1... | collective-permute-start | bytes 3145736 | tf_op jit(solution)/shard_map/ppermute | solution.py:52
  (96 other events, 2031.9 us)
Sparse Core Ops, SparseCore 0:
  11.7 25.3 all-gather.4
  588.7 25.5 all-gather.10
Sparse Core Ops, SparseCore 1:
  103.8 76.1 all-gather.8
  265.2 78.7 all-gather.6
  526.5 47.0 reduce-scatter.4
  718.0 78.2 reduce-scatter.2

commit v3 on v2

v3 whole, which is shorter than its diff:
```python
import functools

import jax
import jax.numpy as jnp
from jax import lax
from jax.experimental import pallas as pl
from jax.experimental.pallas import tpu as pltpu
from jax.sharding import PartitionSpec as P

HEAD_SIZE = 64
SEG = 256
MAX_STEPS = 9
LANES = 2 * HEAD_SIZE
KERNEL_VMEM = 56 * 2**20
SMALL_COST = pl.CostEstimate(flops=2**28, bytes_accessed=2**18, transcendentals=0)


attn_scale = 0.015625
branch_scale = 0.22
norm_eps = 1e-05
rope_base = 10000000.0
masked_score = -1e30


def segment_depth(parents):
    seg_total = parents.shape[0]
    seg_ids = jnp.arange(seg_total, dtype=jnp.int32)
    reach = (parents[:, None] == seg_ids[None, :]) | (seg_ids[:, None] == seg_ids[None, :])
    reach = reach.astype(jnp.float32)
    for doubling in range(4):
        reach = jnp.minimum(jnp.dot(reach, reach, preferred_element_type=jnp.float32), 1.0)
    return jnp.sum(reach, axis=1).astype(jnp.int32) - 1


def rope_tables(position, head_dim):
    half_dim = head_dim // 2
    exponent = jnp.arange(half_dim, dtype=jnp.float32) * (2.0 / head_dim)
    inverse = jnp.power(rope_base, -exponent)
    angles = position.astype(jnp.float32)[:, None] * inverse[None, :]
    return (jnp.cos(angles), jnp.sin(angles))


def rotated(value, axis, step):
    size = lax.axis_size(axis)
    return lax.ppermute(value, axis, [(i, (i + step) % size) for i in range(size)])


def relative_pieces(value, axis):
    return [value] + [rotated(value, axis, k) for k in range(1, lax.axis_size(axis))]


def natural_pieces(pieces, axis):
    size = len(pieces)
    place = lax.axis_index(axis)
    return [
        lax.select_n(place, *[pieces[(i - j) % size] for i in range(size)]) for j in range(size)
    ]


def gathered(value, axis):
    size = lax.axis_size(axis)
    copies = jnp.broadcast_to(value[None], (size, *value.shape))
    return lax.all_to_all(copies, axis, 0, 0, tiled=True)


def exchanged(blocks, axis):
    return lax.all_to_all(blocks, axis, 0, 0, tiled=True)


def summed_pieces(pieces, axis):
    sent = [rotated(pieces[k].astype(jnp.bfloat16), axis, -k) for k in range(1, len(pieces))]
    total = pieces[0].astype(jnp.float32)
    for value in sent:
        total = total + value.astype(jnp.float32)
    return total


def summed_blocks(blocks, axis):
    return jnp.sum(exchanged(blocks.astype(jnp.bfloat16), axis).astype(jnp.float32), axis=0)


def column_blocks(value, count):
    return value.reshape(value.shape[0], count, -1).transpose(1, 0, 2)


def joined_columns(blocks):
    return blocks.transpose(1, 0, 2).reshape(blocks.shape[1], -1)


def relative_columns(value):
    size = lax.axis_size("y")
    place = lax.axis_index("y")
    rows = value.shape[0]
    split = value.reshape(rows, lax.axis_size("z"), size, -1)
    flat = [split[:, :, i].reshape(rows, -1) for i in range(size)]
    return jnp.concatenate(
        [
            lax.select_n(place, *[flat[(i - k) % size] for i in range(size)])
            for k in range(size)
        ],
        axis=1,
    )


def natural_columns(value):
    size = lax.axis_size("y")
    rows = value.shape[0]
    split = value.reshape(rows, size, lax.axis_size("z"), -1)
    parts = natural_pieces([split[:, k] for k in range(size)], "y")
    return jnp.stack(parts, axis=2).reshape(rows, -1)


def together(*values):
    return lax.optimization_barrier(values)


def ancestor_count(parents, seg):
    def climb(step, state):
        current, count = state
        above = parents[current]
        return above, count + jnp.where(above != current, 1, 0)

    return lax.fori_loop(0, MAX_STEPS, climb, (seg, jnp.int32(1)))[1]


def left_lanes(shape):
    return lax.broadcasted_iota(jnp.int32, shape, 1) < HEAD_SIZE


def stacked_heads(pairs, to_left):
    left = left_lanes(pairs[0].shape)
    stack = []
    for pair in pairs:
        swapped = pltpu.roll(pair, HEAD_SIZE, 1)
        for head in (pair, swapped) if to_left else (swapped, pair):
            stack.append(jnp.where(left, head, 0.0) if to_left else jnp.where(left, 0.0, head))
    return jnp.concatenate(stack, axis=0)


def unstacked_heads(stack, from_left):
    left = left_lanes((SEG, 2 * HEAD_SIZE))
    pairs = []
    for first in range(0, stack.shape[0], 2 * SEG):
        even, odd = stack[first : first + SEG], stack[first + SEG : first + 2 * SEG]
        if from_left:
            odd = pltpu.roll(odd, HEAD_SIZE, 1)
        else:
            even = pltpu.roll(even, HEAD_SIZE, 1)
        pairs.append(jnp.where(left, even, odd))
    return pairs


def turned(value, cosine, sine, direction):
    half = HEAD_SIZE // 2
    lane = lax.broadcasted_iota(jnp.int32, value.shape, 1)
    first = lax.rem(lane, HEAD_SIZE) < half
    ahead = pltpu.roll(value, LANES - half, 1)
    behind = pltpu.roll(value, half, 1)
    signed = sine * direction
    return value * cosine + jnp.where(first, -ahead * signed, behind * signed)


def nt_dot(left, right):
    return lax.dot_general(
        left, right, (((1,), (1,)), ((), ())), preferred_element_type=jnp.float32
    )


def nn_dot(left, right):
    return lax.dot_general(
        left, right, (((1,), (0,)), ((), ())), preferred_element_type=jnp.float32
    )


def causal_tile(rows):
    query = lax.rem(lax.broadcasted_iota(jnp.int32, (rows, SEG), 0), SEG)
    return lax.broadcasted_iota(jnp.int32, (rows, SEG), 1) <= query


def lane_blocks(ref):
    return [ref[:, at : at + LANES] for at in range(0, ref.shape[1], LANES)]


def project_kernel(parts, rows, *refs):
    weights, (cosine, sine, out) = refs[:parts], refs[parts:]
    depth = weights[0].shape[0]
    product = sum(nn_dot(rows[:, i * depth : (i + 1) * depth], w[...]) for i, w in enumerate(weights))
    cos, sin = cosine[...], sine[...]
    for at in range(0, product.shape[1], LANES):
        block = turned(product[:, at : at + LANES], cos, sin, 1.0)
        out[:, at : at + LANES] = block.astype(jnp.bfloat16)


def project(rows, weights, cosine, sine):
    count, width = rows.shape
    depth, cols = weights[0].shape
    step = 2 * LANES
    table = pl.BlockSpec((count, LANES), lambda j: (0, 0))
    return pl.pallas_call(
        functools.partial(project_kernel, len(weights)),
        grid=(cols // step,),
        in_specs=[pl.BlockSpec((count, width), lambda j: (0, 0))]
        + [pl.BlockSpec((depth, step), lambda j: (0, j))] * len(weights)
        + [table, table],
        out_specs=pl.BlockSpec((count, step), lambda j: (0, j)),
        out_shape=jax.ShapeDtypeStruct((count, cols), jnp.bfloat16),
        compiler_params=pltpu.CompilerParams(vmem_limit_bytes=KERNEL_VMEM),
        cost_estimate=SMALL_COST,
    )(rows, *weights, cosine, sine)


def attend_kernel(parents, segs, queries, keys_values, out, stats, scores):
    seg = segs[pl.program_id(0)]
    count = ancestor_count(parents, seg)
    pairs = [block.astype(jnp.float32) * attn_scale for block in lane_blocks(queries)]
    stack = stacked_heads(pairs, True).astype(jnp.bfloat16)
    rows = stack.shape[0]

    first = jnp.where(causal_tile(rows), nt_dot(stack, keys_values[seg]), masked_score)
    scores[0] = first

    def folded(tile):
        return jnp.maximum(tile[:, :LANES], tile[:, LANES:])

    def measure(step, state):
        current, top = state
        current = parents[current]
        tile = nt_dot(stack, keys_values[current])
        scores[step] = tile
        return current, jnp.maximum(top, folded(tile))

    top = lax.fori_loop(1, count, measure, (seg, folded(first)))[1]
    row_max = jnp.max(top, axis=1, keepdims=True)
    left = left_lanes((SEG, LANES))

    def gather(step, state):
        current, mixed = state
        terms = jnp.exp(scores[step] - row_max).astype(jnp.bfloat16)
        tile = jnp.where(left, jnp.ones((SEG, LANES), jnp.bfloat16), keys_values[current])
        return parents[current], mixed + nn_dot(terms, tile)

    start = (seg, jnp.zeros((rows, LANES), jnp.float32))
    mixed = lax.fori_loop(0, count, gather, start)[1]
    total = mixed[:, :1]
    mixed = mixed / total
    stats[0] = row_max + jnp.log(total)
    for place, pair in enumerate(unstacked_heads(mixed, False)):
        out[:, place * LANES : (place + 1) * LANES] = pair


def attend_back_kernel(
    parents, segs, queries, grads, attended, stats, cosine, sine, keys_values, *refs
):
    earlier, (grad_queries, grad_kv, kv_sum) = refs[:-3], refs[-3:]
    seg = segs[pl.program_id(0)]
    count = ancestor_count(parents, seg)

    @pl.when(pl.program_id(0) == 0)
    def _():
        kv_sum[...] = earlier[0][...] if earlier else jnp.zeros_like(kv_sum)

    query_pairs = [block.astype(jnp.float32) * attn_scale for block in lane_blocks(queries)]
    grad_pairs = [block.astype(jnp.float32) for block in lane_blocks(grads)]
    left = left_lanes((SEG, LANES))
    deltas = []
    for pair, out in zip(grad_pairs, lane_blocks(attended)):
        product = pair * out
        deltas.append(jnp.sum(jnp.where(left, product, 0.0), axis=1, keepdims=True))
        deltas.append(jnp.sum(jnp.where(left, 0.0, product), axis=1, keepdims=True))
    delta = jnp.concatenate(deltas, axis=0)
    query_wide = stacked_heads(query_pairs, True)
    grad_wide = stacked_heads(grad_pairs, False)
    query_stack, grad_stack = query_wide.astype(jnp.bfloat16), grad_wide.astype(jnp.bfloat16)
    query_turned = query_wide.T.astype(jnp.bfloat16)
    grad_turned = grad_wide.T.astype(jnp.bfloat16)
    log_total = stats[0]
    rows = query_stack.shape[0]

    def visit(current, total, diagonal):
        tile_kv = keys_values[current]
        tile = nt_dot(query_stack, tile_kv)
        if diagonal:
            tile = jnp.where(causal_tile(rows), tile, masked_score)
        probs = jnp.exp(tile - log_total)
        grad_probs = nt_dot(grad_stack, tile_kv)
        grad_tile = (probs * (grad_probs - delta)).astype(jnp.bfloat16)
        kv_sum[current] += nn_dot(query_turned, grad_tile) + nn_dot(
            grad_turned, probs.astype(jnp.bfloat16)
        )
        return total + nn_dot(grad_tile, tile_kv)

    total = visit(seg, jnp.zeros((rows, LANES), jnp.float32), True)

    def climb(step, state):
        current, total = state
        current = parents[current]
        return current, visit(current, total, False)

    total = lax.fori_loop(1, count, climb, (seg, total))[1]
    cos, sin = cosine[...], sine[...]
    for place, pair in enumerate(unstacked_heads(total * attn_scale, True)):
        grad_queries[:, place * LANES : (place + 1) * LANES] = turned(
            pair, cos, sin, -1.0
        ).astype(jnp.bfloat16)

    @pl.when(pl.program_id(0) == pl.num_programs(0) - 1)
    def _():
        grad_kv[...] = kv_sum[...].astype(grad_kv.dtype)


def attention_specs(cols, seg_total):
    block = pl.BlockSpec((SEG, cols), lambda s: (s, 0))
    table = pl.BlockSpec((SEG, LANES), lambda s: (s, 0))
    whole = pl.BlockSpec((seg_total, SEG, LANES), lambda s: (0, 0, 0))
    rows = SEG * (cols // HEAD_SIZE)
    stat = pl.BlockSpec((1, rows, 1), lambda s: (s, 0, 0))
    return block, table, whole, rows, stat, pl.BlockSpec(memory_space=pltpu.SMEM)


def attend(parents, segs, queries, keys_values):
    count, cols = queries.shape
    block, table, whole, rows, stat, scalar = attention_specs(cols, keys_values.shape[0])
    steps = count // SEG
    return pl.pallas_call(
        attend_kernel,
        grid=(steps,),
        in_specs=[scalar, scalar, block, whole],
        out_specs=[block, stat],
        out_shape=[
            jax.ShapeDtypeStruct((count, cols), jnp.float32),
            jax.ShapeDtypeStruct((steps, rows, 1), jnp.float32),
        ],
        scratch_shapes=[pltpu.VMEM((MAX_STEPS + 1, rows, SEG), jnp.float32)],
        compiler_params=pltpu.CompilerParams(vmem_limit_bytes=KERNEL_VMEM),
        cost_estimate=SMALL_COST,
    )(parents, segs, queries, keys_values)


def attend_back(
    parents, segs, queries, grads, attended, stats, cosine, sine, keys_values, earlier=None
):
    count, cols = queries.shape
    seg_total = keys_values.shape[0]
    block, table, whole, rows, stat, scalar = attention_specs(cols, seg_total)
    sums = pl.BlockSpec((seg_total, LANES, SEG), lambda s: (0, 0, 0))
    last = earlier is not None
    sum_type = jnp.bfloat16 if last else jnp.float32
    return pl.pallas_call(
        attend_back_kernel,
        grid=(count // SEG,),
        in_specs=[scalar, scalar, block, block, block, stat, table, table, whole] + [sums] * last,
        out_specs=[block, sums],
        out_shape=[
            jax.ShapeDtypeStruct((count, cols), jnp.bfloat16),
            jax.ShapeDtypeStruct((seg_total, LANES, SEG), sum_type),
        ],
        scratch_shapes=[pltpu.VMEM((seg_total, LANES, SEG), jnp.float32)],
        compiler_params=pltpu.CompilerParams(vmem_limit_bytes=KERNEL_VMEM),
        cost_estimate=SMALL_COST,
    )(
        parents, segs, queries, grads, attended, stats, cosine, sine, keys_values,
        *([earlier] if last else []),
    )


def in_turn(per, count, step):
    for i in range(count):
        pl.when(pl.program_id(1) // per == i)(functools.partial(step, i))


def gate_kernel(per, parts, pieces, rows, *refs):
    gates, ups = refs[: parts * pieces], refs[parts * pieces : 2 * parts * pieces]
    activated, gate_slope, up_slope = refs[2 * parts * pieces :]
    depth = gates[0].shape[0]

    def product(weights, i):
        return sum(
            nn_dot(rows[:, k * depth : (k + 1) * depth], weights[k * pieces + i][...])
            for k in range(parts)
        )

    def step(i):
        gate, up = product(gates, i), product(ups, i)
        sigmoid = 1.0 / (1.0 + jnp.exp(-gate))
        silu = gate * sigmoid
        activated[...] = (silu * up).astype(jnp.bfloat16)
        gate_slope[...] = up * sigmoid * (1.0 + gate * (1.0 - sigmoid))
        up_slope[...] = silu

    in_turn(per, pieces, step)


def gate_back_kernel(per, parts, pieces, *refs):
    grads, weights = refs[:parts], refs[parts : parts + parts * pieces]
    gate_slope, up_slope, grad_gate, grad_up = refs[parts + parts * pieces :]

    def step(i):
        grad = sum(nt_dot(grads[k][...], weights[k * pieces + i][...]) for k in range(parts))
        grad_gate[...] = (grad * gate_slope[...]).astype(jnp.bfloat16)
        grad_up[...] = (grad * up_slope[...]).astype(jnp.bfloat16)

    in_turn(per, pieces, step)


def down_kernel(per, parts, pieces, acts, *refs):
    weights, out = refs[:-1], refs[-1]
    depth = weights[0].shape[0]

    def step(k):
        total = sum(
            nn_dot(acts[:, i * depth : (i + 1) * depth], weights[k * pieces + i][...])
            for i in range(pieces)
        )
        out[...] = total.astype(jnp.bfloat16)

    in_turn(per, parts, step)


def pair_kernel(per, parts, pieces, first, second, *refs):
    gates, ups, out = refs[: parts * pieces], refs[parts * pieces : -1], refs[-1]
    depth = gates[0].shape[1]

    def step(k):
        total = 0.0
        for i in range(pieces):
            columns = slice(i * depth, (i + 1) * depth)
            total = total + nt_dot(first[:, columns], gates[k * pieces + i][...])
            total = total + nt_dot(second[:, columns], ups[k * pieces + i][...])
        out[...] = total.astype(jnp.bfloat16)

    in_turn(per, parts, step)


def wide_call(kernel, whole, weights, tiled, axis, by_piece, outs):
    parts, pieces = len(weights[0]), len(weights[0][0])
    shape = weights[0][0][0].shape
    groups = pieces if by_piece else parts
    tile = (min(whole[0].shape[0], 1024), min(shape[axis], 256))
    per = shape[axis] // tile[1]
    count, cols = whole[0].shape[0], groups * shape[axis]

    def piece_spec(k, i):
        group = i if by_piece else k

        def place(row, col):
            at = jnp.clip(col - group * per, 0, per - 1)
            return (0, at) if axis == 1 else (at, 0)

        return pl.BlockSpec((shape[0], tile[1]) if axis == 1 else (tile[1], shape[1]), place)

    tile_spec = pl.BlockSpec(tile, lambda row, col: (row, col))
    flat = [v for weight in weights for row in weight for v in row]
    return pl.pallas_call(
        functools.partial(kernel, per, parts, pieces),
        grid=(count // tile[0], groups * per),
        in_specs=[pl.BlockSpec((tile[0], v.shape[1]), lambda row, col: (row, 0)) for v in whole]
        + [piece_spec(k, i) for _ in weights for k in range(parts) for i in range(pieces)]
        + [tile_spec] * len(tiled),
        out_specs=[tile_spec] * len(outs),
        out_shape=[jax.ShapeDtypeStruct((count, cols), t) for t in outs],
        compiler_params=pltpu.CompilerParams(vmem_limit_bytes=KERNEL_VMEM),
        cost_estimate=SMALL_COST,
    )(*whole, *flat, *tiled)


def gate_forward(rows, gates, ups):
    outs = (jnp.bfloat16, jnp.float32, jnp.float32)
    return wide_call(gate_kernel, [rows], [gates, ups], [], 1, True, outs)


def gate_backward(grads, downs, gate_slope, up_slope):
    outs = (jnp.bfloat16, jnp.bfloat16)
    return wide_call(gate_back_kernel, grads, [downs], [gate_slope, up_slope], 0, True, outs)


def down_forward(acts, downs):
    return wide_call(down_kernel, [acts], [downs], [], 1, False, (jnp.bfloat16,))[0]


def pair_product(grad_gate, grad_up, gates, ups):
    whole = [grad_gate, grad_up]
    return wide_call(pair_kernel, whole, [gates, ups], [], 0, False, (jnp.bfloat16,))[0]


def row_norm(value):
    inverse = lax.rsqrt(jnp.mean(value * value, axis=-1, keepdims=True) + norm_eps)
    return value * inverse, inverse


def norm_back(grad, normed, inverse, gain):
    scaled = grad * gain
    return inverse * (scaled - normed * jnp.mean(scaled * normed, axis=-1, keepdims=True))


def silu_parts(gate_pre):
    sigmoid = jax.nn.sigmoid(gate_pre)
    return sigmoid, gate_pre * sigmoid


def halves(value, count):
    part = value.shape[1] // count
    return [value[:, i * part : (i + 1) * part] for i in range(count)]


def joined(pieces, outer, inner):
    return jnp.concatenate([jnp.concatenate(row, axis=inner) for row in pieces], axis=outer)


def matmul(left, right):
    return jnp.dot(left, right, preferred_element_type=jnp.float32)


def matmul_turned(left, right):
    return nt_dot(left, right)


def turned_matmul(left, right):
    return lax.dot_general(
        left, right, (((0,), (0,)), ((), ())), preferred_element_type=jnp.float32
    )


def sent_groups(value):
    size = lax.axis_size("y")
    place = lax.axis_index("y")
    width = value.shape[1] // size
    pieces = []
    for k in range(size):
        start = lax.rem(place + k, size) * width
        piece = lax.dynamic_slice_in_dim(value, start, width, 1)
        pieces.append(rotated(piece, "y", k) if k else piece)
    return pieces


def in_groups(pieces):
    size = len(pieces)
    place = lax.axis_index("y")
    return jnp.concatenate(
        [
            lax.select_n(place, *[pieces[(j - i) % size] for i in range(size)])
            for j in range(size)
        ],
        axis=1,
    )


def turned_back(value, cosine_table, sine_table):
    first, second = halves(value, 2)
    return jnp.concatenate(
        [
            first * cosine_table + second * sine_table,
            second * cosine_table - first * sine_table,
        ],
        axis=1,
    )


def tensor_gather(value):
    rows = jnp.stack(natural_pieces(relative_pieces(value, "x"), "x"))
    rows = jnp.stack(natural_pieces(relative_pieces(rows, "c"), "c"), axis=1)
    return rows.reshape(-1, value.shape[1])


def tensor_sum(part, rows):
    x_size, c_size = lax.axis_size("x"), lax.axis_size("c")
    blocks = part.reshape(x_size, c_size, rows, -1)
    c_place, x_place = lax.axis_index("c"), lax.axis_index("x")

    def block(value, place, k, axis):
        size = value.shape[axis]
        return lax.dynamic_index_in_dim(
            value, lax.rem(place - k + size, size), axis, keepdims=False
        )

    mine = summed_pieces([block(blocks, c_place, k, 1) for k in range(c_size)], "c")
    mine = mine.astype(jnp.bfloat16)
    return summed_pieces([block(mine, x_place, k, 0) for k in range(x_size)], "x")


def local(
    tokens,
    norm_gain,
    q_weight,
    key_matrix,
    value_matrix,
    o_weight,
    mlp_gain,
    gate_weight,
    up_weight,
    down_weight,
    parents,
    out_grad,
):
    z_size, y_size, x_size = (lax.axis_size(name) for name in ("z", "y", "x"))
    tensor_size = x_size * lax.axis_size("c")
    low = jnp.bfloat16
    local_rows, width = tokens.shape
    group_rows = local_rows * tensor_size
    kv_cols = key_matrix.shape[1]
    kv_local = kv_cols // HEAD_SIZE
    q_cols = q_weight.shape[1]
    own_width = norm_gain.shape[0]

    own_tokens = relative_columns(tokens)
    own_grad = relative_columns(out_grad).astype(jnp.float32)
    group_tokens = tensor_gather(own_tokens)

    both_gains = jnp.concatenate([norm_gain, mlp_gain])
    both_gains = jnp.pad(both_gains, (0, -both_gains.shape[0] % (2 * kv_cols)))
    key_heads, value_heads = halves(key_matrix, kv_local), halves(value_matrix, kv_local)
    kv_shard = jnp.concatenate(
        [
            jnp.concatenate([v for kv in zip(key_heads, value_heads) for v in kv], axis=1),
            both_gains.reshape(-1, 2 * kv_cols),
        ],
        axis=0,
    )
    kv_z = gathered(kv_shard, "z")
    q_z = lax.all_gather(q_weight, "z", axis=0, tiled=True)
    kv_z, o_weight, group_tokens = together(kv_z, o_weight, group_tokens)

    depth = segment_depth(parents)
    seg_count = group_rows // SEG
    z_place, y_place = lax.axis_index("z"), lax.axis_index("y")
    sources = [lax.rem(y_place - k + y_size, y_size) for k in range(y_size)]
    segs = jnp.concatenate(
        [
            (z_place * y_size + source) * seg_count + jnp.arange(seg_count, dtype=jnp.int32)
            for source in sources
        ]
    )
    seg_ids = jnp.arange(depth.shape[0], dtype=jnp.int32)
    seg_depth = jnp.sum(jnp.where(segs[:, None] == seg_ids[None, :], depth[None, :], 0), axis=1)
    position = (seg_depth[:, None] * SEG + jnp.arange(SEG, dtype=jnp.int32)[None, :]).reshape(-1)
    cosine_table, sine_table = rope_tables(position, HEAD_SIZE)
    cosine_lanes = jnp.tile(cosine_table, (1, 4))
    sine_lanes = jnp.tile(sine_table, (1, 4))
    key_lanes = jnp.arange(LANES) < HEAD_SIZE
    cosine_keys = jnp.where(key_lanes, cosine_lanes[:group_rows], 1.0)
    sine_keys = jnp.where(key_lanes, sine_lanes[:group_rows], 0.0)

    o_z = lax.all_gather(o_weight, "z", axis=0)
    kv_zy = relative_pieces(kv_z, "y")
    kv_weights = [v[:, :own_width].reshape(-1, 2 * kv_cols) for v in kv_zy]
    gains = [
        v[:, own_width:].reshape(z_size, -1)[:, : 2 * own_width].reshape(z_size, 2, own_width)
        for v in kv_zy
    ]
    gains = jnp.stack(gains).astype(jnp.float32)
    gain_one, gain_two = gains[:, :, 0].reshape(-1), gains[:, :, 1].reshape(-1)
    inputs = own_tokens.astype(jnp.float32)
    normed_one, inv_one = row_norm(inputs)
    group_normed, _ = row_norm(group_tokens.astype(jnp.float32))
    rows_one = (group_normed * gain_one).astype(low)
    kv_rows = project(rows_one, kv_weights, cosine_keys, sine_keys)
    kv_swapped = jnp.stack(natural_pieces(sent_groups(kv_rows), "y"))
    q_z, kv_swapped = together(q_z, kv_swapped)

    all_kv = gathered(kv_swapped, "z").reshape(-1, SEG, LANES)
    q_weights = relative_pieces(q_z, "y")
    q_weights, o_z = together(q_weights, o_z)
    o_zy = relative_pieces(joined_columns(o_z), "y")
    query_rows = project(rows_one, q_weights, cosine_lanes[:group_rows], sine_lanes[:group_rows])
    queries = sent_groups(query_rows)
    all_kv, queries, gate_weight, up_weight = together(all_kv, queries, gate_weight, up_weight)

    gate_z = exchanged(column_blocks(gate_weight, z_size), "z")
    seg_lists = jnp.split(segs, y_size)
    attends = [None] * y_size
    for k in range(y_size - 1, 0, -1):
        attends[k] = attend(parents, seg_lists[k], queries[k], all_kv)
    queries[0], attends, o_zy = together(queries[0], attends, o_zy)
    returned = [rotated(attends[k][0].astype(low), "y", -k) for k in range(1, y_size)]
    attends[0] = attend(parents, seg_lists[0], queries[0], all_kv)
    attn_low = in_groups([attends[0][0].astype(low), *returned])
    attn_low, o_zy, gate_z, up_weight = together(attn_low, o_zy, gate_z, up_weight)

    o_full = jnp.concatenate(o_zy, axis=1)
    attn_part = matmul(attn_low, o_full).astype(low)
    attn_mine = tensor_sum(attn_part, local_rows)
    up_z = exchanged(column_blocks(up_weight, z_size), "z")
    gate_zy = relative_pieces(gate_z.reshape(z_size * own_width, -1), "y")
    up_z, gate_zy, attn_mine, down_weight = together(up_z, gate_zy, attn_mine, down_weight)

    middle = inputs + branch_scale * attn_mine
    normed_two, inv_two = row_norm(middle)
    hidden_two = (normed_two * gain_two).astype(low)
    rows_two = lax.all_gather(hidden_two, ("z", "c"), axis=0, tiled=True)
    up_z = up_z.reshape(z_size * own_width, -1)
    up_zy = relative_pieces(up_z, "y")
    gate_zx = relative_pieces(gate_zy[0], "x")
    gate_zx, up_zy, up_z = together(gate_zx, up_zy, up_z)
    up_zx = relative_pieces(up_z, "x")
    gate_far = [relative_pieces(v, "y")[1:] for v in gate_zx[1:]]
    rows_two, up_zx, gate_far, down_weight = together(rows_two, up_zx, gate_far, down_weight)

    down_z = joined_columns(exchanged(down_weight.reshape(z_size, -1, own_width), "z"))
    half = own_width * z_size // 2
    upper = [[rotated(v[:half], "x", i) for i in range(1, x_size)] for v in up_zy[1:]]
    lower = [[rotated(v[half:], "y", k) for v in up_zx[1:]] for k in range(1, y_size)]
    down_z, upper, lower = together(down_z, upper, lower)
    up_far = [
        [jnp.concatenate(pair, axis=0) for pair in zip(*rows)] for rows in zip(upper, lower)
    ]
    gates = [gate_zx] + [
        [gate_zy[k], *[far[k - 1] for far in gate_far]] for k in range(1, y_size)
    ]
    ups = [up_zx] + [[up_zy[k], *up_far[k - 1]] for k in range(1, y_size)]

    grad_mlp = (branch_scale * own_grad).astype(low)
    grad_mlp_rows = lax.all_gather(grad_mlp, ("z", "c"), axis=0, tiled=True)
    down_zy = relative_pieces(down_z, "y")
    down_zx = relative_pieces(down_z, "x")
    activated, gate_slope, up_slope = gate_forward(rows_two, gates, ups)
    down_zy, down_zx, activated, gate_slope, up_slope = together(
        down_zy, down_zx, activated, gate_slope, up_slope
    )
    half = down_z.shape[0] // 2
    upper = [[rotated(v[:half], "x", i) for i in range(1, x_size)] for v in down_zy[1:]]
    lower = [[rotated(v[half:], "y", k) for v in down_zx[1:]] for k in range(1, y_size)]
    upper, lower, grad_mlp_rows = together(upper, lower, grad_mlp_rows)
    down_far = [
        [jnp.concatenate(pair, axis=0) for pair in zip(*rows)] for rows in zip(upper, lower)
    ]
    downs = [down_zx] + [[down_zy[k], *down_far[k - 1]] for k in range(1, y_size)]
    grad_mlp_parts = halves(grad_mlp_rows, y_size)
    mlp_part = down_forward(activated, downs)
    mlp_mine = lax.psum_scatter(mlp_part, ("z", "c"), scatter_dimension=0, tiled=True)
    acts = halves(activated, x_size)
    down_far = [
        summed_pieces([turned_matmul(act, grad) for grad in grad_mlp_parts], "y").astype(low)
        for act in acts[1:]
    ]
    grad_gate_act, grad_up_act = gate_backward(grad_mlp_parts, downs, gate_slope, up_slope)
    grad_gate_act, grad_up_act, down_far = together(grad_gate_act, grad_up_act, down_far)

    down_near = summed_pieces([turned_matmul(acts[0], grad) for grad in grad_mlp_parts], "y")
    grad_down_z = summed_pieces([down_near, *down_far], "x").astype(low)
    input_part = pair_product(grad_gate_act, grad_up_act, gates, ups)
    input_part, grad_down_z, rows_two = together(input_part, grad_down_z, rows_two)

    grad_rows_two = lax.psum_scatter(input_part, ("z", "c"), scatter_dimension=0, tiled=True)
    rows_parts = halves(rows_two, y_size)
    gate_parts, up_parts = halves(grad_gate_act, x_size), halves(grad_up_act, x_size)
    gate_far = [
        summed_pieces([turned_matmul(a, b) for a in rows_parts], "y").astype(low)
        for b in gate_parts[1:]
    ]
    up_far = [
        summed_pieces([turned_matmul(a, b) for b in up_parts], "x").astype(low)
        for a in rows_parts[1:]
    ]
    gate_far, up_far = together(gate_far, up_far)
    gate_near = summed_pieces([turned_matmul(a, gate_parts[0]) for a in rows_parts], "y")
    grad_gate_z = summed_pieces([gate_near, *gate_far], "x").astype(low)
    grad_rows_two, grad_gate_z, up_far, mlp_mine = together(
        grad_rows_two, grad_gate_z, up_far, mlp_mine
    )

    mixed = natural_columns((middle + branch_scale * mlp_mine.astype(jnp.float32)).astype(low))
    grad_rows_two = grad_rows_two.astype(jnp.float32)
    gain_two_part = jnp.sum(grad_rows_two * normed_two, axis=0)
    grad_middle = own_grad + norm_back(grad_rows_two, normed_two, inv_two, gain_two)
    grad_attn = (branch_scale * grad_middle).astype(low)
    grad_gate = exchanged(grad_gate_z.reshape(z_size, own_width, -1), "z")
    up_far = [rotated(v, "y", -1 - i) for i, v in enumerate(up_far)]
    grad_attn_rows = tensor_gather(grad_attn)
    grad_attn_rows, up_far, grad_down_z = together(grad_attn_rows, up_far, grad_down_z)

    grad_heads = sent_groups(matmul_turned(grad_attn_rows, o_full).astype(low))
    up_near = summed_pieces([turned_matmul(rows_parts[0], b) for b in up_parts], "x")
    grad_up_z = sum([v.astype(jnp.float32) for v in up_far], up_near).astype(low)
    grad_heads, grad_gate, grad_down_z, grad_attn_rows = together(
        grad_heads, grad_gate, grad_down_z, grad_attn_rows
    )
    grad_down = exchanged(column_blocks(grad_down_z, z_size), "z")
    grad_o_y = summed_pieces(
        [turned_matmul(attn_low, v) for v in halves(grad_attn_rows, y_size)], "y"
    ).astype(low)
    cosines, sines = jnp.split(cosine_lanes, y_size), jnp.split(sine_lanes, y_size)
    grad_queries, sums = [None] * y_size, None
    for k in range(y_size - 1, 0, -1):
        grad_queries[k], sums = attend_back(
            parents, seg_lists[k], queries[k], grad_heads[k], *attends[k], cosines[k], sines[k],
            all_kv, sums,
        )
    grad_queries[1:], sums, grad_o_y, grad_up_z = together(
        grad_queries[1:], sums, grad_o_y, grad_up_z
    )
    grad_o = lax.psum_scatter(
        column_blocks(grad_o_y, z_size), "z", scatter_dimension=0, tiled=True
    )[0]
    returned = [rotated(v, "y", -k) for k, v in enumerate(grad_queries[1:], 1)]
    grad_queries[0], grad_kv = attend_back(
        parents, seg_lists[0], queries[0], grad_heads[0], *attends[0], cosines[0], sines[0],
        all_kv, sums,
    )
    grad_queries = in_groups([grad_queries[0], *returned])
    grad_queries, grad_kv, grad_down, grad_up_z = together(
        grad_queries, grad_kv, grad_down, grad_up_z
    )

    def owned_rows(left, right):
        return summed_pieces([turned_matmul(v, right) for v in halves(left, y_size)], "y").astype(
            low
        )

    kv_mine = summed_blocks(grad_kv.reshape(z_size, y_size * seg_count, LANES, SEG), "z")
    grad_q_y = owned_rows(rows_one, grad_queries)
    q_full = jnp.concatenate(q_weights, axis=0)
    query_part = matmul_turned(grad_queries, q_full)
    kv_mine, query_part, grad_q_y, grad_up_z = together(kv_mine, query_part, grad_q_y, grad_up_z)

    grad_q = lax.psum_scatter(
        grad_q_y.reshape(z_size, own_width, -1), "z", scatter_dimension=0, tiled=True
    )[0]
    grad_up = exchanged(grad_up_z.reshape(z_size, own_width, -1), "z")
    kv_mine = kv_mine.transpose(0, 2, 1).reshape(y_size, group_rows, LANES)
    kv_mine = [lax.dynamic_index_in_dim(kv_mine, s, 0, keepdims=False) for s in sources]
    kv_mine = jnp.concatenate(kv_mine, axis=0)
    grad_keys = turned_back(kv_mine[:, :HEAD_SIZE], cosine_table, sine_table)
    grad_kv_rows = jnp.concatenate([grad_keys, kv_mine[:, HEAD_SIZE:]], axis=1).astype(low)
    grad_kv_rows = in_groups(
        [grad_kv_rows[:group_rows]]
        + [
            rotated(grad_kv_rows[k * group_rows : (k + 1) * group_rows], "y", -k)
            for k in range(1, y_size)
        ]
    )
    kv_full = jnp.concatenate(kv_weights, axis=0)
    input_one = (query_part + matmul_turned(grad_kv_rows, kv_full)).astype(low)
    grad_kv_y = owned_rows(rows_one, grad_kv_rows)
    grad_rows_one = tensor_sum(input_one, local_rows)
    grad_kv_y, grad_rows_one = together(grad_kv_y, grad_rows_one)
    grad_kv_weight = summed_blocks(grad_kv_y.reshape(z_size, own_width, -1), "z")
    grad_q, grad_o = grad_q.astype(jnp.float32), grad_o.astype(jnp.float32)
    gain_one_part = jnp.sum(grad_rows_one * normed_one, axis=0)
    grad_inputs = grad_middle + norm_back(grad_rows_one, normed_one, inv_one, gain_one)
    grad_tokens = natural_columns(grad_inputs.astype(low))
    grad_gate, grad_up = (joined_columns(v).astype(jnp.float32) for v in (grad_gate, grad_up))
    grad_down = grad_down.reshape(-1, own_width).astype(jnp.float32)

    gain_parts = jnp.stack([gain_one_part, gain_two_part], axis=0)
    gain_parts = natural_columns(gain_parts).reshape(2, z_size * y_size, 1, own_width)
    gain_parts = jnp.broadcast_to(
        gain_parts, (2, z_size * y_size, tensor_size, own_width)
    ).reshape(2, -1, own_width).transpose(1, 0, 2)
    gain_sums = jnp.sum(exchanged(gain_parts, ("z", "y", "x", "c")), axis=0)
    grad_heads = halves(grad_kv_weight, 2 * kv_local)
    return (
        mixed,
        grad_tokens,
        gain_sums[0],
        grad_q,
        jnp.concatenate(grad_heads[::2], axis=1),
        jnp.concatenate(grad_heads[1::2], axis=1),
        grad_o,
        gain_sums[1],
        grad_gate,
        grad_up,
        grad_down,
    )


def solution(mesh):
    dp_size, tensor_size = mesh.shape["dp"], mesh.shape["tensor"]
    fine = jax.sharding.Mesh(
        mesh.devices.reshape(dp_size // 2, 2, tensor_size // 2, 2), ("z", "y", "x", "c")
    )
    dp, tensor = ("z", "y"), ("x", "c")
    tokens = P(dp + tensor, None)
    rows = P(dp, tensor)
    columns = P(tensor, dp)
    in_specs = (
        tokens,
        P(dp),
        rows,
        rows,
        rows,
        columns,
        P(dp),
        rows,
        rows,
        columns,
        P(),
        tokens,
    )
    out_specs = (
        tokens,
        tokens,
        P(dp),
        rows,
        rows,
        rows,
        columns,
        P(dp),
        rows,
        rows,
        columns,
    )
    return jax.shard_map(local, mesh=fine, in_specs=in_specs, out_specs=out_specs, check_vma=False)
```

time: 895 us -> 752 us (0.84)
  waiting for transfers between devices: 411 us -> 319 us
  Pallas kernels: 38.9 us -> 111 us
  matrix products: 121 us -> 53.3 us
  blocking collectives: 66.6 us -> 0 us
  local copies, waits for them, and re-layouts: 46.3 us -> 68.3 us
  starting transfers between devices: 135 us -> 117 us
    pallas_call x2 -> x10, Pallas kernels: 38.9 us -> 111 us  [the longest x4 52.2 us: wide_call(): pl.pallas_call(functools.partial(kernel, per, parts, pieces), grid=(count...]
    all_to_all x2 -> x0, blocking collectives: 66.6 us -> none  [the longest x1 38.2 us: exchanged(): return lax.all_to_all(blocks, axis, 0, 0, tiled=True)]
    ppermute x27 -> x40, waiting for transfers between devices: 253 us -> 194 us  [rotated(): lax.ppermute(value, axis, [(i, (i + step) % size) for i in range(size)])]
    all_to_all x10 -> x9, waiting for transfers between devices: 125 us -> 84.8 us  [exchanged(): return lax.all_to_all(blocks, axis, 0, 0, tiled=True)]
    dot_general x6 -> x1, matrix products: 39.8 us -> 1.34 us  [matmul(): return jnp.dot(left, right, preferred_element_type=jnp.float32)]
    all_gather x2, waiting for transfers between devices: 0.02 us -> 36.2 us  [the longest x1 36.2 us: local(): o_z = lax.all_gather(o_weight, 'z', axis=0)]
    dot_general x6 -> x3, matrix products: 41.1 us -> 8.18 us  [nt_dot(): lax.dot_general(left, right, (((1,), (1,)), ((), ())), preferred_element_...]
    all_to_all x3 -> x2, waiting for transfers between devices: 32.7 us -> 3.45 us  [gathered(): return lax.all_to_all(copies, axis, 0, 0, tiled=True)]
  transfers between devices with their start and end apart: 46 -> 59, of which waited for: 25 -> 33; matrix products, arithmetic and copies ran while one was open for 19% -> 20% of each run, Pallas kernels for 4% -> 14%
where the time goes in v3:
time: 752 us; the launch traced here: 741 us
  waiting for transfers between devices  319 us (42%)
  starting transfers between devices  117 us (16%)
  Pallas kernels  111 us (15%)
  local copies, waits for them, and re-layouts  68.3 us (9%)
  other arithmetic  56.2 us (7%)
  matrix products  53.3 us (7%)
  between operations  16 us (2%)
    ppermute x40, waiting for transfers between devices, rotated(): lax.ppermute(value, axis, [(i, (i + step) % size) for i in range(size)])  194 us
    all_to_all x9, waiting for transfers between devices, exchanged(): return lax.all_to_all(blocks, axis, 0, 0, tiled=True)  84.8 us
    ppermute x40, starting transfers between devices, rotated(): lax.ppermute(value, axis, [(i, (i + step) % size) for i in range(size)])  58.3 us
    pallas_call x4, Pallas kernels, wide_call(): pl.pallas_call(functools.partial(kernel, per, parts, pieces), grid=(count...  52.2 us
    all_to_all x9, starting transfers between devices, exchanged(): return lax.all_to_all(blocks, axis, 0, 0, tiled=True)  49.4 us
    dot_general x18, matrix products, turned_matmul(): lax.dot_general(left, right, (((0,), (0,)), ((), ())), preferred_element_...  43.2 us
    all_gather x1, waiting for transfers between devices, local(): o_z = lax.all_gather(o_weight, 'z', axis=0)  36.2 us
    pallas_call x2, Pallas kernels, attend_back(): pl.pallas_call(attend_back_kernel, grid=(count // SEG,), in_specs=[scalar...  27.6 us
  transfers between devices with their start and end apart: 59, of which 33 were waited for; matrix products, arithmetic and copies ran while one was open for 20% of the time, Pallas kernels for 14%

profile of v3, /device:TPU:0, one launch (start us, length us, event | category | flops | bytes accessed | tf_op | source)
XLA Modules:
  0.0 741.0 jit_solution(16974609075292856097)
XLA Ops:
  38.1 8.7 %collective-permute-done.2 = bf16[4,258,256]{2,0,1:T(4,128)(2,1)S(1)} collective-permute-done((bf16[4,258,256]{2,0,1:T(4,128)(2,1)S(1)}, bf16[4,258,256]{2,0,1:T(4,128)(2,1)S(1)}, u32[]{:S(2)}, u32[]{:S(2)}) %collective-permute-start.2) | collective-permute-done | bytes 528416 | tf_op jit(solution)/shard_map/ppermute | solution.py:45
  66.5 36.2 %all-gather.12.cloned.1.call-done = bf16[2048,256]{1,0:T(8,128)(2,1)} async-done(((bf16[512,256]{1,0:T(8,128)(2,1)}), bf16[2048,256]{1,0:T(8,128)(2,1)}) %all-gather.12.cloned.1.call-update) | async-done | bytes 1048592 | tf_op jit(solution)/shard_map/all_gather | solution.py:642
  123.6 10.6 %shard_map.205 = (f32[512,256]{1,0:T(8,128)}, f32[2,1024,1]{2,1,0:T(8,128)}) custom-call(s32[16]{0:T(128)} %parents.7, s32[2]{0:T(128)} %copy-done.74, bf16[512,256]{1,0:T(8,128)(2,1)} %copy-done.47, bf16[16,256,128]{2,1,0:T(8,128)(2,1)} %bitcast.211), custom_call_target="tpu_custom_call" | custom-call | flops 268435456 | bytes 262144 | tf_op jit(solution)/shard_map/pallas_call | solution.py:324
  142.6 12.0 %shard_map.206 = (f32[512,256]{1,0:T(8,128)}, f32[2,1024,1]{2,1,0:T(8,128)}) custom-call(s32[16]{0:T(128)} %parents.7, s32[2]{0:T(128)} %copy-done.73, bf16[512,256]{1,0:T(8,128)(2,1)} %get-tuple-element.120.queries, bf16[16,256,128]{2,1,0:T(8,128)(2,1)} %bitcast.212), custom_call_target="tpu_custom_call" | custom-call | flops 268435456 | bytes 262144 | tf_op jit(solution)/shard_map/pallas_call | solution.py:324
  179.0 12.6 %collective-permute-done.10 = bf16[128,2048]{1,0:T(8,128)(2,1)S(1)} collective-permute-done((bf16[128,2048]{1,0:T(8,128)(2,1)}, bf16[128,2048]{1,0:T(8,128)(2,1)S(1)}, u32[]{:S(2)}, u32[]{:S(2)}) %collective-permute-start.10) | collective-permute-done | bytes 524320 | tf_op jit(solution)/shard_map/ppermute | solution.py:45
  208.2 20.7 %collective-permute-done.11.refs_1_ = bf16[1024,512]{1,0:T(8,128)(2,1)S(1)} collective-permute-done((bf16[1024,512]{1,0:T(8,128)(2,1)S(1)}, bf16[1024,512]{1,0:T(8,128)(2,1)S(1)}, u32[]{:S(2)}, u32[]{:S(2)}) %collective-permute-start.11) | collective-permute-done | bytes 1048608 | tf_op jit(solution)/shard_map/ppermute | solution.py:45
  233.1 21.3 %collective-permute-done.13.refs_5_ = bf16[1024,512]{1,0:T(8,128)(2,1)S(1)} collective-permute-done((bf16[1024,512]{1,0:T(8,128)(2,1)S(1)}, bf16[1024,512]{1,0:T(8,128)(2,1)S(1)}, u32[]{:S(2)}, u32[]{:S(2)}) %collective-permute-start.13) | collective-permute-done | bytes 1048608 | tf_op jit(solution)/shard_map/ppermute | solution.py:45
  264.0 45.5 %all-to-all-done.4 = bf16[4,512,256]{2,1,0:T(8,128)(2,1)} async-done(((bf16[4,512,256]{2,1,0:T(8,128)(2,1)}), bf16[4,512,256]{2,1,0:T(8,128)(2,1)}, u32[]{:S(2)}, u32[]{:S(2)}) %all-to-all-start.4) | async-done | bytes 1048608 | tf_op jit(solution)/shard_map/all_to_all | solution.py:67
  318.3 15.6 %shard_map.207 = (bf16[1024,1024]{1,0:T(8,128)(2,1)}, f32[1024,1024]{1,0:T(8,128)}, f32[1024,1024]{1,0:T(8,128)}) custom-call(bf16[1024,2048]{1,0:T(8,128)(2,1)} %all-gather.8.cloned.1.call-done.rows, bf16[1024,512]{1,0:T(8,128)(2,1)} %bitcast.218, bf16[1024,512]{1,0:T(8,128)(2,1)} %copy-done.23, bf16[1024,512]{1,0:T(8,128)(2,1)} %collective-permute-done.8.refs_2_, ...), custom_call_target="tpu_custom_call" | custom-call | flops 268435456 | bytes 262144 | tf_op jit(solution)/shard_map/pallas_call | solution.py:453
  350.8 10.4 %shard_map.210 = bf16[1024,2048]{1,0:T(8,128)(2,1)} custom-call(bf16[1024,1024]{1,0:T(8,128)(2,1)} %get-tuple-element.162.acts, bf16[512,1024]{1,0:T(8,128)(2,1)} %bitcast.227, bf16[512,1024]{1,0:T(8,128)(2,1)} %copy-done.16, bf16[512,1024]{1,0:T(8,128)(2,1)} %copy-done.15, bf16[512,1024]{1,0:T(8,128)(2,1)} %copy-done.18), custom_call_target="tpu_custom_call" | custom-call | flops 268435456 | bytes 262144 | tf_op jit(solution)/shard_map/pallas_call | solution.py:453
  373.9 11.1 %shard_map.208 = (bf16[1024,1024]{1,0:T(8,128)(2,1)}, bf16[1024,1024]{1,0:T(8,128)(2,1)}) custom-call(bf16[1024,1024]{1,0:T(8,128)(2,1)} %get-tuple-element.210.refs_0_, bf16[1024,1024]{1,0:T(8,128)(2,1)} %get-tuple-element.209.refs_1_, bf16[512,1024]{1,0:T(8,128)(2,1)} %bitcast.228, bf16[512,1024]{1,0:T(8,128)(2,1)} %copy-done.16, ...), custom_call_target="tpu_custom_call" | custom-call | flops 268435456 | bytes 262144 | tf_op jit(solution)/shard_map/pallas_call | solution.py:453
  385.0 8.5 %collective-permute-done.21 = bf16[512,1024]{1,0:T(8,128)(2,1)} collective-permute-done((bf16[512,1024]{1,0:T(8,128)(2,1)}, bf16[512,1024]{1,0:T(8,128)(2,1)}, u32[]{:S(2)}, u32[]{:S(2)}) %collective-permute-start.21) | collective-permute-done | bytes 1048608 | tf_op jit(solution)/shard_map/ppermute | solution.py:45
  400.2 15.1 %shard_map.209 = bf16[1024,2048]{1,0:T(8,128)(2,1)} custom-call(bf16[1024,1024]{1,0:T(8,128)(2,1)} %get-tuple-element.163.first, bf16[1024,1024]{1,0:T(8,128)(2,1)} %get-tuple-element.164.second, bf16[1024,512]{1,0:T(8,128)(2,1)} %bitcast.219, bf16[1024,512]{1,0:T(8,128)(2,1)} %copy-done.23, bf16[1024,512]{1,0:T(8,128)(2,1)} %collective-permute-done.8.refs_2_, ...), custom_call_target="tpu_custom_call" | custom-call | flops 268435456 | bytes 262144 | tf_op jit(solution)/shard_map/pallas_call | solution.py:453
  429.2 18.0 %collective-permute-done.26 = bf16[1024,512]{1,0:T(8,128)(2,1)S(1)} collective-permute-done((bf16[1024,512]{1,0:T(8,128)(2,1)S(1)}, bf16[1024,512]{1,0:T(8,128)(2,1)S(1)}, u32[]{:S(2)}, u32[]{:S(2)}) %collective-permute-start.26) | collective-permute-done | bytes 1048608 | tf_op jit(solution)/shard_map/ppermute | solution.py:45
  455.1 10.6 %collective-permute-done.27 = bf16[1024,512]{1,0:T(8,128)(2,1)S(1)} collective-permute-done((bf16[1024,512]{1,0:T(8,128)(2,1)S(1)}, bf16[1024,512]{1,0:T(8,128)(2,1)S(1)}, u32[]{:S(2)}, u32[]{:S(2)}) %collective-permute-start.27) | collective-permute-done | bytes 1048608 | tf_op jit(solution)/shard_map/ppermute | solution.py:45
  471.9 9.0 %collective-permute-done.28 = bf16[128,2048]{1,0:T(8,128)(2,1)S(1)} collective-permute-done((bf16[128,2048]{1,0:T(8,128)(2,1)S(1)}, bf16[128,2048]{1,0:T(8,128)(2,1)S(1)}, u32[]{:S(2)}, u32[]{:S(2)}) %collective-permute-start.28) | collective-permute-done | bytes 524320 | tf_op jit(solution)/shard_map/ppermute | solution.py:45
  489.5 18.4 %collective-permute-done.30 = bf16[1024,512]{1,0:T(8,128)(2,1)} collective-permute-done((bf16[1024,512]{1,0:T(8,128)(2,1)}, bf16[1024,512]{1,0:T(8,128)(2,1)}, u32[]{:S(2)}, u32[]{:S(2)}) %collective-permute-start.30) | collective-permute-done | bytes 1048608 | tf_op jit(solution)/shard_map/ppermute | solution.py:45
  541.5 12.9 %shard_map.211 = (bf16[512,256]{1,0:T(8,128)(2,1)}, f32[16,128,256]{2,1,0:T(8,128)}) custom-call(s32[16]{0:T(128)} %parents.7, s32[2]{0:T(128)} %copy-done.74, bf16[512,256]{1,0:T(8,128)(2,1)} %copy-done.47, bf16[512,256]{1,0:T(8,128)(2,1)} %copy-done.60, f32[512,256]{1,0:T(8,128)} %get-tuple-element.122.attended, f32[2,1024,1]{2,1,0:T(8,128)} %get-tuple-element.180.stats, ...), custom_call_target="tpu_custom_call" | custom-call | flops 268435456 | bytes 262144 | tf_op jit(solution)/shard_map/pallas_call | solution.py:348
  560.2 14.7 %shard_map.212 = (bf16[512,256]{1,0:T(8,128)(2,1)}, bf16[16,128,256]{2,1,0:T(8,128)(2,1)}) custom-call(s32[16]{0:T(128)} %parents.7, s32[2]{0:T(128)} %copy-done.73, bf16[512,256]{1,0:T(8,128)(2,1)} %get-tuple-element.120.queries, bf16[512,256]{1,0:T(8,128)(2,1)} %get-tuple-element.177.grads, f32[512,256]{1,0:T(8,128)} %get-tuple-element.121.attended, ...), custom_call_target="tpu_custom_call" | custom-call | flops 268435456 | bytes 262144 | tf_op jit(solution)/shard_map/pallas_call | solution.py:348
  576.9 12.9 %all-to-all-start.7 = ((bf16[4,4,128,256]{3,2,1,0:T(8,128)(2,1)}), bf16[4,4,128,256]{3,2,1,0:T(8,128)(2,1)}, u32[]{:S(2)}, u32[]{:S(2)}) async-start(bf16[4,4,128,256]{3,2,1,0:T(8,128)(2,1)} %bitcast.265), calls=%async_computation.9 | async-start | bytes 2097152 | tf_op jit(solution)/shard_map/all_to_all | solution.py:67
  603.1 14.2 %collective-permute-done.35 = bf16[1024,512]{1,0:T(8,128)(2,1)} collective-permute-done((bf16[1024,512]{1,0:T(8,128)(2,1)}, bf16[1024,512]{1,0:T(8,128)(2,1)}, u32[]{:S(2)}, u32[]{:S(2)}) %collective-permute-start.35) | collective-permute-done | bytes 1048608 | tf_op jit(solution)/shard_map/ppermute | solution.py:45
  620.3 8.2 %all-to-all-done.7 = bf16[4,4,128,256]{3,2,1,0:T(8,128)(2,1)} async-done(((bf16[4,4,128,256]{3,2,1,0:T(8,128)(2,1)}), bf16[4,4,128,256]{3,2,1,0:T(8,128)(2,1)}, u32[]{:S(2)}, u32[]{:S(2)}) %all-to-all-start.7) | async-done | bytes 1048608 | tf_op jit(solution)/shard_map/all_to_all | solution.py:67
  675.4 21.2 %all-to-all-done.10 = bf16[4,256,512]{2,1,0:T(8,128)(2,1)} async-done(((bf16[4,256,512]{2,1,0:T(8,128)(2,1)}), bf16[4,256,512]{2,1,0:T(8,128)(2,1)}, u32[]{:S(2)}, u32[]{:S(2)}) %all-to-all-start.10) | async-done | bytes 1048608 | tf_op jit(solution)/shard_map/all_to_all | solution.py:67
  722.8 9.9 %all-to-all-done.9 = bf16[4,256,256]{2,1,0:T(8,128)(2,1)S(1)} async-done(((bf16[4,256,256]{2,1,0:T(8,128)(2,1)}), bf16[4,256,256]{2,1,0:T(8,128)(2,1)S(1)}, u32[]{:S(2)}, u32[]{:S(2)}) %all-to-all-start.9) | async-done | bytes 524320 | tf_op jit(solution)/shard_map/all_to_all | solution.py:67
  (443 shorter events, 346.8 us)
Async XLA Ops:
  18.9 41.4 %all-gather.6.cloned.1.call-start = ((), (), s32[]{:S(2)}) async-start(), calls=%async_computation.15 | async-start | bytes 1310720 | tf_op jit(solution)/shard_map/all_gather | solution.py:619
  19.6 83.1 %all-gather.12.cloned.1.call-start = ((), (), s32[]{:S(2)}) async-start(), calls=%async_computation.22 | async-start | bytes 1310720 | tf_op jit(solution)/shard_map/all_gather | solution.py:642
  61.4 57.0 %all-to-all-start.1 = ((bf16[4,2,512,128]{3,2,1,0:T(8,128)(2,1)}), bf16[4,2,512,128]{3,2,1,0:T(8,128)(2,1)S(1)}, u32[]{:S(2)}, u32[]{:S(2)}) async-start(bf16[4,2,512,128]{3,2,1,0:T(8,128)(2,1)} %broadcast_in_dim.67), calls=%async_computation.1 | async-start | bytes 2097152 | tf_op jit(solution)/shard_map/all_to_all | solution.py:63
  65.0 37.8 %collective-permute-start.4 = (bf16[1024,512]{1,0:T(8,128)(2,1)S(1)}, bf16[1024,512]{1,0:T(8,128)(2,1)}, u32[]{:S(2)}, u32[]{:S(2)}) collective-permute-start(bf16[1024,512]{1,0:T(8,128)(2,1)S(1)} %copy-done.32), channel_id=1, source_target_pairs={{0,4},{4,0},{1,5},{5,1},{2,6},{6,2},{3,7},{7,3},{8,12},{12,8},{9,1... | collective-permute-start | bytes 3145736 | tf_op jit(solution)/shard_map/ppermute | solution.py:45
  113.0 27.1 %collective-permute-start.6 = (bf16[512,1024]{0,1:T(8,128)(2,1)}, bf16[512,1024]{0,1:T(8,128)(2,1)}, u32[]{:S(2)}, u32[]{:S(2)}) collective-permute-start(bf16[512,1024]{0,1:T(8,128)(2,1)} %bitcast.19), channel_id=1, source_target_pairs={{0,4},{4,0},{1,5},{5,1},{2,6},{6,2},{3,7},{7,3},{8,12},{12,8},{9,1... | collective-permute-start | bytes 3145736 | tf_op jit(solution)/shard_map/ppermute | solution.py:45
  119.8 36.0 %all-to-all-start.2 = ((bf16[4,256,512]{2,1,0:T(8,128)(2,1)}), bf16[4,256,512]{2,1,0:T(8,128)(2,1)S(1)}, u32[]{:S(2)}, u32[]{:S(2)}) async-start(bf16[4,256,512]{2,1,0:T(8,128)(2,1)} %bitcast.246), calls=%async_computation.2 | async-start | bytes 2097152 | tf_op jit(solution)/shard_map/all_to_all | solution.py:67
  163.8 33.7 %all-to-all-start.3 = ((bf16[4,256,512]{2,1,0:T(8,128)(2,1)}), bf16[4,256,512]{2,1,0:T(8,128)(2,1)S(1)}, u32[]{:S(2)}, u32[]{:S(2)}) async-start(bf16[4,256,512]{2,1,0:T(8,128)(2,1)} %bitcast.245), calls=%async_computation.3 | async-start | bytes 2097152 | tf_op jit(solution)/shard_map/all_to_all | solution.py:67
  170.9 83.9 %all-gather.8.cloned.1.call-start = ((), (), s32[]{:S(2)}) async-start(), calls=%async_computation.16 | async-start | bytes 4718592 | tf_op jit(solution)/shard_map/all_gather | solution.py:688
  200.9 138.1 %all-gather.10.cloned.1.call-start = ((), (), s32[]{:S(2)}) async-start(), calls=%async_computation.17 | async-start | bytes 4718592 | tf_op jit(solution)/shard_map/all_gather | solution.py:711
  254.8 54.8 %all-to-all-start.4 = ((bf16[4,512,256]{2,1,0:T(8,128)(2,1)}), bf16[4,512,256]{2,1,0:T(8,128)(2,1)}, u32[]{:S(2)}, u32[]{:S(2)}) async-start(bf16[4,512,256]{2,1,0:T(8,128)(2,1)} %bitcast.262), calls=%async_computation.4 | async-start | bytes 2097152 | tf_op jit(solution)/shard_map/all_to_all | solution.py:67
  259.2 207.9 %reduce-scatter.7.cloned.1.call-start = ((), (), s32[]{:S(2)}) async-start(), calls=%async_computation.19 | async-start | bytes 4718592 | tf_op jit(solution)/shard_map/reduce_scatter | solution.py:728
  260.4 50.6 %collective-permute-start.15 = (bf16[512,512]{1,0:T(8,128)(2,1)}, bf16[512,512]{1,0:T(8,128)(2,1)S(1)}, u32[]{:S(2)}, u32[]{:S(2)}) collective-permute-start(bf16[512,512]{1,0:T(8,128)(2,1)} %slice.193), channel_id=1, source_target_pairs={{0,2},{2,0},{1,3},{3,1},{4,6},{6,4},{5,7},{7,5},{8,10},{10,8},{9,1... | collective-permute-start | bytes 1572872 | tf_op jit(solution)/shard_map/ppermute | solution.py:45
  262.6 48.4 %collective-permute-start.16 = (bf16[512,512]{1,0:T(8,128)(2,1)}, bf16[512,512]{1,0:T(8,128)(2,1)S(1)}, u32[]{:S(2)}, u32[]{:S(2)}) collective-permute-start(bf16[512,512]{1,0:T(8,128)(2,1)} %slice.194), channel_id=1, source_target_pairs={{0,4},{4,0},{1,5},{5,1},{2,6},{6,2},{3,7},{7,3},{8,12},{12,8},{9,1... | collective-permute-start | bytes 1572872 | tf_op jit(solution)/shard_map/ppermute | solution.py:45
  361.2 105.9 %reduce-scatter.5.cloned.1.call-start = ((), (), s32[]{:S(2)}) async-start(), calls=%async_computation.18 | async-start | bytes 4718592 | tf_op jit(solution)/shard_map/reduce_scatter | solution.py:742
  369.9 45.4 %collective-permute-start.22 = (bf16[512,1024]{1,0:T(8,128)(2,1)}, bf16[512,1024]{1,0:T(8,128)(2,1)}, u32[]{:S(2)}, u32[]{:S(2)}) collective-permute-start(bf16[512,1024]{1,0:T(8,128)(2,1)} %convolution_convert_fusion.5), channel_id=1, source_target_pairs={{0,4},{4,0},{1,5},{5,1},{2,6},{6,2},{3,7},{7,3},{8,12},{12,8},{9,1... | collective-permute-start | bytes 3145736 | tf_op jit(solution)/shard_map/ppermute | solution.py:45
  427.7 27.3 %collective-permute-start.24 = (bf16[1024,512]{1,0:T(8,128)(2,1)S(1)}, bf16[1024,512]{1,0:T(8,128)(2,1)S(1)}, u32[]{:S(2)}, u32[]{:S(2)}) collective-permute-start(bf16[1024,512]{1,0:T(8,128)(2,1)S(1)} %convolution_convert_fusion.4), channel_id=1, source_target_pairs={{0,4},{4,0},{1,5},{5,1},{2,6},{6,2},{3,7},{7,3},{8,12},{12,8},{9,1... | collective-permute-start | bytes 3145736 | tf_op jit(solution)/shard_map/ppermute | solution.py:45
  483.5 31.6 %all-to-all-start.5 = ((bf16[4,256,512]{2,1,0:T(8,128)(2,1)}), bf16[4,256,512]{2,1,0:T(8,128)(2,1)S(1)}, u32[]{:S(2)}, u32[]{:S(2)}) async-start(bf16[4,256,512]{2,1,0:T(8,128)(2,1)} %bitcast.237), calls=%async_computation.7 | async-start | bytes 2097152 | tf_op jit(solution)/shard_map/all_to_all | solution.py:67
  521.8 32.7 %collective-permute-start.32 = (bf16[512,1024]{1,0:T(8,128)(2,1)}, bf16[512,1024]{1,0:T(8,128)(2,1)}, u32[]{:S(2)}, u32[]{:S(2)}) collective-permute-start(bf16[512,1024]{1,0:T(8,128)(2,1)} %convolution_convert_fusion.8), channel_id=1, source_target_pairs={{0,4},{4,0},{1,5},{5,1},{2,6},{6,2},{3,7},{7,3},{8,12},{12,8},{9,1... | collective-permute-start | bytes 3145736 | tf_op jit(solution)/shard_map/ppermute | solution.py:45
  527.6 49.3 %all-to-all-start.6 = ((bf16[4,512,256]{2,1,0:T(8,128)(2,1)}), bf16[4,512,256]{2,1,0:T(8,128)(2,1)}, u32[]{:S(2)}, u32[]{:S(2)}) async-start(bf16[4,512,256]{2,1,0:T(8,128)(2,1)} %bitcast.205), calls=%async_computation.8 | async-start | bytes 2097152 | tf_op jit(solution)/shard_map/all_to_all | solution.py:67
  576.9 51.5 %all-to-all-start.7 = ((bf16[4,4,128,256]{3,2,1,0:T(8,128)(2,1)}), bf16[4,4,128,256]{3,2,1,0:T(8,128)(2,1)}, u32[]{:S(2)}, u32[]{:S(2)}) async-start(bf16[4,4,128,256]{3,2,1,0:T(8,128)(2,1)} %bitcast.265), calls=%async_computation.9 | async-start | bytes 2097152 | tf_op jit(solution)/shard_map/all_to_all | solution.py:67
  589.8 67.7 %reduce-scatter.11.cloned.1.call-start = ((), (), s32[]{:S(2)}) async-start(), calls=%async_computation.21 | async-start | bytes 1310720 | tf_op jit(solution)/shard_map/reduce_scatter | solution.py:790
  649.6 47.0 %all-to-all-start.10 = ((bf16[4,256,512]{2,1,0:T(8,128)(2,1)}), bf16[4,256,512]{2,1,0:T(8,128)(2,1)}, u32[]{:S(2)}, u32[]{:S(2)}) async-start(bf16[4,256,512]{2,1,0:T(8,128)(2,1)} %bitcast.235), calls=%async_computation.14 | async-start | bytes 2097152 | tf_op jit(solution)/shard_map/all_to_all | solution.py:67
  654.7 66.3 %reduce-scatter.9.cloned.1.call-start = ((), (), s32[]{:S(2)}) async-start(), calls=%async_computation.20 | async-start | bytes 1310720 | tf_op jit(solution)/shard_map/reduce_scatter | solution.py:814
  665.5 34.1 %collective-permute-start.39 = (bf16[128,2048]{1,0:T(8,128)(2,1)}, bf16[128,2048]{1,0:T(8,128)(2,1)}, u32[]{:S(2)}, u32[]{:S(2)}) collective-permute-start(bf16[128,2048]{1,0:T(8,128)(2,1)} %dynamic-slice_bitcast_fusion.2), channel_id=1, source_target_pairs={{0,2},{2,0},{1,3},{3,1},{4,6},{6,4},{5,7},{7,5},{8,10},{10,8},{9,1... | collective-permute-start | bytes 1572872 | tf_op jit(solution)/shard_map/ppermute | solution.py:45
  (116 other events, 1964.4 us)
Sparse Core Ops, SparseCore 0:
  21.3 29.3 all-gather.5
  56.0 46.7 all-gather.11
  201.0 48.3 all-gather.7
  251.5 66.5 all-gather.9
  361.3 46.9 reduce-scatter.6
  418.7 47.0 reduce-scatter.4
  598.1 33.7 reduce-scatter.10
  658.0 38.4 reduce-scatter.8

commit v4 on v3

--- a/solution.py
+++ b/solution.py
@@ -112,6 +112,10 @@
 
 def together(*values):
     return lax.optimization_barrier(values)
+
+
+def after(value, *others):
+    return lax.optimization_barrier((value, *others))[0]
 
 
 def ancestor_count(parents, seg):
@@ -209,7 +213,7 @@
     )(rows, *weights, cosine, sine)
 
 
-def attend_kernel(parents, segs, queries, keys_values, out, stats, scores):
+def attend_kernel(parents, segs, queries, keys_values, out, stats, out_low, scores):
     seg = segs[pl.program_id(0)]
     count = ancestor_count(parents, seg)
     pairs = [block.astype(jnp.float32) * attn_scale for block in lane_blocks(queries)]
@@ -246,6 +250,7 @@
     stats[0] = row_max + jnp.log(total)
     for place, pair in enumerate(unstacked_heads(mixed, False)):
         out[:, place * LANES : (place + 1) * LANES] = pair
+        out_low[:, place * LANES : (place + 1) * LANES] = pair.astype(jnp.bfloat16)
 
 
 def attend_back_kernel(
@@ -325,10 +330,11 @@
         attend_kernel,
         grid=(steps,),
         in_specs=[scalar, scalar, block, whole],
-        out_specs=[block, stat],
+        out_specs=[block, stat, block],
         out_shape=[
             jax.ShapeDtypeStruct((count, cols), jnp.float32),
             jax.ShapeDtypeStruct((steps, rows, 1), jnp.float32),
+            jax.ShapeDtypeStruct((count, cols), jnp.bfloat16),
         ],
         scratch_shapes=[pltpu.VMEM((MAX_STEPS + 1, rows, SEG), jnp.float32)],
         compiler_params=pltpu.CompilerParams(vmem_limit_bytes=KERNEL_VMEM),
@@ -390,12 +396,16 @@
     in_turn(per, pieces, step)
 
 
-def gate_back_kernel(per, parts, pieces, *refs):
-    grads, weights = refs[:parts], refs[parts : parts + parts * pieces]
-    gate_slope, up_slope, grad_gate, grad_up = refs[parts + parts * pieces :]
+def gate_back_kernel(per, parts, pieces, grads, *refs):
+    weights, (gate_slope, up_slope, grad_gate, grad_up) = refs[:-4], refs[-4:]
+    blocks, _, depth = weights[0].shape
 
     def step(i):
-        grad = sum(nt_dot(grads[k][...], weights[k * pieces + i][...]) for k in range(parts))
+        grad = 0.0
+        for k in range(parts):
+            for z in range(blocks):
+                at = (k * blocks + z) * depth
+                grad = grad + nt_dot(grads[:, at : at + depth], weights[k * pieces + i][z])
         grad_gate[...] = (grad * gate_slope[...]).astype(jnp.bfloat16)
         grad_up[...] = (grad * up_slope[...]).astype(jnp.bfloat16)
 
@@ -404,11 +414,11 @@
 
 def down_kernel(per, parts, pieces, acts, *refs):
     weights, out = refs[:-1], refs[-1]
-    depth = weights[0].shape[0]
+    depth = weights[0].shape[1]
 
     def step(k):
         total = sum(
-            nn_dot(acts[:, i * depth : (i + 1) * depth], weights[k * pieces + i][...])
+            nn_dot(acts[:, i * depth : (i + 1) * depth], weights[k * pieces + i][0])
             for i in range(pieces)
         )
         out[...] = total.astype(jnp.bfloat16)
@@ -416,16 +426,16 @@
     in_turn(per, parts, step)
 
 
-def pair_kernel(per, parts, pieces, first, second, *refs):
-    gates, ups, out = refs[: parts * pieces], refs[parts * pieces : -1], refs[-1]
-    depth = gates[0].shape[1]
+def turned_kernel(terms, per, parts, pieces, *refs):
+    lefts, weights, out = refs[:terms], refs[terms:-1], refs[-1]
+    depth = weights[0].shape[1]
 
     def step(k):
         total = 0.0
-        for i in range(pieces):
-            columns = slice(i * depth, (i + 1) * depth)
-            total = total + nt_dot(first[:, columns], gates[k * pieces + i][...])
-            total = total + nt_dot(second[:, columns], ups[k * pieces + i][...])
+        for term, left in enumerate(lefts):
+            for i in range(pieces):
+                weight = weights[(term * parts + k) * pieces + i]
+                total = total + nt_dot(left[:, i * depth : (i + 1) * depth], weight[...])
         out[...] = total.astype(jnp.bfloat16)
 
     in_turn(per, parts, step)
@@ -435,18 +445,23 @@
     parts, pieces = len(weights[0]), len(weights[0][0])
     shape = weights[0][0][0].shape
     groups = pieces if by_piece else parts
-    tile = (min(whole[0].shape[0], 1024), min(shape[axis], 256))
-    per = shape[axis] // tile[1]
-    count, cols = whole[0].shape[0], groups * shape[axis]
+    if len(shape) == 3 and axis == 0:
+        width, block, per = shape[0] * shape[2], (1, *shape[1:]), shape[0]
+    else:
+        width = shape[axis]
+        per = width // min(width, 256)
+        block = tuple(n // per if at == axis else n for at, n in enumerate(shape))
+    tile = (min(whole[0].shape[0], 1024), width // per)
+    count, cols = whole[0].shape[0], groups * width
 
     def piece_spec(k, i):
         group = i if by_piece else k
 
         def place(row, col):
             at = jnp.clip(col - group * per, 0, per - 1)
-            return (0, at) if axis == 1 else (at, 0)
-
-        return pl.BlockSpec((shape[0], tile[1]) if axis == 1 else (tile[1], shape[1]), place)
+            return tuple(at if dim == axis else 0 for dim in range(len(shape)))
+
+        return pl.BlockSpec(block, place)
 
     tile_spec = pl.BlockSpec(tile, lambda row, col: (row, col))
     flat = [v for weight in weights for row in weight for v in row]
@@ -470,16 +485,98 @@
 
 def gate_backward(grads, downs, gate_slope, up_slope):
     outs = (jnp.bfloat16, jnp.bfloat16)
-    return wide_call(gate_back_kernel, grads, [downs], [gate_slope, up_slope], 0, True, outs)
+    return wide_call(gate_back_kernel, [grads], [downs], [gate_slope, up_slope], 1, True, outs)
 
 
 def down_forward(acts, downs):
-    return wide_call(down_kernel, [acts], [downs], [], 1, False, (jnp.bfloat16,))[0]
-
-
-def pair_product(grad_gate, grad_up, gates, ups):
-    whole = [grad_gate, grad_up]
-    return wide_call(pair_kernel, whole, [gates, ups], [], 0, False, (jnp.bfloat16,))[0]
+    if downs[0][0].shape[2] % LANES:
+        rows = [jnp.concatenate([joined_columns(v) for v in row], axis=0) for row in downs]
+        return nn_dot(acts, jnp.concatenate(rows, axis=1)).astype(jnp.bfloat16)
+    return wide_call(down_kernel, [acts], [downs], [], 0, False, (jnp.bfloat16,))[0]
+
+
+def turned_product(lefts, weights):
+    kernel = functools.partial(turned_kernel, len(lefts))
+    return wide_call(kernel, lefts, weights, [], 0, False, (jnp.bfloat16,))[0]
+
+
+def o_kernel(parts, place, *refs):
+    rows, weights, out = refs[:-1 - parts], refs[-1 - parts : -1], refs[-1]
+    blocks = weights[0].shape[0]
+    depth = rows[0].shape[1]
+    at = lax.rem(pl.program_id(0), blocks)
+    for k in range(parts):
+
+        @pl.when(pl.program_id(0) // blocks == k)
+        def _(k=k):
+            total = 0.0
+            for i, piece in enumerate(rows):
+                group = lax.rem(place[0] + i, len(rows))
+                start = pl.multiple_of(group * depth, depth)
+                total = total + nn_dot(piece[...], weights[k][at, pl.ds(start, depth), :])
+            out[...] = total.astype(jnp.bfloat16)
+
+
+def o_forward(pieces, weights, place):
+    count, depth = pieces[0].shape
+    blocks, _, step = weights[0].shape
+    if step % LANES:
+        full = jnp.concatenate([joined_columns(v) for v in weights], axis=1)
+        return nn_dot(in_groups(pieces), full).astype(jnp.bfloat16)
+    whole = pl.BlockSpec(weights[0].shape, lambda j: (0, 0, 0))
+    return pl.pallas_call(
+        functools.partial(o_kernel, len(weights)),
+        grid=(len(weights) * blocks,),
+        in_specs=[pl.BlockSpec(memory_space=pltpu.SMEM)]
+        + [pl.BlockSpec((count, depth), lambda j: (0, 0))] * len(pieces)
+        + [whole] * len(weights),
+        out_specs=pl.BlockSpec((count, step), lambda j: (0, j)),
+        out_shape=jax.ShapeDtypeStruct((count, len(weights) * blocks * step), jnp.bfloat16),
+        compiler_params=pltpu.CompilerParams(vmem_limit_bytes=KERNEL_VMEM),
+        cost_estimate=SMALL_COST,
+    )(place.astype(jnp.int32).reshape(1), *pieces, *weights)
+
+
+def o_back_kernel(parts, rows, *refs):
+    weights, out = refs[:parts], refs[parts]
+    blocks, _, step = weights[0].shape
+    total = 0.0
+    for k in range(parts):
+        for z in range(blocks):
+            at = (k * blocks + z) * step
+            total = total + nt_dot(rows[:, at : at + step], weights[k][z])
+    out[...] = total.astype(jnp.bfloat16)
+
+
+def o_backward(rows, weights):
+    return pl.pallas_call(
+        functools.partial(o_back_kernel, len(weights)),
+        out_shape=jax.ShapeDtypeStruct((rows.shape[0], weights[0].shape[1]), jnp.bfloat16),
+        compiler_params=pltpu.CompilerParams(vmem_limit_bytes=KERNEL_VMEM),
+        cost_estimate=SMALL_COST,
+    )(rows, *weights)
+
+
+def split_kernel(*refs):
+    values, out = refs[:-1], refs[-1]
+    for i, value in enumerate(values):
+        out[0, i] = value[...]
+
+
+def split_columns(values, count):
+    rows, cols = values[0].shape
+    step = cols // count
+    if step % LANES:
+        return jnp.stack([column_blocks(v, count) for v in values], axis=1)
+    return pl.pallas_call(
+        split_kernel,
+        grid=(count,),
+        in_specs=[pl.BlockSpec((rows, step), lambda j: (0, j))] * len(values),
+        out_specs=pl.BlockSpec((1, len(values), rows, step), lambda j: (j, 0, 0, 0)),
+        out_shape=jax.ShapeDtypeStruct((count, len(values), rows, step), values[0].dtype),
+        compiler_params=pltpu.CompilerParams(vmem_limit_bytes=KERNEL_VMEM),
+        cost_estimate=SMALL_COST,
+    )(*values)
 
 
 def row_norm(value):
@@ -502,8 +599,16 @@
     return [value[:, i * part : (i + 1) * part] for i in range(count)]
 
 
-def joined(pieces, outer, inner):
-    return jnp.concatenate([jnp.concatenate(row, axis=inner) for row in pieces], axis=outer)
+def crossed(by_x, by_y):
+    half = by_x[0].shape[0] // 2
+    upper = [[rotated(v[:half], "x", i) for i in range(1, len(by_x))] for v in by_y[1:]]
+    lower = [[rotated(v[half:], "y", k) for v in by_x[1:]] for k in range(1, len(by_y))]
+    return upper, lower
+
+
+def quarters(by_x, by_y, upper, lower):
+    far = [[jnp.concatenate(v, axis=0) for v in zip(*rows)] for rows in zip(upper, lower)]
+    return [by_x] + [[by_y[k], *far[k - 1]] for k in range(1, len(by_y))]
 
 
 def matmul(left, right):
@@ -544,37 +649,55 @@
     )
 
 
-def turned_back(value, cosine_table, sine_table):
-    first, second = halves(value, 2)
-    return jnp.concatenate(
-        [
-            first * cosine_table + second * sine_table,
-            second * cosine_table - first * sine_table,
-        ],
-        axis=1,
-    )
-
-
-def tensor_gather(value):
-    rows = jnp.stack(natural_pieces(relative_pieces(value, "x"), "x"))
+def in_order(pieces):
+    return natural_pieces(pieces, "y")
+
+
+def turned_sum_kernel(blocks, cosine, sine, out):
+    total = sum(blocks[i, 0].astype(jnp.float32) for i in range(blocks.shape[0]))
+    out[...] = turned(total.T, cosine[...], sine[...], -1.0).astype(jnp.bfloat16)
+
+
+def turned_sum(blocks, cosine, sine):
+    terms, segs, lanes, seg = blocks.shape
+    table = pl.BlockSpec((seg, lanes), lambda s: (s, 0))
+    return pl.pallas_call(
+        turned_sum_kernel,
+        grid=(segs,),
+        in_specs=[pl.BlockSpec((terms, 1, lanes, seg), lambda s: (0, s, 0, 0)), table, table],
+        out_specs=table,
+        out_shape=jax.ShapeDtypeStruct((segs * seg, lanes), jnp.bfloat16),
+        compiler_params=pltpu.CompilerParams(vmem_limit_bytes=KERNEL_VMEM),
+        cost_estimate=SMALL_COST,
+    )(blocks, cosine, sine)
+
+
+def gathered_core(x_pieces):
+    rows = jnp.stack(natural_pieces(x_pieces, "x"))
     rows = jnp.stack(natural_pieces(relative_pieces(rows, "c"), "c"), axis=1)
-    return rows.reshape(-1, value.shape[1])
+    return rows.reshape(-1, rows.shape[-1])
+
+
+def own_first(value, axis):
+    size = value.shape[0]
+    place = lax.axis_index(axis)
+    return [
+        lax.dynamic_index_in_dim(value, lax.rem(place - k + size, size), 0, keepdims=False)
+        for k in range(size)
+    ]
+
+
+def core_sum(part, rows):
+    blocks = part.reshape(lax.axis_size("x"), lax.axis_size("c"), rows, -1)
+    return summed_pieces(own_first(blocks.transpose(1, 0, 2, 3), "c"), "c").astype(jnp.bfloat16)
+
+
+def x_blocks(value):
+    return own_first(value, "x")
 
 
 def tensor_sum(part, rows):
-    x_size, c_size = lax.axis_size("x"), lax.axis_size("c")
-    blocks = part.reshape(x_size, c_size, rows, -1)
-    c_place, x_place = lax.axis_index("c"), lax.axis_index("x")
-
-    def block(value, place, k, axis):
-        size = value.shape[axis]
-        return lax.dynamic_index_in_dim(
-            value, lax.rem(place - k + size, size), axis, keepdims=False
-        )
-
-    mine = summed_pieces([block(blocks, c_place, k, 1) for k in range(c_size)], "c")
-    mine = mine.astype(jnp.bfloat16)
-    return summed_pieces([block(mine, x_place, k, 0) for k in range(x_size)], "x")
+    return summed_pieces(x_blocks(core_sum(part, rows)), "x")
 
 
 def local(
@@ -603,8 +726,6 @@
 
     own_tokens = relative_columns(tokens)
     own_grad = relative_columns(out_grad).astype(jnp.float32)
-    group_tokens = tensor_gather(own_tokens)
-
     both_gains = jnp.concatenate([norm_gain, mlp_gain])
     both_gains = jnp.pad(both_gains, (0, -both_gains.shape[0] % (2 * kv_cols)))
     key_heads, value_heads = halves(key_matrix, kv_local), halves(value_matrix, kv_local)
@@ -615,9 +736,13 @@
         ],
         axis=0,
     )
-    kv_z = gathered(kv_shard, "z")
+    kv_copies = jnp.broadcast_to(kv_shard[None], (z_size, *kv_shard.shape))
+    kv_copies, q_weight = together(kv_copies, q_weight)
+    kv_z = exchanged(kv_copies, "z")
     q_z = lax.all_gather(q_weight, "z", axis=0, tiled=True)
-    kv_z, o_weight, group_tokens = together(kv_z, o_weight, group_tokens)
+    group_tokens = gathered_core(relative_pieces(own_tokens, "x"))
+    kv_z, o_weight = together(kv_z, o_weight)
+    o_z = lax.all_gather(o_weight, "z", axis=0)
 
     depth = segment_depth(parents)
     seg_count = group_rows // SEG
@@ -639,7 +764,6 @@
     cosine_keys = jnp.where(key_lanes, cosine_lanes[:group_rows], 1.0)
     sine_keys = jnp.where(key_lanes, sine_lanes[:group_rows], 0.0)
 
-    o_z = lax.all_gather(o_weight, "z", axis=0)
     kv_zy = relative_pieces(kv_z, "y")
     kv_weights = [v[:, :own_width].reshape(-1, 2 * kv_cols) for v in kv_zy]
     gains = [
@@ -652,193 +776,202 @@
     normed_one, inv_one = row_norm(inputs)
     group_normed, _ = row_norm(group_tokens.astype(jnp.float32))
     rows_one = (group_normed * gain_one).astype(low)
+    rows_one, q_z = together(rows_one, q_z)
+    q_weights = relative_pieces(q_z, "y")
     kv_rows = project(rows_one, kv_weights, cosine_keys, sine_keys)
     kv_swapped = jnp.stack(natural_pieces(sent_groups(kv_rows), "y"))
-    q_z, kv_swapped = together(q_z, kv_swapped)
-
     all_kv = gathered(kv_swapped, "z").reshape(-1, SEG, LANES)
-    q_weights = relative_pieces(q_z, "y")
-    q_weights, o_z = together(q_weights, o_z)
-    o_zy = relative_pieces(joined_columns(o_z), "y")
+    wide_blocks = split_columns(after((gate_weight, up_weight), kv_z), z_size)
+    q_weights, wide_blocks = together(q_weights, wide_blocks)
     query_rows = project(rows_one, q_weights, cosine_lanes[:group_rows], sine_lanes[:group_rows])
     queries = sent_groups(query_rows)
-    all_kv, queries, gate_weight, up_weight = together(all_kv, queries, gate_weight, up_weight)
-
-    gate_z = exchanged(column_blocks(gate_weight, z_size), "z")
+    tables = [jnp.split(v, y_size) for v in (cosine_lanes, sine_lanes)]
+    key_tables = [
+        jnp.concatenate(in_order(jnp.split(v, y_size)))
+        for v in (jnp.where(key_lanes, cosine_lanes, 1.0), jnp.where(key_lanes, sine_lanes, 0.0))
+    ]
+    all_kv, queries, o_z, wide_blocks, tables, key_tables = together(
+        all_kv, queries, o_z, wide_blocks, tables, key_tables
+    )
+
+    wide_z = exchanged(wide_blocks, "z")
+    o_weights = relative_pieces(o_z, "y")
     seg_lists = jnp.split(segs, y_size)
-    attends = [None] * y_size
+    attends, lows = [None] * y_size, [None] * y_size
     for k in range(y_size - 1, 0, -1):
-        attends[k] = attend(parents, seg_lists[k], queries[k], all_kv)
-    queries[0], attends, o_zy = together(queries[0], attends, o_zy)
-    returned = [rotated(attends[k][0].astype(low), "y", -k) for k in range(1, y_size)]
-    attends[0] = attend(parents, seg_lists[0], queries[0], all_kv)
-    attn_low = in_groups([attends[0][0].astype(low), *returned])
-    attn_low, o_zy, gate_z, up_weight = together(attn_low, o_zy, gate_z, up_weight)
-
-    o_full = jnp.concatenate(o_zy, axis=1)
-    attn_part = matmul(attn_low, o_full).astype(low)
-    attn_mine = tensor_sum(attn_part, local_rows)
-    up_z = exchanged(column_blocks(up_weight, z_size), "z")
-    gate_zy = relative_pieces(gate_z.reshape(z_size * own_width, -1), "y")
-    up_z, gate_zy, attn_mine, down_weight = together(up_z, gate_zy, attn_mine, down_weight)
+        *attends[k], lows[k] = attend(parents, seg_lists[k], queries[k], all_kv)
+    queries[0], attends[1:], lows[1:] = together(queries[0], attends[1:], lows[1:])
+    returned = [rotated(v, "y", -k) for k, v in enumerate(lows[1:], 1)]
+    *attends[0], lows[0] = attend(parents, seg_lists[0], queries[0], all_kv)
+    attn_pieces = [lows[0], *returned]
+    attn_pieces, o_weights = together(attn_pieces, o_weights)
+    attn_part = o_forward(attn_pieces, o_weights, y_place)
+    attn_low = in_groups(attn_pieces)
+    attn_core = core_sum(attn_part, local_rows)
+    attn_core, wide_z = together(attn_core, wide_z)
+
+    gate_z, up_z = (wide_z[:, i].reshape(z_size * own_width, -1) for i in range(2))
+    gate_zy, up_zy = relative_pieces(gate_z, "y"), relative_pieces(up_z, "y")
+    gate_zx = relative_pieces(gate_z, "x")
+    attn_mine = summed_pieces(x_blocks(attn_core), "x")
+    attn_mine, up_z, down_weight = together(attn_mine, up_z, down_weight)
 
     middle = inputs + branch_scale * attn_mine
     normed_two, inv_two = row_norm(middle)
     hidden_two = (normed_two * gain_two).astype(low)
     rows_two = lax.all_gather(hidden_two, ("z", "c"), axis=0, tiled=True)
-    up_z = up_z.reshape(z_size * own_width, -1)
-    up_zy = relative_pieces(up_z, "y")
-    gate_zx = relative_pieces(gate_zy[0], "x")
-    gate_zx, up_zy, up_z = together(gate_zx, up_zy, up_z)
+    down_z = exchanged(down_weight.reshape(z_size, -1, own_width), "z")
+    gate_zx, gate_zy, up_z = together(gate_zx, gate_zy, up_z)
+    gate_far = [relative_pieces(v, "y")[1:] for v in gate_zx[1:]]
     up_zx = relative_pieces(up_z, "x")
-    gate_far = [relative_pieces(v, "y")[1:] for v in gate_zx[1:]]
-    rows_two, up_zx, gate_far, down_weight = together(rows_two, up_zx, gate_far, down_weight)
-
-    down_z = joined_columns(exchanged(down_weight.reshape(z_size, -1, own_width), "z"))
-    half = own_width * z_size // 2
-    upper = [[rotated(v[:half], "x", i) for i in range(1, x_size)] for v in up_zy[1:]]
-    lower = [[rotated(v[half:], "y", k) for v in up_zx[1:]] for k in range(1, y_size)]
-    down_z, upper, lower = together(down_z, upper, lower)
-    up_far = [
-        [jnp.concatenate(pair, axis=0) for pair in zip(*rows)] for rows in zip(upper, lower)
-    ]
-    gates = [gate_zx] + [
-        [gate_zy[k], *[far[k - 1] for far in gate_far]] for k in range(1, y_size)
-    ]
+    grad_mlp = (branch_scale * own_grad).astype(low)
+    up_zx, up_zy, grad_mlp, down_z = together(up_zx, up_zy, grad_mlp, down_z)
+    grad_mlp_rows = lax.all_gather(grad_mlp, ("z", "c"), axis=0, tiled=True)
+    up_far = [relative_pieces(v, "x")[1:] for v in up_zy[1:]]
+    rows_two, gate_far, up_far, down_z = together(rows_two, gate_far, up_far, down_z)
+    down_zy, down_zx = relative_pieces(down_z, "y"), relative_pieces(down_z, "x")
+    gates = [gate_zx] + [[gate_zy[k], *[v[k - 1] for v in gate_far]] for k in range(1, y_size)]
     ups = [up_zx] + [[up_zy[k], *up_far[k - 1]] for k in range(1, y_size)]
-
-    grad_mlp = (branch_scale * own_grad).astype(low)
-    grad_mlp_rows = lax.all_gather(grad_mlp, ("z", "c"), axis=0, tiled=True)
-    down_zy = relative_pieces(down_z, "y")
-    down_zx = relative_pieces(down_z, "x")
     activated, gate_slope, up_slope = gate_forward(rows_two, gates, ups)
     down_zy, down_zx, activated, gate_slope, up_slope = together(
         down_zy, down_zx, activated, gate_slope, up_slope
     )
-    half = down_z.shape[0] // 2
-    upper = [[rotated(v[:half], "x", i) for i in range(1, x_size)] for v in down_zy[1:]]
-    lower = [[rotated(v[half:], "y", k) for v in down_zx[1:]] for k in range(1, y_size)]
-    upper, lower, grad_mlp_rows = together(upper, lower, grad_mlp_rows)
-    down_far = [
-        [jnp.concatenate(pair, axis=0) for pair in zip(*rows)] for rows in zip(upper, lower)
-    ]
-    downs = [down_zx] + [[down_zy[k], *down_far[k - 1]] for k in range(1, y_size)]
-    grad_mlp_parts = halves(grad_mlp_rows, y_size)
+    down_crossed = together(*crossed(down_zx, down_zy))
+    downs = quarters(down_zx, down_zy, *down_crossed)
     mlp_part = down_forward(activated, downs)
+    mlp_part, grad_mlp_rows = together(mlp_part, grad_mlp_rows)
+
     mlp_mine = lax.psum_scatter(mlp_part, ("z", "c"), scatter_dimension=0, tiled=True)
+    grad_parts, rows_parts = halves(grad_mlp_rows, y_size), halves(rows_two, y_size)
     acts = halves(activated, x_size)
-    down_far = [
-        summed_pieces([turned_matmul(act, grad) for grad in grad_mlp_parts], "y").astype(low)
-        for act in acts[1:]
-    ]
-    grad_gate_act, grad_up_act = gate_backward(grad_mlp_parts, downs, gate_slope, up_slope)
-    grad_gate_act, grad_up_act, down_far = together(grad_gate_act, grad_up_act, down_far)
-
-    down_near = summed_pieces([turned_matmul(acts[0], grad) for grad in grad_mlp_parts], "y")
-    grad_down_z = summed_pieces([down_near, *down_far], "x").astype(low)
-    input_part = pair_product(grad_gate_act, grad_up_act, gates, ups)
-    input_part, grad_down_z, rows_two = together(input_part, grad_down_z, rows_two)
+    down_far = [summed_pieces([turned_matmul(a, b) for a in grad_parts], "y").astype(low) for b in acts[1:]]
+    grad_gate_act, grad_up_act = gate_backward(grad_mlp_rows, downs, gate_slope, up_slope)
+    grad_gate_act, grad_up_act = together(grad_gate_act, grad_up_act)
+
+    gate_parts, up_parts = halves(grad_gate_act, x_size), halves(grad_up_act, x_size)
+    gate_dots = [[turned_matmul(a, b) for a in rows_parts] for b in gate_parts[1:]]
+    up_dots = [[turned_matmul(a, b) for b in up_parts] for a in rows_parts[1:]]
+    for dots in gate_dots + up_dots:
+        dots[1:] = [v.astype(low) for v in dots[1:]]
+    grad_gate_act, gate_dots, up_dots = together(grad_gate_act, gate_dots, up_dots)
+    gate_far = [summed_pieces(v, "y").astype(low) for v in gate_dots]
+    up_far = [summed_pieces(v, "x").astype(low) for v in up_dots]
+    input_part = turned_product([grad_gate_act, grad_up_act], [gates, ups])
+    input_part, down_far = together(input_part, down_far)
 
     grad_rows_two = lax.psum_scatter(input_part, ("z", "c"), scatter_dimension=0, tiled=True)
-    rows_parts = halves(rows_two, y_size)
-    gate_parts, up_parts = halves(grad_gate_act, x_size), halves(grad_up_act, x_size)
-    gate_far = [
-        summed_pieces([turned_matmul(a, b) for a in rows_parts], "y").astype(low)
-        for b in gate_parts[1:]
-    ]
-    up_far = [
-        summed_pieces([turned_matmul(a, b) for b in up_parts], "x").astype(low)
-        for a in rows_parts[1:]
-    ]
-    gate_far, up_far = together(gate_far, up_far)
+    gate_far, up_far, acts = together(gate_far, up_far, acts)
+    down_near = summed_pieces([turned_matmul(a, acts[0]) for a in grad_parts], "y")
+    down_far = [rotated(v, "x", -1 - i) for i, v in enumerate(down_far)]
+    down_near, down_far, gate_parts = together(down_near, down_far, gate_parts)
+    grad_down_z = sum([v.astype(jnp.float32) for v in down_far], down_near).astype(low)
     gate_near = summed_pieces([turned_matmul(a, gate_parts[0]) for a in rows_parts], "y")
-    grad_gate_z = summed_pieces([gate_near, *gate_far], "x").astype(low)
-    grad_rows_two, grad_gate_z, up_far, mlp_mine = together(
-        grad_rows_two, grad_gate_z, up_far, mlp_mine
-    )
-
-    mixed = natural_columns((middle + branch_scale * mlp_mine.astype(jnp.float32)).astype(low))
+    gate_far = [rotated(v, "x", -1 - i) for i, v in enumerate(gate_far)]
+    up_near = [turned_matmul(rows_parts[0], b) for b in up_parts]
+    up_near[1:] = [v.astype(low) for v in up_near[1:]]
+    grad_rows_two, mlp_mine, up_far, up_near, grad_down_z = together(
+        grad_rows_two, mlp_mine, up_far, up_near, grad_down_z
+    )
     grad_rows_two = grad_rows_two.astype(jnp.float32)
     gain_two_part = jnp.sum(grad_rows_two * normed_two, axis=0)
     grad_middle = own_grad + norm_back(grad_rows_two, normed_two, inv_two, gain_two)
     grad_attn = (branch_scale * grad_middle).astype(low)
-    grad_gate = exchanged(grad_gate_z.reshape(z_size, own_width, -1), "z")
+    attn_x = relative_pieces(grad_attn, "x")
     up_far = [rotated(v, "y", -1 - i) for i, v in enumerate(up_far)]
-    grad_attn_rows = tensor_gather(grad_attn)
-    grad_attn_rows, up_far, grad_down_z = together(grad_attn_rows, up_far, grad_down_z)
-
-    grad_heads = sent_groups(matmul_turned(grad_attn_rows, o_full).astype(low))
-    up_near = summed_pieces([turned_matmul(rows_parts[0], b) for b in up_parts], "x")
-    grad_up_z = sum([v.astype(jnp.float32) for v in up_far], up_near).astype(low)
-    grad_heads, grad_gate, grad_down_z, grad_attn_rows = together(
-        grad_heads, grad_gate, grad_down_z, grad_attn_rows
-    )
-    grad_down = exchanged(column_blocks(grad_down_z, z_size), "z")
-    grad_o_y = summed_pieces(
-        [turned_matmul(attn_low, v) for v in halves(grad_attn_rows, y_size)], "y"
-    ).astype(low)
-    cosines, sines = jnp.split(cosine_lanes, y_size), jnp.split(sine_lanes, y_size)
+    grad_gate_z = sum([v.astype(jnp.float32) for v in gate_far], gate_near).astype(low)
+    wide_z = jnp.stack([v.reshape(z_size, own_width, -1) for v in (grad_gate_z, grad_down_z)], 1)
+    attn_x, wide_z, up_near = together(attn_x, wide_z, up_near)
+    wide_z = exchanged(wide_z, "z")
+    grad_attn_rows = gathered_core(attn_x)
+    grad_heads = o_backward(grad_attn_rows, o_weights)
+    grad_heads, grad_attn_rows, up_near = together(grad_heads, grad_attn_rows, up_near)
+
+    grad_heads = sent_groups(grad_heads)
+    o_dots = [turned_matmul(v, attn_low) for v in halves(grad_attn_rows, y_size)[1:]]
+    o_dots = [v.astype(low) for v in o_dots]
+    grad_heads, o_dots, up_near, grad_attn_rows = together(
+        grad_heads, o_dots, up_near, grad_attn_rows
+    )
+    o_sent = [rotated(v, "y", -1 - i) for i, v in enumerate(o_dots)]
+    up_mine = [rotated(v, "x", -1 - i) for i, v in enumerate(up_near[1:])]
+    cosines, sines = tables
     grad_queries, sums = [None] * y_size, None
     for k in range(y_size - 1, 0, -1):
         grad_queries[k], sums = attend_back(
             parents, seg_lists[k], queries[k], grad_heads[k], *attends[k], cosines[k], sines[k],
             all_kv, sums,
         )
-    grad_queries[1:], sums, grad_o_y, grad_up_z = together(
-        grad_queries[1:], sums, grad_o_y, grad_up_z
-    )
-    grad_o = lax.psum_scatter(
-        column_blocks(grad_o_y, z_size), "z", scatter_dimension=0, tiled=True
-    )[0]
+    grad_o_y = turned_matmul(halves(grad_attn_rows, y_size)[0], attn_low)
+    grad_o_y = sum([v.astype(jnp.float32) for v in o_sent], grad_o_y).astype(low)
+    grad_queries[1:], sums, grad_o_y = together(grad_queries[1:], sums, grad_o_y)
+    grad_o = lax.psum_scatter(grad_o_y, "z", scatter_dimension=0, tiled=True)
     returned = [rotated(v, "y", -k) for k, v in enumerate(grad_queries[1:], 1)]
     grad_queries[0], grad_kv = attend_back(
         parents, seg_lists[0], queries[0], grad_heads[0], *attends[0], cosines[0], sines[0],
         all_kv, sums,
     )
+    grad_queries[0], grad_kv, returned, up_far, up_mine, up_near, wide_z = together(
+        grad_queries[0], grad_kv, returned, up_far, up_mine, up_near, wide_z
+    )
+
+    def owned_dots(left, right):
+        dots = [turned_matmul(v, right) for v in halves(left, y_size)]
+        return dots[:1] + [v.astype(low) for v in dots[1:]]
+
+    def sent_back(dots):
+        return [rotated(v, "y", -1 - i) for i, v in enumerate(dots[1:])]
+
+    def total(own, sent):
+        return sum([v.astype(jnp.float32) for v in sent], own).astype(low)
+
+    kv_mine = exchanged(grad_kv.reshape(z_size, y_size * seg_count, LANES, SEG), "z")
     grad_queries = in_groups([grad_queries[0], *returned])
-    grad_queries, grad_kv, grad_down, grad_up_z = together(
-        grad_queries, grad_kv, grad_down, grad_up_z
-    )
-
-    def owned_rows(left, right):
-        return summed_pieces([turned_matmul(v, right) for v in halves(left, y_size)], "y").astype(
-            low
-        )
-
-    kv_mine = summed_blocks(grad_kv.reshape(z_size, y_size * seg_count, LANES, SEG), "z")
-    grad_q_y = owned_rows(rows_one, grad_queries)
+    query_dots = owned_dots(rows_one, grad_queries)
+    query_sent = sent_back(query_dots)
     q_full = jnp.concatenate(q_weights, axis=0)
     query_part = matmul_turned(grad_queries, q_full)
-    kv_mine, query_part, grad_q_y, grad_up_z = together(kv_mine, query_part, grad_q_y, grad_up_z)
-
-    grad_q = lax.psum_scatter(
-        grad_q_y.reshape(z_size, own_width, -1), "z", scatter_dimension=0, tiled=True
-    )[0]
+    grad_up_z = total(up_near[0], up_far + up_mine)
+    kv_mine, query_part, query_dots, query_sent, grad_up_z = together(
+        kv_mine, query_part, query_dots, query_sent, grad_up_z
+    )
+
     grad_up = exchanged(grad_up_z.reshape(z_size, own_width, -1), "z")
-    kv_mine = kv_mine.transpose(0, 2, 1).reshape(y_size, group_rows, LANES)
-    kv_mine = [lax.dynamic_index_in_dim(kv_mine, s, 0, keepdims=False) for s in sources]
-    kv_mine = jnp.concatenate(kv_mine, axis=0)
-    grad_keys = turned_back(kv_mine[:, :HEAD_SIZE], cosine_table, sine_table)
-    grad_kv_rows = jnp.concatenate([grad_keys, kv_mine[:, HEAD_SIZE:]], axis=1).astype(low)
+    kv_mine = turned_sum(kv_mine, *key_tables).reshape(y_size, group_rows, LANES)
+    kv_mine = own_first(kv_mine, "y")
     grad_kv_rows = in_groups(
-        [grad_kv_rows[:group_rows]]
-        + [
-            rotated(grad_kv_rows[k * group_rows : (k + 1) * group_rows], "y", -k)
-            for k in range(1, y_size)
-        ]
+        [kv_mine[0]] + [rotated(v, "y", -k) for k, v in enumerate(kv_mine[1:], 1)]
     )
     kv_full = jnp.concatenate(kv_weights, axis=0)
     input_one = (query_part + matmul_turned(grad_kv_rows, kv_full)).astype(low)
-    grad_kv_y = owned_rows(rows_one, grad_kv_rows)
-    grad_rows_one = tensor_sum(input_one, local_rows)
-    grad_kv_y, grad_rows_one = together(grad_kv_y, grad_rows_one)
-    grad_kv_weight = summed_blocks(grad_kv_y.reshape(z_size, own_width, -1), "z")
-    grad_q, grad_o = grad_q.astype(jnp.float32), grad_o.astype(jnp.float32)
+    input_core = core_sum(input_one, local_rows)
+    kv_dots = owned_dots(rows_one, grad_kv_rows)
+    kv_sent = sent_back(kv_dots)
+    input_core, query_sent, query_dots, grad_up = together(
+        input_core, query_sent, query_dots, grad_up
+    )
+    grad_q_y = total(query_dots[0], query_sent)
+    grad_q = lax.psum_scatter(grad_q_y, "z", scatter_dimension=0, tiled=True)
+    input_x = x_blocks(input_core)
+    input_sent = [rotated(v, "x", -1 - i) for i, v in enumerate(input_x[1:])]
+    input_x[0], input_sent, kv_sent, kv_dots, mlp_mine = together(
+        input_x[0], input_sent, kv_sent, kv_dots, mlp_mine
+    )
+    grad_rows_one = sum([v.astype(jnp.float32) for v in input_sent], input_x[0].astype(jnp.float32))
+    kv_blocks = own_first(total(kv_dots[0], kv_sent).reshape(z_size, own_width, -1), "z")
+    kv_sent = [rotated(v, "z", -1 - i) for i, v in enumerate(kv_blocks[1:])]
     gain_one_part = jnp.sum(grad_rows_one * normed_one, axis=0)
     grad_inputs = grad_middle + norm_back(grad_rows_one, normed_one, inv_one, gain_one)
+    kv_sent, kv_blocks, grad_inputs, wide_z, grad_up, grad_q, grad_o, mlp_mine = together(
+        kv_sent, kv_blocks, grad_inputs, wide_z, grad_up, grad_q, grad_o, mlp_mine
+    )
+    mixed = natural_columns((middle + branch_scale * mlp_mine.astype(jnp.float32)).astype(low))
     grad_tokens = natural_columns(grad_inputs.astype(low))
-    grad_gate, grad_up = (joined_columns(v).astype(jnp.float32) for v in (grad_gate, grad_up))
-    grad_down = grad_down.reshape(-1, own_width).astype(jnp.float32)
+    grad_kv_weight = sum([v.astype(jnp.float32) for v in kv_sent], kv_blocks[0].astype(jnp.float32))
+    grad_q, grad_o = grad_q.astype(jnp.float32), grad_o.astype(jnp.float32).T
+    grad_gate, grad_down, grad_up = (
+        joined_columns(v).astype(jnp.float32) for v in (wide_z[:, 0], wide_z[:, 1], grad_up)
+    )
+    grad_down = grad_down.T
 
     gain_parts = jnp.stack([gain_one_part, gain_two_part], axis=0)
     gain_parts = natural_columns(gain_parts).reshape(2, z_size * y_size, 1, own_width)

time: 752 us -> 670 us (0.89)
  waiting for transfers between devices: 319 us -> 268 us
  starting transfers between devices: 117 us -> 83 us
  Pallas kernels: 111 us -> 126 us
    all_to_all x9 -> x7, waiting for transfers between devices: 84.8 us -> 46.9 us  [exchanged(): return lax.all_to_all(blocks, axis, 0, 0, tiled=True)]
    all_gather x1, waiting for transfers between devices: 36.2 us -> 11.5 us  [local(): o_z = lax.all_gather(o_weight, 'z', axis=0)]
    pallas_call x0 -> x4, Pallas kernels: none -> 18 us  [the longest x1 6.06 us: o_forward(): pl.pallas_call(functools.partial(o_kernel, len(weights)), grid=(len(weigh...]
    ppermute x40 -> x42, starting transfers between devices: 58.3 us -> 40.7 us  [rotated(): lax.ppermute(value, axis, [(i, (i + step) % size) for i in range(size)])]
    all_to_all x9 -> x7, starting transfers between devices: 49.4 us -> 37.7 us  [exchanged(): return lax.all_to_all(blocks, axis, 0, 0, tiled=True)]
    ppermute x40 -> x42, waiting for transfers between devices: 194 us -> 206 us  [rotated(): lax.ppermute(value, axis, [(i, (i + step) % size) for i in range(size)])]
    optimization_barrier x1 -> x6, local copies, waits for them, and re-layouts: 0.2 us -> 10.9 us  [together(): return lax.optimization_barrier(values)]
    unnamed x172 -> x168, local copies, waits for them, and re-layouts: 17.2 us -> 15.1 us
  transfers between devices with their start and end apart: 59 -> 58, of which waited for: 33 -> 35; matrix products, arithmetic and copies ran while one was open for 20% -> 19% of each run, Pallas kernels for 14% -> 18%
where the time goes in v4:
time: 670 us; the launch traced here: 663 us
  waiting for transfers between devices  268 us (40%)
  Pallas kernels  126 us (19%)
  starting transfers between devices  83 us (12%)
  local copies, waits for them, and re-layouts  66.1 us (10%)
  other arithmetic  54 us (8%)
  matrix products  49.7 us (7%)
  between operations  16.1 us (2%)
    ppermute x42, waiting for transfers between devices, rotated(): lax.ppermute(value, axis, [(i, (i + step) % size) for i in range(size)])  206 us
    pallas_call x4, Pallas kernels, wide_call(): pl.pallas_call(functools.partial(kernel, per, parts, pieces), grid=(count...  52.6 us
    all_to_all x7, waiting for transfers between devices, exchanged(): return lax.all_to_all(blocks, axis, 0, 0, tiled=True)  46.9 us
    dot_general x18, matrix products, turned_matmul(): lax.dot_general(left, right, (((0,), (0,)), ((), ())), preferred_element_...  41.9 us
    ppermute x42, starting transfers between devices, rotated(): lax.ppermute(value, axis, [(i, (i + step) % size) for i in range(size)])  40.7 us
    all_to_all x7, starting transfers between devices, exchanged(): return lax.all_to_all(blocks, axis, 0, 0, tiled=True)  37.7 us
    pallas_call x2, Pallas kernels, attend_back(): pl.pallas_call(attend_back_kernel, grid=(count // SEG,), in_specs=[scalar...  26 us
    pallas_call x2, Pallas kernels, attend(): pl.pallas_call(attend_kernel, grid=(steps,), in_specs=[scalar, scalar, bl...  21.3 us
  transfers between devices with their start and end apart: 58, of which 35 were waited for; matrix products, arithmetic and copies ran while one was open for 19% of the time, Pallas kernels for 18%

profile of v4, /device:TPU:0, one launch (start us, length us, event | category | flops | bytes accessed | tf_op | source)
XLA Modules:
  0.0 663.2 jit_solution(9041277952355706614)
XLA Ops:
  25.9 8.2 %all-to-all-done = bf16[4,258,256]{2,1,0:T(8,128)(2,1)S(1)} async-done(((bf16[4,258,256]{2,1,0:T(8,128)(2,1)}), bf16[4,258,256]{2,1,0:T(8,128)(2,1)S(1)}, u32[]{:S(2)}, u32[]{:S(2)}) %all-to-all-start) | async-done | bytes 528416 | tf_op jit(solution)/shard_map/all_to_all | solution.py:67
  39.5 8.2 %collective-permute-done.2 = bf16[4,258,256]{2,0,1:T(4,128)(2,1)} collective-permute-done((bf16[4,258,256]{2,0,1:T(4,128)(2,1)}, bf16[4,258,256]{2,0,1:T(4,128)(2,1)}, u32[]{:S(2)}, u32[]{:S(2)}) %collective-permute-start.2) | collective-permute-done | bytes 528416 | tf_op jit(solution)/shard_map/ppermute | solution.py:45
  93.9 11.5 %all-gather.12.cloned.1.call-done = bf16[2048,256]{1,0:T(8,128)(2,1)} async-done(((bf16[512,256]{1,0:T(8,128)(2,1)}), bf16[2048,256]{1,0:T(8,128)(2,1)}) %all-gather.12.cloned.1.call-update) | async-done | bytes 1048592 | tf_op jit(solution)/shard_map/all_gather | solution.py:745
  116.7 12.7 %shard_map.206 = (f32[512,256]{1,0:T(8,128)}, f32[2,1024,1]{2,1,0:T(8,128)}, bf16[512,256]{1,0:T(8,128)(2,1)}) custom-call(s32[16]{0:T(128)} %parents.7, s32[2]{0:T(128)} %copy-done.69, bf16[512,256]{1,0:T(8,128)(2,1)} %copy-done.45, bf16[16,256,128]{2,1,0:T(8,128)(2,1)} %bitcast.200), custom_call_target="tpu_custom_call" | custom-call | flops 268435456 | bytes 262144 | tf_op jit(solution)/shard_map/pallas_call | solution.py:329
  129.4 8.6 %shard_map.207 = (f32[512,256]{1,0:T(8,128)}, f32[2,1024,1]{2,1,0:T(8,128)}, bf16[512,256]{1,0:T(8,128)(2,1)}) custom-call(s32[16]{0:T(128)} %parents.7, s32[2]{0:T(128)} %copy-done.68, bf16[512,256]{1,0:T(8,128)(2,1)} %get-tuple-element.169.queries, bf16[16,256,128]{2,1,0:T(8,128)(2,1)} %bitcast.201), custom_call_target="tpu_custom_call" | custom-call | flops 268435456 | bytes 262144 | tf_op jit(solution)/shard_map/pallas_call | solution.py:329
  168.6 8.2 %collective-permute-done.9 = bf16[128,2048]{1,0:T(8,128)(2,1)S(1)} collective-permute-done((bf16[128,2048]{1,0:T(8,128)(2,1)S(1)}, bf16[128,2048]{1,0:T(8,128)(2,1)S(1)}, u32[]{:S(2)}, u32[]{:S(2)}) %collective-permute-start.9) | collective-permute-done | bytes 524320 | tf_op jit(solution)/shard_map/ppermute | solution.py:45
  181.9 8.4 %all-to-all-start.3 = ((bf16[4,512,256]{2,1,0:T(8,128)(2,1)}), bf16[4,512,256]{2,1,0:T(8,128)(2,1)S(1)}, u32[]{:S(2)}, u32[]{:S(2)}) async-start(bf16[4,512,256]{2,1,0:T(8,128)(2,1)} %bitcast.245), calls=%async_computation.3 | async-start | bytes 2097152 | tf_op jit(solution)/shard_map/all_to_all | solution.py:67
  192.4 10.0 %collective-permute-done.10.refs_1_.refs_3_ = bf16[1024,512]{1,0:T(8,128)(2,1)} collective-permute-done((bf16[1024,512]{1,0:T(8,128)(2,1)}, bf16[1024,512]{1,0:T(8,128)(2,1)}, u32[]{:S(2)}, u32[]{:S(2)}) %collective-permute-start.10) | collective-permute-done | bytes 1048608 | tf_op jit(solution)/shard_map/ppermute | solution.py:45
  213.6 12.6 %collective-permute-done.14.refs_6_.refs_8_ = bf16[1024,512]{1,0:T(8,128)(2,1)} collective-permute-done((bf16[1024,512]{1,0:T(8,128)(2,1)S(1)}, bf16[1024,512]{1,0:T(8,128)(2,1)}, u32[]{:S(2)}, u32[]{:S(2)}) %collective-permute-start.14) | collective-permute-done | bytes 1048608 | tf_op jit(solution)/shard_map/ppermute | solution.py:45
  226.2 14.4 %all-to-all-done.3.refs_0_ = bf16[4,512,256]{2,1,0:T(8,128)(2,1)S(1)} async-done(((bf16[4,512,256]{2,1,0:T(8,128)(2,1)}), bf16[4,512,256]{2,1,0:T(8,128)(2,1)S(1)}, u32[]{:S(2)}, u32[]{:S(2)}) %all-to-all-start.3) | async-done | bytes 1048608 | tf_op jit(solution)/shard_map/all_to_all | solution.py:67
  243.1 20.6 %collective-permute-done.12.refs_3_.refs_5_ = bf16[1024,512]{1,0:T(8,128)(2,1)} collective-permute-done((bf16[1024,512]{1,0:T(8,128)(2,1)}, bf16[1024,512]{1,0:T(8,128)(2,1)}, u32[]{:S(2)}, u32[]{:S(2)}) %collective-permute-start.12) | collective-permute-done | bytes 1048608 | tf_op jit(solution)/shard_map/ppermute | solution.py:45
  266.1 15.7 %shard_map.209 = (bf16[1024,1024]{1,0:T(8,128)(2,1)}, f32[1024,1024]{1,0:T(8,128)}, f32[1024,1024]{1,0:T(8,128)}) custom-call(bf16[1024,2048]{1,0:T(8,128)(2,1)} %all-gather.8.cloned.1.call-done.rows, bf16[1024,512]{1,0:T(8,128)(2,1)} %bitcast.33.refs_0_.refs_2_, bf16[1024,512]{1,0:T(8,128)(2,1)} %collective-permute-done.10.refs_1_.refs_3_, ...), custom_call_target="tpu_custom_call" | custom-call | flops 268435456 | bytes 262144 | tf_op jit(solution)/shard_map/pallas_call | solution.py:468
  289.9 8.6 %collective-permute-done.18 = bf16[2,512,256]{2,1,0:T(8,128)(2,1)S(1)} collective-permute-done((bf16[2,512,256]{2,1,0:T(8,128)(2,1)S(1)}, bf16[2,512,256]{2,1,0:T(8,128)(2,1)S(1)}, u32[]{:S(2)}, u32[]{:S(2)}) %collective-permute-start.18) | collective-permute-done | bytes 524320 | tf_op jit(solution)/shard_map/ppermute | solution.py:45
  299.7 10.2 %shard_map.210 = bf16[1024,2048]{1,0:T(8,128)(2,1)} custom-call(bf16[1024,1024]{1,0:T(8,128)(2,1)} %get-tuple-element.198.acts, bf16[4,512,256]{2,1,0:T(8,128)(2,1)} %copy-done.5, bf16[4,512,256]{2,1,0:T(8,128)(2,1)} %copy-done.12, bf16[4,512,256]{2,1,0:T(8,128)(2,1)} %copy-done.11, bf16[4,512,256]{2,1,0:T(8,128)(2,1)} %copy-done.13), custom_call_target="tpu_custom_call" | custom-call | flops 268435456 | bytes 262144 | tf_op jit(solution)/shard_map/pallas_call | solution.py:468
  310.4 11.6 %shard_map.211 = (bf16[1024,1024]{1,0:T(8,128)(2,1)}, bf16[1024,1024]{1,0:T(8,128)(2,1)}) custom-call(bf16[1024,2048]{1,0:T(8,128)(2,1)} %all-gather.10.cloned.1.call-done.grads, bf16[4,512,256]{2,1,0:T(8,128)(2,1)} %copy-done.5, bf16[4,512,256]{2,1,0:T(8,128)(2,1)} %copy-done.12, bf16[4,512,256]{2,1,0:T(8,128)(2,1)} %copy-done.11, ...), custom_call_target="tpu_custom_call" | custom-call | flops 268435456 | bytes 262144 | tf_op jit(solution)/shard_map/pallas_call | solution.py:468
  335.3 15.1 %shard_map.212 = bf16[1024,2048]{1,0:T(8,128)(2,1)} custom-call(bf16[1024,1024]{1,0:T(8,128)(2,1)} %get-tuple-element.210.refs_0_, bf16[1024,1024]{1,0:T(8,128)(2,1)} %get-tuple-element.209.refs_1_, bf16[1024,512]{1,0:T(8,128)(2,1)} %bitcast.33.refs_0_.refs_2_, bf16[1024,512]{1,0:T(8,128)(2,1)} %collective-permute-done.10.refs_1_.refs_3_, ...), custom_call_target="tpu_custom_call" | custom-call | flops 268435456 | bytes 262144 | tf_op jit(solution)/shard_map/pallas_call | solution.py:468
  357.8 16.3 %collective-permute-done.22 = bf16[1024,512]{1,0:T(8,128)(2,1)S(1)} collective-permute-done((bf16[1024,512]{1,0:T(8,128)(2,1)}, bf16[1024,512]{1,0:T(8,128)(2,1)S(1)}, u32[]{:S(2)}, u32[]{:S(2)}) %collective-permute-start.22) | collective-permute-done | bytes 1048608 | tf_op jit(solution)/shard_map/ppermute | solution.py:45
  387.5 11.3 %collective-permute-done.23 = bf16[1024,512]{1,0:T(8,128)(2,1)S(1)} collective-permute-done((bf16[1024,512]{1,0:T(8,128)(2,1)S(1)}, bf16[1024,512]{1,0:T(8,128)(2,1)S(1)}, u32[]{:S(2)}, u32[]{:S(2)}) %collective-permute-start.23) | collective-permute-done | bytes 1048608 | tf_op jit(solution)/shard_map/ppermute | solution.py:45
  416.8 9.7 %collective-permute-done.27 = bf16[1024,512]{1,0:T(8,128)(2,1)} collective-permute-done((bf16[1024,512]{1,0:T(8,128)(2,1)}, bf16[1024,512]{1,0:T(8,128)(2,1)}, u32[]{:S(2)}, u32[]{:S(2)}) %collective-permute-start.27) | collective-permute-done | bytes 1048608 | tf_op jit(solution)/shard_map/ppermute | solution.py:45
  462.3 15.2 %shard_map.214 = (bf16[512,256]{1,0:T(8,128)(2,1)}, f32[16,128,256]{2,1,0:T(8,128)}) custom-call(s32[16]{0:T(128)} %parents.7, s32[2]{0:T(128)} %copy-done.69, bf16[512,256]{1,0:T(8,128)(2,1)} %copy-done.45, bf16[512,256]{1,0:T(8,128)(2,1)} %copy-done.60, f32[512,256]{1,0:T(8,128)} %get-tuple-element.242.attended, f32[2,1024,1]{2,1,0:T(8,128)} %get-tuple-element.243.stats, ...), custom_call_target="tpu_custom_call" | custom-call | flops 268435456 | bytes 262144 | tf_op jit(solution)/shard_map/pallas_call | solution.py:354
  490.7 10.7 %shard_map.215 = (bf16[512,256]{1,0:T(8,128)(2,1)}, bf16[16,128,256]{2,1,0:T(8,128)(2,1)}) custom-call(s32[16]{0:T(128)} %parents.7, s32[2]{0:T(128)} %copy-done.68, bf16[512,256]{1,0:T(8,128)(2,1)} %get-tuple-element.169.queries, bf16[512,256]{1,0:T(8,128)(2,1)} %get-tuple-element.236.grads, f32[512,256]{1,0:T(8,128)} %get-tuple-element.237.attended, ...), custom_call_target="tpu_custom_call" | custom-call | flops 268435456 | bytes 262144 | tf_op jit(solution)/shard_map/pallas_call | solution.py:354
  529.1 13.3 %collective-permute-done.34 = bf16[1024,512]{1,0:T(8,128)(2,1)} collective-permute-done((bf16[1024,512]{1,0:T(8,128)(2,1)}, bf16[1024,512]{1,0:T(8,128)(2,1)}, u32[]{:S(2)}, u32[]{:S(2)}) %collective-permute-start.34) | collective-permute-done | bytes 1048608 | tf_op jit(solution)/shard_map/ppermute | solution.py:45
  568.1 21.9 %all-to-all-done.6 = bf16[4,256,512]{2,1,0:T(8,128)(2,1)} async-done(((bf16[4,256,512]{2,1,0:T(8,128)(2,1)}), bf16[4,256,512]{2,1,0:T(8,128)(2,1)}, u32[]{:S(2)}, u32[]{:S(2)}) %all-to-all-start.6) | async-done | bytes 1048608 | tf_op jit(solution)/shard_map/all_to_all | solution.py:67
  623.3 11.2 %collective-permute-done.40 = bf16[256,256]{1,0:T(8,128)(2,1)S(1)} collective-permute-done((bf16[256,256]{1,0:T(8,128)(2,1)S(1)}, bf16[256,256]{1,0:T(8,128)(2,1)S(1)}, u32[]{:S(2)}, u32[]{:S(2)}) %collective-permute-start.40) | collective-permute-done | bytes 131104 | tf_op jit(solution)/shard_map/ppermute | solution.py:45
  (441 shorter events, 353.0 us)
Async XLA Ops:
  18.9 36.1 %all-gather.6.cloned.1.call-start = ((), (), s32[]{:S(2)}) async-start(), calls=%async_computation.12 | async-start | bytes 1310720 | tf_op jit(solution)/shard_map/all_gather | solution.py:742
  19.6 85.8 %all-gather.12.cloned.1.call-start = ((), (), s32[]{:S(2)}) async-start(), calls=%async_computation.19 | async-start | bytes 1310720 | tf_op jit(solution)/shard_map/all_gather | solution.py:745
  68.2 40.5 %all-to-all-start.1 = ((bf16[4,2,512,128]{3,2,1,0:T(8,128)(2,1)}), bf16[4,2,512,128]{3,2,1,0:T(8,128)(2,1)S(1)}, u32[]{:S(2)}, u32[]{:S(2)}) async-start(bf16[4,2,512,128]{3,2,1,0:T(8,128)(2,1)} %broadcast_in_dim.81), calls=%async_computation.1 | async-start | bytes 2097152 | tf_op jit(solution)/shard_map/all_to_all | solution.py:63
  110.2 52.6 %all-to-all-start.2 = ((bf16[4,2,256,512]{3,2,1,0:T(8,128)(2,1)}), bf16[4,2,256,512]{3,2,1,0:T(8,128)(2,1)}, u32[]{:S(2)}, u32[]{:S(2)}) async-start(bf16[4,2,256,512]{3,2,1,0:T(8,128)(2,1)} %shard_map.204), calls=%async_computation.2 | async-start | bytes 4194304 | tf_op jit(solution)/shard_map/all_to_all | solution.py:67
  114.8 151.0 %all-gather.8.cloned.1.call-start = ((), (), s32[]{:S(2)}) async-start(), calls=%async_computation.13 | async-start | bytes 4718592 | tf_op jit(solution)/shard_map/all_gather | solution.py:822
  115.1 30.0 %collective-permute-start.7 = (bf16[4,512,256]{2,1,0:T(8,128)(2,1)S(1)}, bf16[4,512,256]{2,1,0:T(8,128)(2,1)S(1)}, u32[]{:S(2)}, u32[]{:S(2)}) collective-permute-start(bf16[4,512,256]{2,1,0:T(8,128)(2,1)S(1)} %bitcast.223), channel_id=1, source_target_pairs={{0,4},{4,0},{1,5},{5,1},{2,6},{6,2},{3,7},{7,3},{8,12},{12,8},{9,1... | collective-permute-start | bytes 3145736 | tf_op jit(solution)/shard_map/ppermute | solution.py:45
  180.5 26.4 %collective-permute-start.11 = (bf16[1024,512]{1,0:T(8,128)(2,1)}, bf16[1024,512]{1,0:T(8,128)(2,1)}, u32[]{:S(2)}, u32[]{:S(2)}) collective-permute-start(bf16[1024,512]{1,0:T(8,128)(2,1)} %bitcast.33.refs_0_.refs_2_), channel_id=1, source_target_pairs={{0,4},{4,0},{1,5},{5,1},{2,6},{6,2},{3,7},{7,3},{8,12},{12,8},{9,1... | collective-permute-start | bytes 3145736 | tf_op jit(solution)/shard_map/ppermute | solution.py:45
  181.9 58.6 %all-to-all-start.3 = ((bf16[4,512,256]{2,1,0:T(8,128)(2,1)}), bf16[4,512,256]{2,1,0:T(8,128)(2,1)S(1)}, u32[]{:S(2)}, u32[]{:S(2)}) async-start(bf16[4,512,256]{2,1,0:T(8,128)(2,1)} %bitcast.245), calls=%async_computation.3 | async-start | bytes 2097152 | tf_op jit(solution)/shard_map/all_to_all | solution.py:67
  190.3 119.6 %all-gather.10.cloned.1.call-start = ((), (), s32[]{:S(2)}) async-start(), calls=%async_computation.14 | async-start | bytes 4718592 | tf_op jit(solution)/shard_map/all_gather | solution.py:829
  190.3 35.8 %collective-permute-start.14 = (bf16[1024,512]{1,0:T(8,128)(2,1)S(1)}, bf16[1024,512]{1,0:T(8,128)(2,1)}, u32[]{:S(2)}, u32[]{:S(2)}) collective-permute-start(bf16[1024,512]{1,0:T(8,128)(2,1)S(1)} %bitcast.206), channel_id=1, source_target_pairs={{0,4},{4,0},{1,5},{5,1},{2,6},{6,2},{3,7},{7,3},{8,12},{12,8},{9,1... | collective-permute-start | bytes 3145736 | tf_op jit(solution)/shard_map/ppermute | solution.py:45
  240.6 169.9 %reduce-scatter.7.cloned.1.call-start = ((), (), s32[]{:S(2)}) async-start(), calls=%async_computation.16 | async-start | bytes 4718592 | tf_op jit(solution)/shard_map/reduce_scatter | solution.py:844
  310.0 100.6 %reduce-scatter.5.cloned.1.call-start = ((), (), s32[]{:S(2)}) async-start(), calls=%async_computation.15 | async-start | bytes 4718592 | tf_op jit(solution)/shard_map/reduce_scatter | solution.py:862
  324.3 26.0 %collective-permute-start.20 = (bf16[1024,512]{1,0:T(8,128)(2,1)}, bf16[1024,512]{1,0:T(8,128)(2,1)}, u32[]{:S(2)}, u32[]{:S(2)}) collective-permute-start(bf16[1024,512]{1,0:T(8,128)(2,1)} %fusion.18), channel_id=1, source_target_pairs={{0,4},{4,0},{1,5},{5,1},{2,6},{6,2},{3,7},{7,3},{8,12},{12,8},{9,1... | collective-permute-start | bytes 3145736 | tf_op jit(solution)/shard_map/ppermute | solution.py:45
  380.3 26.2 %collective-permute-start.24 = (bf16[1024,512]{1,0:T(8,128)(2,1)S(1)}, bf16[1024,512]{1,0:T(8,128)(2,1)S(1)}, u32[]{:S(2)}, u32[]{:S(2)}) collective-permute-start(bf16[1024,512]{1,0:T(8,128)(2,1)S(1)} %copy-done.78), channel_id=1, source_target_pairs={{0,2},{2,0},{1,3},{3,1},{4,6},{6,4},{5,7},{7,5},{8,10},{10,8},{9,1... | collective-permute-start | bytes 3145736 | tf_op jit(solution)/shard_map/ppermute | solution.py:45
  387.5 39.0 %collective-permute-start.27 = (bf16[1024,512]{1,0:T(8,128)(2,1)}, bf16[1024,512]{1,0:T(8,128)(2,1)}, u32[]{:S(2)}, u32[]{:S(2)}) collective-permute-start(bf16[1024,512]{1,0:T(8,128)(2,1)} %add_convert_fusion.7), channel_id=1, source_target_pairs={{0,2},{2,0},{1,3},{3,1},{4,6},{6,4},{5,7},{7,5},{8,10},{10,8},{9,1... | collective-permute-start | bytes 3145736 | tf_op jit(solution)/shard_map/ppermute | solution.py:45
  433.2 76.5 %all-to-all-start.4 = ((bf16[4,2,256,512]{3,2,1,0:T(8,128)(2,1)}), bf16[4,2,256,512]{3,2,1,0:T(8,128)(2,1)}, u32[]{:S(2)}, u32[]{:S(2)}) async-start(bf16[4,2,256,512]{3,2,1,0:T(8,128)(2,1)} %pad_maximum_fusion), calls=%async_computation.6 | async-start | bytes 4194304 | tf_op jit(solution)/shard_map/all_to_all | solution.py:67
  456.3 26.4 %collective-permute-start.30 = (bf16[1024,512]{1,0:T(8,128)(2,1)}, bf16[1024,512]{1,0:T(8,128)(2,1)}, u32[]{:S(2)}, u32[]{:S(2)}) collective-permute-start(bf16[1024,512]{1,0:T(8,128)(2,1)} %convolution_convert_fusion.5), channel_id=1, source_target_pairs={{0,4},{4,0},{1,5},{5,1},{2,6},{6,2},{3,7},{7,3},{8,12},{12,8},{9,1... | collective-permute-start | bytes 3145736 | tf_op jit(solution)/shard_map/ppermute | solution.py:45
  457.8 47.4 %collective-permute-start.32 = (bf16[1024,512]{1,0:T(8,128)(2,1)}, bf16[1024,512]{1,0:T(8,128)(2,1)}, u32[]{:S(2)}, u32[]{:S(2)}) collective-permute-start(bf16[1024,512]{1,0:T(8,128)(2,1)} %add_convert_fusion.6), channel_id=1, source_target_pairs={{0,4},{4,0},{1,5},{5,1},{2,6},{6,2},{3,7},{7,3},{8,12},{12,8},{9,1... | collective-permute-start | bytes 3145736 | tf_op jit(solution)/shard_map/ppermute | solution.py:45
  458.4 46.8 %collective-permute-start.33 = (bf16[1024,512]{1,0:T(8,128)(2,1)}, bf16[1024,512]{1,0:T(8,128)(2,1)}, u32[]{:S(2)}, u32[]{:S(2)}) collective-permute-start(bf16[1024,512]{1,0:T(8,128)(2,1)} %convolution_convert_fusion.1), channel_id=1, source_target_pairs={{0,2},{2,0},{1,3},{3,1},{4,6},{6,4},{5,7},{7,5},{8,10},{10,8},{9,1... | collective-permute-start | bytes 3145736 | tf_op jit(solution)/shard_map/ppermute | solution.py:45
  509.6 32.8 %all-to-all-start.5 = ((bf16[4,4,128,256]{3,2,1,0:T(8,128)(2,1)}), bf16[4,4,128,256]{3,2,1,0:T(8,128)(2,1)}, u32[]{:S(2)}, u32[]{:S(2)}) async-start(bf16[4,4,128,256]{3,2,1,0:T(8,128)(2,1)} %bitcast.246), calls=%async_computation.7 | async-start | bytes 2097152 | tf_op jit(solution)/shard_map/all_to_all | solution.py:67
  547.5 42.5 %all-to-all-start.6 = ((bf16[4,256,512]{2,1,0:T(8,128)(2,1)}), bf16[4,256,512]{2,1,0:T(8,128)(2,1)}, u32[]{:S(2)}, u32[]{:S(2)}) async-start(bf16[4,256,512]{2,1,0:T(8,128)(2,1)} %bitcast.220), calls=%async_computation.8 | async-start | bytes 2097152 | tf_op jit(solution)/shard_map/all_to_all | solution.py:67
  552.3 65.5 %reduce-scatter.11.cloned.1.call-start = ((), (), s32[]{:S(2)}) async-start(), calls=%async_computation.18 | async-start | bytes 1310720 | tf_op jit(solution)/shard_map/reduce_scatter | solution.py:907
  560.1 74.4 %reduce-scatter.9.cloned.1.call-start = ((), (), s32[]{:S(2)}) async-start(), calls=%async_computation.17 | async-start | bytes 1310720 | tf_op jit(solution)/shard_map/reduce_scatter | solution.py:953
  563.7 35.5 %collective-permute-start.38 = (bf16[1024,256]{1,0:T(8,128)(2,1)}, bf16[1024,256]{1,0:T(8,128)(2,1)}, u32[]{:S(2)}, u32[]{:S(2)}) collective-permute-start(bf16[1024,256]{1,0:T(8,128)(2,1)} %convolution_convert_fusion.6), channel_id=1, source_target_pairs={{0,4},{4,0},{1,5},{5,1},{2,6},{6,2},{3,7},{7,3},{8,12},{12,8},{9,1... | collective-permute-start | bytes 1572872 | tf_op jit(solution)/shard_map/ppermute | solution.py:45
  (113 other events, 1447.6 us)
Sparse Core Ops, SparseCore 0:
  21.3 29.3 all-gather.5
  61.3 44.0 all-gather.11
  178.9 71.6 all-gather.7
  252.6 45.6 all-gather.9
  310.1 47.7 reduce-scatter.6
  360.0 48.1 reduce-scatter.4
  560.2 33.3 reduce-scatter.10
  596.9 33.3 reduce-scatter.8

commit v5 on v4

--- a/solution.py
+++ b/solution.py
@@ -185,23 +185,45 @@
     return [ref[:, at : at + LANES] for at in range(0, ref.shape[1], LANES)]
 
 
-def project_kernel(parts, rows, *refs):
+def key_tables(cosine, sine):
+    left = left_lanes(cosine.shape)
+    return jnp.where(left, cosine, 1.0), jnp.where(left, sine, 0.0)
+
+
+def settle_kernel(*refs):
+    count = len(refs) // 2
+    for value, out in zip(refs[:count], refs[count:]):
+        out[...] = value[...]
+
+
+def settled(*values):
+    return pl.pallas_call(
+        settle_kernel,
+        out_shape=[jax.ShapeDtypeStruct(v.shape, v.dtype) for v in values],
+        compiler_params=pltpu.CompilerParams(vmem_limit_bytes=KERNEL_VMEM),
+        cost_estimate=SMALL_COST,
+    )(*values)
+
+
+def project_kernel(parts, keys, rows, *refs):
     weights, (cosine, sine, out) = refs[:parts], refs[parts:]
     depth = weights[0].shape[0]
     product = sum(nn_dot(rows[:, i * depth : (i + 1) * depth], w[...]) for i, w in enumerate(weights))
     cos, sin = cosine[...], sine[...]
+    if keys:
+        cos, sin = key_tables(cos, sin)
     for at in range(0, product.shape[1], LANES):
         block = turned(product[:, at : at + LANES], cos, sin, 1.0)
         out[:, at : at + LANES] = block.astype(jnp.bfloat16)
 
 
-def project(rows, weights, cosine, sine):
+def project(rows, weights, cosine, sine, keys=False):
     count, width = rows.shape
     depth, cols = weights[0].shape
     step = 2 * LANES
     table = pl.BlockSpec((count, LANES), lambda j: (0, 0))
     return pl.pallas_call(
-        functools.partial(project_kernel, len(weights)),
+        functools.partial(project_kernel, len(weights), keys),
         grid=(cols // step,),
         in_specs=[pl.BlockSpec((count, width), lambda j: (0, 0))]
         + [pl.BlockSpec((depth, step), lambda j: (0, j))] * len(weights)
@@ -343,9 +365,10 @@
 
 
 def attend_back(
-    parents, segs, queries, grads, attended, stats, cosine, sine, keys_values, earlier=None
+    parents, segs, queries, grads, attended, stats, cosine, sine, place, keys_values, earlier=None
 ):
     count, cols = queries.shape
+    first = place * (count // SEG)
     seg_total = keys_values.shape[0]
     block, table, whole, rows, stat, scalar = attention_specs(cols, seg_total)
     sums = pl.BlockSpec((seg_total, LANES, SEG), lambda s: (0, 0, 0))
@@ -354,7 +377,10 @@
     return pl.pallas_call(
         attend_back_kernel,
         grid=(count // SEG,),
-        in_specs=[scalar, scalar, block, block, block, stat, table, table, whole] + [sums] * last,
+        in_specs=[scalar, scalar, block, block, block, stat]
+        + [pl.BlockSpec((SEG, LANES), lambda s: (first + s, 0))] * 2
+        + [whole]
+        + [sums] * last,
         out_specs=[block, sums],
         out_shape=[
             jax.ShapeDtypeStruct((count, cols), jnp.bfloat16),
@@ -579,6 +605,36 @@
     )(*values)
 
 
+def finish_kernel(pair, single, first, second, third):
+    first[...] = pair[0, 0].astype(jnp.float32)
+    second[...] = pair[0, 1].astype(jnp.float32).T
+    third[...] = single[0].astype(jnp.float32)
+
+
+def finished(pair, single):
+    count, _, rows, cols = pair.shape
+    if cols % LANES or rows % LANES:
+        first, second, third = (joined_columns(v) for v in (pair[:, 0], pair[:, 1], single))
+        return [v.astype(jnp.float32) for v in (first, second.T, third)]
+    side = pl.BlockSpec((rows, cols), lambda z: (0, z))
+    return pl.pallas_call(
+        finish_kernel,
+        grid=(count,),
+        in_specs=[
+            pl.BlockSpec((1, 2, rows, cols), lambda z: (z, 0, 0, 0)),
+            pl.BlockSpec((1, rows, cols), lambda z: (z, 0, 0)),
+        ],
+        out_specs=[side, pl.BlockSpec((cols, rows), lambda z: (z, 0)), side],
+        out_shape=[
+            jax.ShapeDtypeStruct((rows, count * cols), jnp.float32),
+            jax.ShapeDtypeStruct((count * cols, rows), jnp.float32),
+            jax.ShapeDtypeStruct((rows, count * cols), jnp.float32),
+        ],
+        compiler_params=pltpu.CompilerParams(vmem_limit_bytes=KERNEL_VMEM),
+        cost_estimate=SMALL_COST,
+    )(pair, single)
+
+
 def row_norm(value):
     inverse = lax.rsqrt(jnp.mean(value * value, axis=-1, keepdims=True) + norm_eps)
     return value * inverse, inverse
@@ -655,7 +711,8 @@
 
 def turned_sum_kernel(blocks, cosine, sine, out):
     total = sum(blocks[i, 0].astype(jnp.float32) for i in range(blocks.shape[0]))
-    out[...] = turned(total.T, cosine[...], sine[...], -1.0).astype(jnp.bfloat16)
+    cos, sin = key_tables(cosine[...], sine[...])
+    out[...] = turned(total.T, cos, sin, -1.0).astype(jnp.bfloat16)
 
 
 def turned_sum(blocks, cosine, sine):
@@ -760,11 +817,11 @@
     cosine_table, sine_table = rope_tables(position, HEAD_SIZE)
     cosine_lanes = jnp.tile(cosine_table, (1, 4))
     sine_lanes = jnp.tile(sine_table, (1, 4))
-    key_lanes = jnp.arange(LANES) < HEAD_SIZE
-    cosine_keys = jnp.where(key_lanes, cosine_lanes[:group_rows], 1.0)
-    sine_keys = jnp.where(key_lanes, sine_lanes[:group_rows], 0.0)
+    ordered = [jnp.concatenate(in_order(jnp.split(v, y_size))) for v in (cosine_lanes, sine_lanes)]
+    cosine_lanes, sine_lanes, *ordered = settled(cosine_lanes, sine_lanes, *ordered)
 
     kv_zy = relative_pieces(kv_z, "y")
+    kv_zy, cosine_lanes, sine_lanes, ordered = together(kv_zy, cosine_lanes, sine_lanes, ordered)
     kv_weights = [v[:, :own_width].reshape(-1, 2 * kv_cols) for v in kv_zy]
     gains = [
         v[:, own_width:].reshape(z_size, -1)[:, : 2 * own_width].reshape(z_size, 2, own_width)
@@ -778,21 +835,14 @@
     rows_one = (group_normed * gain_one).astype(low)
     rows_one, q_z = together(rows_one, q_z)
     q_weights = relative_pieces(q_z, "y")
-    kv_rows = project(rows_one, kv_weights, cosine_keys, sine_keys)
+    kv_rows = project(rows_one, kv_weights, cosine_lanes, sine_lanes, keys=True)
     kv_swapped = jnp.stack(natural_pieces(sent_groups(kv_rows), "y"))
     all_kv = gathered(kv_swapped, "z").reshape(-1, SEG, LANES)
     wide_blocks = split_columns(after((gate_weight, up_weight), kv_z), z_size)
     q_weights, wide_blocks = together(q_weights, wide_blocks)
-    query_rows = project(rows_one, q_weights, cosine_lanes[:group_rows], sine_lanes[:group_rows])
+    query_rows = project(rows_one, q_weights, cosine_lanes, sine_lanes)
     queries = sent_groups(query_rows)
-    tables = [jnp.split(v, y_size) for v in (cosine_lanes, sine_lanes)]
-    key_tables = [
-        jnp.concatenate(in_order(jnp.split(v, y_size)))
-        for v in (jnp.where(key_lanes, cosine_lanes, 1.0), jnp.where(key_lanes, sine_lanes, 0.0))
-    ]
-    all_kv, queries, o_z, wide_blocks, tables, key_tables = together(
-        all_kv, queries, o_z, wide_blocks, tables, key_tables
-    )
+    all_kv, queries, o_z, wide_blocks = together(all_kv, queries, o_z, wide_blocks)
 
     wide_z = exchanged(wide_blocks, "z")
     o_weights = relative_pieces(o_z, "y")
@@ -863,14 +913,15 @@
     gate_far, up_far, acts = together(gate_far, up_far, acts)
     down_near = summed_pieces([turned_matmul(a, acts[0]) for a in grad_parts], "y")
     down_far = [rotated(v, "x", -1 - i) for i, v in enumerate(down_far)]
-    down_near, down_far, gate_parts = together(down_near, down_far, gate_parts)
+    down_near, down_far, mlp_mine = together(down_near, down_far, mlp_mine)
+    mixed = natural_columns((middle + branch_scale * mlp_mine.astype(jnp.float32)).astype(low))
     grad_down_z = sum([v.astype(jnp.float32) for v in down_far], down_near).astype(low)
     gate_near = summed_pieces([turned_matmul(a, gate_parts[0]) for a in rows_parts], "y")
     gate_far = [rotated(v, "x", -1 - i) for i, v in enumerate(gate_far)]
     up_near = [turned_matmul(rows_parts[0], b) for b in up_parts]
     up_near[1:] = [v.astype(low) for v in up_near[1:]]
-    grad_rows_two, mlp_mine, up_far, up_near, grad_down_z = together(
-        grad_rows_two, mlp_mine, up_far, up_near, grad_down_z
+    grad_rows_two, mixed, up_far, up_near, grad_down_z = together(
+        grad_rows_two, mixed, up_far, up_near, grad_down_z
     )
     grad_rows_two = grad_rows_two.astype(jnp.float32)
     gain_two_part = jnp.sum(grad_rows_two * normed_two, axis=0)
@@ -881,10 +932,12 @@
     grad_gate_z = sum([v.astype(jnp.float32) for v in gate_far], gate_near).astype(low)
     wide_z = jnp.stack([v.reshape(z_size, own_width, -1) for v in (grad_gate_z, grad_down_z)], 1)
     attn_x, wide_z, up_near = together(attn_x, wide_z, up_near)
-    wide_z = exchanged(wide_z, "z")
     grad_attn_rows = gathered_core(attn_x)
     grad_heads = o_backward(grad_attn_rows, o_weights)
-    grad_heads, grad_attn_rows, up_near = together(grad_heads, grad_attn_rows, up_near)
+    grad_heads, grad_attn_rows, up_near, wide_z = together(
+        grad_heads, grad_attn_rows, up_near, wide_z
+    )
+    wide_z = exchanged(wide_z, "z")
 
     grad_heads = sent_groups(grad_heads)
     o_dots = [turned_matmul(v, attn_low) for v in halves(grad_attn_rows, y_size)[1:]]
@@ -894,12 +947,11 @@
     )
     o_sent = [rotated(v, "y", -1 - i) for i, v in enumerate(o_dots)]
     up_mine = [rotated(v, "x", -1 - i) for i, v in enumerate(up_near[1:])]
-    cosines, sines = tables
     grad_queries, sums = [None] * y_size, None
     for k in range(y_size - 1, 0, -1):
         grad_queries[k], sums = attend_back(
-            parents, seg_lists[k], queries[k], grad_heads[k], *attends[k], cosines[k], sines[k],
-            all_kv, sums,
+            parents, seg_lists[k], queries[k], grad_heads[k], *attends[k], cosine_lanes,
+            sine_lanes, k, all_kv, sums,
         )
     grad_o_y = turned_matmul(halves(grad_attn_rows, y_size)[0], attn_low)
     grad_o_y = sum([v.astype(jnp.float32) for v in o_sent], grad_o_y).astype(low)
@@ -907,11 +959,12 @@
     grad_o = lax.psum_scatter(grad_o_y, "z", scatter_dimension=0, tiled=True)
     returned = [rotated(v, "y", -k) for k, v in enumerate(grad_queries[1:], 1)]
     grad_queries[0], grad_kv = attend_back(
-        parents, seg_lists[0], queries[0], grad_heads[0], *attends[0], cosines[0], sines[0],
-        all_kv, sums,
-    )
-    grad_queries[0], grad_kv, returned, up_far, up_mine, up_near, wide_z = together(
-        grad_queries[0], grad_kv, returned, up_far, up_mine, up_near, wide_z
+        parents, seg_lists[0], queries[0], grad_heads[0], *attends[0], cosine_lanes, sine_lanes,
+        0, all_kv, sums,
+    )
+    grad_kv, wide_z = together(grad_kv, wide_z)
+    grad_queries[0], returned, up_far, up_mine, up_near = after(
+        (grad_queries[0], returned, up_far, up_mine, up_near), grad_kv
     )
 
     def owned_dots(left, right):
@@ -931,12 +984,12 @@
     q_full = jnp.concatenate(q_weights, axis=0)
     query_part = matmul_turned(grad_queries, q_full)
     grad_up_z = total(up_near[0], up_far + up_mine)
-    kv_mine, query_part, query_dots, query_sent, grad_up_z = together(
-        kv_mine, query_part, query_dots, query_sent, grad_up_z
+    kv_mine, query_part, query_dots, query_sent, grad_up_z, grad_o = together(
+        kv_mine, query_part, query_dots, query_sent, grad_up_z, grad_o
     )
 
     grad_up = exchanged(grad_up_z.reshape(z_size, own_width, -1), "z")
-    kv_mine = turned_sum(kv_mine, *key_tables).reshape(y_size, group_rows, LANES)
+    kv_mine = turned_sum(kv_mine, *ordered).reshape(y_size, group_rows, LANES)
     kv_mine = own_first(kv_mine, "y")
     grad_kv_rows = in_groups(
         [kv_mine[0]] + [rotated(v, "y", -k) for k, v in enumerate(kv_mine[1:], 1)]
@@ -944,41 +997,38 @@
     kv_full = jnp.concatenate(kv_weights, axis=0)
     input_one = (query_part + matmul_turned(grad_kv_rows, kv_full)).astype(low)
     input_core = core_sum(input_one, local_rows)
+    grad_q_y = total(query_dots[0], query_sent)
     kv_dots = owned_dots(rows_one, grad_kv_rows)
     kv_sent = sent_back(kv_dots)
-    input_core, query_sent, query_dots, grad_up = together(
-        input_core, query_sent, query_dots, grad_up
-    )
-    grad_q_y = total(query_dots[0], query_sent)
+    input_core, grad_q_y, grad_up, wide_z, grad_o = together(
+        input_core, grad_q_y, grad_up, wide_z, grad_o
+    )
     grad_q = lax.psum_scatter(grad_q_y, "z", scatter_dimension=0, tiled=True)
     input_x = x_blocks(input_core)
     input_sent = [rotated(v, "x", -1 - i) for i, v in enumerate(input_x[1:])]
-    input_x[0], input_sent, kv_sent, kv_dots, mlp_mine = together(
-        input_x[0], input_sent, kv_sent, kv_dots, mlp_mine
+    input_x[0], input_sent, kv_sent, kv_dots, wide_z, grad_up, grad_o = together(
+        input_x[0], input_sent, kv_sent, kv_dots, wide_z, grad_up, grad_o
     )
     grad_rows_one = sum([v.astype(jnp.float32) for v in input_sent], input_x[0].astype(jnp.float32))
     kv_blocks = own_first(total(kv_dots[0], kv_sent).reshape(z_size, own_width, -1), "z")
     kv_sent = [rotated(v, "z", -1 - i) for i, v in enumerate(kv_blocks[1:])]
     gain_one_part = jnp.sum(grad_rows_one * normed_one, axis=0)
     grad_inputs = grad_middle + norm_back(grad_rows_one, normed_one, inv_one, gain_one)
-    kv_sent, kv_blocks, grad_inputs, wide_z, grad_up, grad_q, grad_o, mlp_mine = together(
-        kv_sent, kv_blocks, grad_inputs, wide_z, grad_up, grad_q, grad_o, mlp_mine
-    )
-    mixed = natural_columns((middle + branch_scale * mlp_mine.astype(jnp.float32)).astype(low))
-    grad_tokens = natural_columns(grad_inputs.astype(low))
-    grad_kv_weight = sum([v.astype(jnp.float32) for v in kv_sent], kv_blocks[0].astype(jnp.float32))
-    grad_q, grad_o = grad_q.astype(jnp.float32), grad_o.astype(jnp.float32).T
-    grad_gate, grad_down, grad_up = (
-        joined_columns(v).astype(jnp.float32) for v in (wide_z[:, 0], wide_z[:, 1], grad_up)
-    )
-    grad_down = grad_down.T
-
     gain_parts = jnp.stack([gain_one_part, gain_two_part], axis=0)
     gain_parts = natural_columns(gain_parts).reshape(2, z_size * y_size, 1, own_width)
     gain_parts = jnp.broadcast_to(
         gain_parts, (2, z_size * y_size, tensor_size, own_width)
     ).reshape(2, -1, own_width).transpose(1, 0, 2)
-    gain_sums = jnp.sum(exchanged(gain_parts, ("z", "y", "x", "c")), axis=0)
+    gain_parts = exchanged(gain_parts, ("z", "y", "x", "c"))
+    grad_tokens = natural_columns(grad_inputs.astype(low))
+    gain_parts, kv_sent, kv_blocks, wide_z, grad_up, grad_o, grad_tokens = together(
+        gain_parts, kv_sent, kv_blocks, wide_z, grad_up, grad_o, grad_tokens
+    )
+    gain_sums = jnp.sum(gain_parts, axis=0)
+    grad_gate, grad_down, grad_up = finished(wide_z, grad_up)
+    grad_o = grad_o.astype(jnp.float32).T
+    grad_kv_weight = sum([v.astype(jnp.float32) for v in kv_sent], kv_blocks[0].astype(jnp.float32))
+    grad_q = grad_q.astype(jnp.float32)
     grad_heads = halves(grad_kv_weight, 2 * kv_local)
     return (
         mixed,

time: 670 us -> 645 us (0.963)
  local copies, waits for them, and re-layouts: 66.1 us -> 43.7 us
    optimization_barrier x6 -> x2, local copies, waits for them, and re-layouts: 10.9 us -> 0.28 us  [together(): return lax.optimization_barrier(values)]
    ppermute x42, waiting for transfers between devices: 206 us -> 214 us  [rotated(): lax.ppermute(value, axis, [(i, (i + step) % size) for i in range(size)])]
    pallas_call x2 -> x4, Pallas kernels: 8.28 us -> 16.2 us  [the longest x2 8.26 us: project(): pl.pallas_call(functools.partial(project_kernel, len(weights), keys), gri...]
    all_gather x1, waiting for transfers between devices: 11.5 us -> 4.67 us  [local(): o_z = lax.all_gather(o_weight, 'z', axis=0)]
    unnamed x168 -> x128, local copies, waits for them, and re-layouts: 15.1 us -> 11.8 us
  transfers between devices with their start and end apart: 58 -> 58, of which waited for: 35 -> 37; matrix products, arithmetic and copies ran while one was open for 19% -> 20% of each run, Pallas kernels for 18% -> 18%
where the time goes in v5:
time: 645 us; the launch traced here: 635 us
  waiting for transfers between devices  268 us (42%)
  Pallas kernels  128 us (20%)
  starting transfers between devices  77.7 us (12%)
  other arithmetic  52.6 us (8%)
  matrix products  48.5 us (8%)
  local copies, waits for them, and re-layouts  43.7 us (7%)
  between operations  15.8 us (2%)
    ppermute x42, waiting for transfers between devices, rotated(): lax.ppermute(value, axis, [(i, (i + step) % size) for i in range(size)])  214 us
    pallas_call x4, Pallas kernels, wide_call(): pl.pallas_call(functools.partial(kernel, per, parts, pieces), grid=(count...  52.8 us
    all_to_all x7, waiting for transfers between devices, exchanged(): return lax.all_to_all(blocks, axis, 0, 0, tiled=True)  45.5 us
    dot_general x18, matrix products, turned_matmul(): lax.dot_general(left, right, (((0,), (0,)), ((), ())), preferred_element_...  40.7 us
    ppermute x42, starting transfers between devices, rotated(): lax.ppermute(value, axis, [(i, (i + step) % size) for i in range(size)])  37.3 us
    all_to_all x7, starting transfers between devices, exchanged(): return lax.all_to_all(blocks, axis, 0, 0, tiled=True)  35.8 us
    pallas_call x2, Pallas kernels, attend_back(): pl.pallas_call(attend_back_kernel, grid=(count // SEG,), in_specs=[scalar...  22.8 us
    pallas_call x2, Pallas kernels, attend(): pl.pallas_call(attend_kernel, grid=(steps,), in_specs=[scalar, scalar, bl...  18.6 us
  transfers between devices with their start and end apart: 58, of which 37 were waited for; matrix products, arithmetic and copies ran while one was open for 20% of the time, Pallas kernels for 18%

profile of v5, /device:TPU:0, one launch (start us, length us, event | category | flops | bytes accessed | tf_op | source)
XLA Modules:
  0.0 635.0 jit_solution(3492791689208523670)
XLA Ops:
  71.0 18.7 %collective-permute-done.4.refs_1_ = bf16[1024,512]{1,0:T(8,128)(2,1)} collective-permute-done((bf16[1024,512]{1,0:T(8,128)(2,1)S(1)}, bf16[1024,512]{1,0:T(8,128)(2,1)}, u32[]{:S(2)}, u32[]{:S(2)}) %collective-permute-start.4) | collective-permute-done | bytes 1048608 | tf_op jit(solution)/shard_map/ppermute | solution.py:45
  113.0 9.3 %shard_map.207 = (f32[512,256]{1,0:T(8,128)}, f32[2,1024,1]{2,1,0:T(8,128)}, bf16[512,256]{1,0:T(8,128)(2,1)}) custom-call(s32[16]{0:T(128)} %parents.7, s32[2]{0:T(128)} %copy-done.54, bf16[512,256]{1,0:T(8,128)(2,1)} %copy-done.37, bf16[16,256,128]{2,1,0:T(8,128)(2,1)} %bitcast.171), custom_call_target="tpu_custom_call" | custom-call | flops 268435456 | bytes 262144 | tf_op jit(solution)/shard_map/pallas_call | solution.py:351
  122.9 9.3 %shard_map.208 = (f32[512,256]{1,0:T(8,128)}, f32[2,1024,1]{2,1,0:T(8,128)}, bf16[512,256]{1,0:T(8,128)(2,1)}) custom-call(s32[16]{0:T(128)} %parents.7, s32[2]{0:T(128)} %copy-done.55, bf16[512,256]{1,0:T(8,128)(2,1)} %get-tuple-element.188.queries, bf16[16,256,128]{2,1,0:T(8,128)(2,1)} %bitcast.172), custom_call_target="tpu_custom_call" | custom-call | flops 268435456 | bytes 262144 | tf_op jit(solution)/shard_map/pallas_call | solution.py:351
  132.1 9.9 %collective-permute-done.6.refs_1_ = bf16[512,256]{1,0:T(8,128)(2,1)S(1)} collective-permute-done((bf16[512,256]{1,0:T(8,128)(2,1)}, bf16[512,256]{1,0:T(8,128)(2,1)S(1)}, u32[]{:S(2)}, u32[]{:S(2)}) %collective-permute-start.6) | collective-permute-done | bytes 262176 | tf_op jit(solution)/shard_map/ppermute | solution.py:45
  164.7 8.9 %collective-permute-done.9 = bf16[128,2048]{1,0:T(8,128)(2,1)S(1)} collective-permute-done((bf16[128,2048]{1,0:T(8,128)(2,1)}, bf16[128,2048]{1,0:T(8,128)(2,1)S(1)}, u32[]{:S(2)}, u32[]{:S(2)}) %collective-permute-start.9) | collective-permute-done | bytes 524320 | tf_op jit(solution)/shard_map/ppermute | solution.py:45
  178.6 7.0 %all-to-all-start.3 = ((bf16[4,512,256]{2,1,0:T(8,128)(2,1)}), bf16[4,512,256]{2,1,0:T(8,128)(2,1)S(1)}, u32[]{:S(2)}, u32[]{:S(2)}) async-start(bf16[4,512,256]{2,1,0:T(8,128)(2,1)} %bitcast.215), calls=%async_computation.3 | async-start | bytes 2097152 | tf_op jit(solution)/shard_map/all_to_all | solution.py:67
  185.6 13.4 %collective-permute-done.10.refs_1_.refs_3_ = bf16[1024,512]{1,0:T(8,128)(2,1)} collective-permute-done((bf16[1024,512]{1,0:T(8,128)(2,1)S(1)}, bf16[1024,512]{1,0:T(8,128)(2,1)}, u32[]{:S(2)}, u32[]{:S(2)}) %collective-permute-start.10) | collective-permute-done | bytes 1048608 | tf_op jit(solution)/shard_map/ppermute | solution.py:45
  207.5 15.2 %collective-permute-done.14.refs_6_.refs_8_ = bf16[1024,512]{1,0:T(8,128)(2,1)} collective-permute-done((bf16[1024,512]{1,0:T(8,128)(2,1)}, bf16[1024,512]{1,0:T(8,128)(2,1)}, u32[]{:S(2)}, u32[]{:S(2)}) %collective-permute-start.14) | collective-permute-done | bytes 1048608 | tf_op jit(solution)/shard_map/ppermute | solution.py:45
  222.7 13.2 %all-to-all-done.3.refs_0_ = bf16[4,512,256]{2,1,0:T(8,128)(2,1)S(1)} async-done(((bf16[4,512,256]{2,1,0:T(8,128)(2,1)}), bf16[4,512,256]{2,1,0:T(8,128)(2,1)S(1)}, u32[]{:S(2)}, u32[]{:S(2)}) %all-to-all-start.3) | async-done | bytes 1048608 | tf_op jit(solution)/shard_map/all_to_all | solution.py:67
  236.4 23.1 %collective-permute-done.12.refs_3_.refs_5_ = bf16[1024,512]{1,0:T(8,128)(2,1)} collective-permute-done((bf16[1024,512]{1,0:T(8,128)(2,1)}, bf16[1024,512]{1,0:T(8,128)(2,1)}, u32[]{:S(2)}, u32[]{:S(2)}) %collective-permute-start.12) | collective-permute-done | bytes 1048608 | tf_op jit(solution)/shard_map/ppermute | solution.py:45
  261.5 15.7 %shard_map.210 = (bf16[1024,1024]{1,0:T(8,128)(2,1)}, f32[1024,1024]{1,0:T(8,128)}, f32[1024,1024]{1,0:T(8,128)}) custom-call(bf16[1024,2048]{1,0:T(8,128)(2,1)} %all-gather.8.cloned.1.call-done.rows, bf16[1024,512]{1,0:T(8,128)(2,1)} %bitcast.177, bf16[1024,512]{1,0:T(8,128)(2,1)} %collective-permute-done.10.refs_1_.refs_3_, ...), custom_call_target="tpu_custom_call" | custom-call | flops 268435456 | bytes 262144 | tf_op jit(solution)/shard_map/pallas_call | solution.py:494
  284.9 7.2 %collective-permute-done.18 = bf16[2,512,256]{2,1,0:T(8,128)(2,1)S(1)} collective-permute-done((bf16[2,512,256]{2,1,0:T(8,128)(2,1)S(1)}, bf16[2,512,256]{2,1,0:T(8,128)(2,1)S(1)}, u32[]{:S(2)}, u32[]{:S(2)}) %collective-permute-start.18) | collective-permute-done | bytes 524320 | tf_op jit(solution)/shard_map/ppermute | solution.py:45
  293.6 10.2 %shard_map.211 = bf16[1024,2048]{1,0:T(8,128)(2,1)} custom-call(bf16[1024,1024]{1,0:T(8,128)(2,1)} %get-tuple-element.217.acts, bf16[4,512,256]{2,1,0:T(8,128)(2,1)} %copy-done.4, bf16[4,512,256]{2,1,0:T(8,128)(2,1)} %copy-done.10, bf16[4,512,256]{2,1,0:T(8,128)(2,1)} %copy-done.9, bf16[4,512,256]{2,1,0:T(8,128)(2,1)} %copy-done.11), custom_call_target="tpu_custom_call" | custom-call | flops 268435456 | bytes 262144 | tf_op jit(solution)/shard_map/pallas_call | solution.py:494
  304.3 11.7 %shard_map.212 = (bf16[1024,1024]{1,0:T(8,128)(2,1)}, bf16[1024,1024]{1,0:T(8,128)(2,1)}) custom-call(bf16[1024,2048]{1,0:T(8,128)(2,1)} %all-gather.10.cloned.1.call-done.grads, bf16[4,512,256]{2,1,0:T(8,128)(2,1)} %copy-done.4, bf16[4,512,256]{2,1,0:T(8,128)(2,1)} %copy-done.10, bf16[4,512,256]{2,1,0:T(8,128)(2,1)} %copy-done.9, ...), custom_call_target="tpu_custom_call" | custom-call | flops 268435456 | bytes 262144 | tf_op jit(solution)/shard_map/pallas_call | solution.py:494
  329.7 15.1 %shard_map.213 = bf16[1024,2048]{1,0:T(8,128)(2,1)} custom-call(bf16[1024,1024]{1,0:T(8,128)(2,1)} %get-tuple-element.229.refs_0_, bf16[1024,1024]{1,0:T(8,128)(2,1)} %get-tuple-element.228.refs_1_, bf16[1024,512]{1,0:T(8,128)(2,1)} %bitcast.178, bf16[1024,512]{1,0:T(8,128)(2,1)} %collective-permute-done.10.refs_1_.refs_3_, ...), custom_call_target="tpu_custom_call" | custom-call | flops 268435456 | bytes 262144 | tf_op jit(solution)/shard_map/pallas_call | solution.py:494
  352.3 15.8 %collective-permute-done.22 = bf16[1024,512]{1,0:T(8,128)(2,1)S(1)} collective-permute-done((bf16[1024,512]{1,0:T(8,128)(2,1)}, bf16[1024,512]{1,0:T(8,128)(2,1)S(1)}, u32[]{:S(2)}, u32[]{:S(2)}) %collective-permute-start.22) | collective-permute-done | bytes 1048608 | tf_op jit(solution)/shard_map/ppermute | solution.py:45
  385.7 14.0 %collective-permute-done.23 = bf16[1024,512]{1,0:T(8,128)(2,1)S(1)} collective-permute-done((bf16[1024,512]{1,0:T(8,128)(2,1)S(1)}, bf16[1024,512]{1,0:T(8,128)(2,1)S(1)}, u32[]{:S(2)}, u32[]{:S(2)}) %collective-permute-start.23) | collective-permute-done | bytes 1048608 | tf_op jit(solution)/shard_map/ppermute | solution.py:45
  448.0 7.2 %collective-permute-done.29.grads = bf16[512,256]{1,0:T(8,128)(2,1)S(1)} collective-permute-done((bf16[512,256]{1,0:T(8,128)(2,1)S(1)}, bf16[512,256]{1,0:T(8,128)(2,1)S(1)}, u32[]{:S(2)}, u32[]{:S(2)}) %collective-permute-start.29) | collective-permute-done | bytes 262176 | tf_op jit(solution)/shard_map/ppermute | solution.py:45
  457.5 11.2 %shard_map.215 = (bf16[512,256]{1,0:T(8,128)(2,1)}, f32[16,128,256]{2,1,0:T(8,128)}) custom-call(s32[16]{0:T(128)} %parents.7, s32[2]{0:T(128)} %copy-done.54, bf16[512,256]{1,0:T(8,128)(2,1)} %copy-done.37, bf16[512,256]{1,0:T(8,128)(2,1)} %copy-done.45, f32[512,256]{1,0:T(8,128)} %get-tuple-element.261.attended, f32[2,1024,1]{2,1,0:T(8,128)} %get-tuple-element.262.stats, ...), custom_call_target="tpu_custom_call" | custom-call | flops 268435456 | bytes 262144 | tf_op jit(solution)/shard_map/pallas_call | solution.py:377
  468.7 12.5 %collective-permute-done.30 = bf16[1024,512]{1,0:T(8,128)(2,1)S(1)} collective-permute-done((bf16[1024,512]{1,0:T(8,128)(2,1)S(1)}, bf16[1024,512]{1,0:T(8,128)(2,1)S(1)}, u32[]{:S(2)}, u32[]{:S(2)}) %collective-permute-start.30) | collective-permute-done | bytes 1048608 | tf_op jit(solution)/shard_map/ppermute | solution.py:45
  483.6 11.6 %shard_map.216 = (bf16[512,256]{1,0:T(8,128)(2,1)}, bf16[16,128,256]{2,1,0:T(8,128)(2,1)}) custom-call(s32[16]{0:T(128)} %parents.7, s32[2]{0:T(128)} %copy-done.55, bf16[512,256]{1,0:T(8,128)(2,1)} %get-tuple-element.188.queries, bf16[512,256]{1,0:T(8,128)(2,1)} %get-tuple-element.257.grads, f32[512,256]{1,0:T(8,128)} %get-tuple-element.258.attended, ...), custom_call_target="tpu_custom_call" | custom-call | flops 268435456 | bytes 262144 | tf_op jit(solution)/shard_map/pallas_call | solution.py:377
  525.7 13.2 %collective-permute-done.34 = bf16[1024,512]{1,0:T(8,128)(2,1)} collective-permute-done((bf16[1024,512]{1,0:T(8,128)(2,1)}, bf16[1024,512]{1,0:T(8,128)(2,1)}, u32[]{:S(2)}, u32[]{:S(2)}) %collective-permute-start.34) | collective-permute-done | bytes 1048608 | tf_op jit(solution)/shard_map/ppermute | solution.py:45
  577.9 8.7 %collective-permute-done.37 = bf16[128,2048]{1,0:T(8,128)(2,1)} collective-permute-done((bf16[128,2048]{1,0:T(8,128)(2,1)}, bf16[128,2048]{1,0:T(8,128)(2,1)}, u32[]{:S(2)}, u32[]{:S(2)}) %collective-permute-start.37) | collective-permute-done | bytes 524320 | tf_op jit(solution)/shard_map/ppermute | solution.py:45
  602.7 14.9 %all-to-all-done.7 = f32[32,2,256]{2,1,0:T(2,128)S(1)} async-done(((f32[32,2,256]{2,1,0:T(2,128)}), f32[32,2,256]{2,1,0:T(2,128)S(1)}, u32[]{:S(2)}, u32[]{:S(2)}) %all-to-all-start.7) | async-done | bytes 65568 | tf_op jit(solution)/shard_map/all_to_all | solution.py:67
  (391 shorter events, 322.3 us)
Async XLA Ops:
  16.4 34.0 %all-gather.6.cloned.1.call-start = ((), (), s32[]{:S(2)}) async-start(), calls=%async_computation.12 | async-start | bytes 1310720 | tf_op jit(solution)/shard_map/all_gather | solution.py:799
  21.7 80.6 %all-gather.12.cloned.1.call-start = ((), (), s32[]{:S(2)}) async-start(), calls=%async_computation.19 | async-start | bytes 1310720 | tf_op jit(solution)/shard_map/all_gather | solution.py:802
  62.2 43.6 %all-to-all-start.1 = ((bf16[4,2,512,128]{3,2,1,0:T(8,128)(2,1)}), bf16[4,2,512,128]{3,2,1,0:T(8,128)(2,1)S(1)}, u32[]{:S(2)}, u32[]{:S(2)}) async-start(bf16[4,2,512,128]{3,2,1,0:T(8,128)(2,1)} %broadcast_in_dim.23), calls=%async_computation.1 | async-start | bytes 2097152 | tf_op jit(solution)/shard_map/all_to_all | solution.py:63
  106.8 52.9 %all-to-all-start.2 = ((bf16[4,2,256,512]{3,2,1,0:T(8,128)(2,1)}), bf16[4,2,256,512]{3,2,1,0:T(8,128)(2,1)}, u32[]{:S(2)}, u32[]{:S(2)}) async-start(bf16[4,2,256,512]{3,2,1,0:T(8,128)(2,1)} %shard_map.205), calls=%async_computation.2 | async-start | bytes 4194304 | tf_op jit(solution)/shard_map/all_to_all | solution.py:67
  111.2 148.3 %all-gather.8.cloned.1.call-start = ((), (), s32[]{:S(2)}) async-start(), calls=%async_computation.13 | async-start | bytes 4718592 | tf_op jit(solution)/shard_map/all_gather | solution.py:872
  111.5 30.5 %collective-permute-start.7 = (bf16[4,512,256]{2,1,0:T(8,128)(2,1)S(1)}, bf16[4,512,256]{2,1,0:T(8,128)(2,1)S(1)}, u32[]{:S(2)}, u32[]{:S(2)}) collective-permute-start(bf16[4,512,256]{2,1,0:T(8,128)(2,1)S(1)} %bitcast.197), channel_id=1, source_target_pairs={{0,4},{4,0},{1,5},{5,1},{2,6},{6,2},{3,7},{7,3},{8,12},{12,8},{9,1... | collective-permute-start | bytes 3145736 | tf_op jit(solution)/shard_map/ppermute | solution.py:45
  177.2 26.2 %collective-permute-start.11 = (bf16[1024,512]{1,0:T(8,128)(2,1)S(1)}, bf16[1024,512]{1,0:T(8,128)(2,1)}, u32[]{:S(2)}, u32[]{:S(2)}) collective-permute-start(bf16[1024,512]{1,0:T(8,128)(2,1)S(1)} %bitcast.176), channel_id=1, source_target_pairs={{0,4},{4,0},{1,5},{5,1},{2,6},{6,2},{3,7},{7,3},{8,12},{12,8},{9,1... | collective-permute-start | bytes 3145736 | tf_op jit(solution)/shard_map/ppermute | solution.py:45
  178.6 57.3 %all-to-all-start.3 = ((bf16[4,512,256]{2,1,0:T(8,128)(2,1)}), bf16[4,512,256]{2,1,0:T(8,128)(2,1)S(1)}, u32[]{:S(2)}, u32[]{:S(2)}) async-start(bf16[4,512,256]{2,1,0:T(8,128)(2,1)} %bitcast.215), calls=%async_computation.3 | async-start | bytes 2097152 | tf_op jit(solution)/shard_map/all_to_all | solution.py:67
  185.6 118.2 %all-gather.10.cloned.1.call-start = ((), (), s32[]{:S(2)}) async-start(), calls=%async_computation.14 | async-start | bytes 4718592 | tf_op jit(solution)/shard_map/all_gather | solution.py:879
  185.6 37.1 %collective-permute-start.14 = (bf16[1024,512]{1,0:T(8,128)(2,1)}, bf16[1024,512]{1,0:T(8,128)(2,1)}, u32[]{:S(2)}, u32[]{:S(2)}) collective-permute-start(bf16[1024,512]{1,0:T(8,128)(2,1)} %bitcast.179), channel_id=1, source_target_pairs={{0,4},{4,0},{1,5},{5,1},{2,6},{6,2},{3,7},{7,3},{8,12},{12,8},{9,1... | collective-permute-start | bytes 3145736 | tf_op jit(solution)/shard_map/ppermute | solution.py:45
  235.9 169.9 %reduce-scatter.7.cloned.1.call-start = ((), (), s32[]{:S(2)}) async-start(), calls=%async_computation.16 | async-start | bytes 4718592 | tf_op jit(solution)/shard_map/reduce_scatter | solution.py:894
  303.9 108.4 %reduce-scatter.5.cloned.1.call-start = ((), (), s32[]{:S(2)}) async-start(), calls=%async_computation.15 | async-start | bytes 4718592 | tf_op jit(solution)/shard_map/reduce_scatter | solution.py:912
  318.4 26.5 %collective-permute-start.20 = (bf16[1024,512]{1,0:T(8,128)(2,1)}, bf16[1024,512]{1,0:T(8,128)(2,1)}, u32[]{:S(2)}, u32[]{:S(2)}) collective-permute-start(bf16[1024,512]{1,0:T(8,128)(2,1)} %fusion.18), channel_id=1, source_target_pairs={{0,4},{4,0},{1,5},{5,1},{2,6},{6,2},{3,7},{7,3},{8,12},{12,8},{9,1... | collective-permute-start | bytes 3145736 | tf_op jit(solution)/shard_map/ppermute | solution.py:45
  373.5 26.2 %collective-permute-start.23 = (bf16[1024,512]{1,0:T(8,128)(2,1)S(1)}, bf16[1024,512]{1,0:T(8,128)(2,1)S(1)}, u32[]{:S(2)}, u32[]{:S(2)}) collective-permute-start(bf16[1024,512]{1,0:T(8,128)(2,1)S(1)} %fusion.21), channel_id=1, source_target_pairs={{0,4},{4,0},{1,5},{5,1},{2,6},{6,2},{3,7},{7,3},{8,12},{12,8},{9,1... | collective-permute-start | bytes 3145736 | tf_op jit(solution)/shard_map/ppermute | solution.py:45
  377.4 41.2 %collective-permute-start.26 = (bf16[1024,512]{1,0:T(8,128)(2,1)}, bf16[1024,512]{1,0:T(8,128)(2,1)}, u32[]{:S(2)}, u32[]{:S(2)}) collective-permute-start(bf16[1024,512]{1,0:T(8,128)(2,1)} %convolution_convert_fusion), channel_id=1, source_target_pairs={{0,4},{4,0},{1,5},{5,1},{2,6},{6,2},{3,7},{7,3},{8,12},{12,8},{9,1... | collective-permute-start | bytes 3145736 | tf_op jit(solution)/shard_map/ppermute | solution.py:45
  383.8 41.0 %collective-permute-start.27 = (bf16[1024,512]{1,0:T(8,128)(2,1)}, bf16[1024,512]{1,0:T(8,128)(2,1)}, u32[]{:S(2)}, u32[]{:S(2)}) collective-permute-start(bf16[1024,512]{1,0:T(8,128)(2,1)} %add_convert_fusion.7), channel_id=1, source_target_pairs={{0,2},{2,0},{1,3},{3,1},{4,6},{6,4},{5,7},{7,5},{8,10},{10,8},{9,1... | collective-permute-start | bytes 3145736 | tf_op jit(solution)/shard_map/ppermute | solution.py:45
  439.3 57.8 %all-to-all-start.4 = ((bf16[4,2,256,512]{3,2,1,0:T(8,128)(2,1)}), bf16[4,2,256,512]{3,2,1,0:T(8,128)(2,1)}, u32[]{:S(2)}, u32[]{:S(2)}) async-start(bf16[4,2,256,512]{3,2,1,0:T(8,128)(2,1)} %pad_maximum_fusion), calls=%async_computation.6 | async-start | bytes 4194304 | tf_op jit(solution)/shard_map/all_to_all | solution.py:67
  443.8 81.9 %reduce-scatter.9.cloned.1.call-start = ((), (), s32[]{:S(2)}) async-start(), calls=%async_computation.17 | async-start | bytes 1310720 | tf_op jit(solution)/shard_map/reduce_scatter | solution.py:959
  455.2 26.1 %collective-permute-start.30 = (bf16[1024,512]{1,0:T(8,128)(2,1)S(1)}, bf16[1024,512]{1,0:T(8,128)(2,1)S(1)}, u32[]{:S(2)}, u32[]{:S(2)}) collective-permute-start(bf16[1024,512]{1,0:T(8,128)(2,1)S(1)} %convolution_convert_fusion.5), channel_id=1, source_target_pairs={{0,4},{4,0},{1,5},{5,1},{2,6},{6,2},{3,7},{7,3},{8,12},{12,8},{9,1... | collective-permute-start | bytes 3145736 | tf_op jit(solution)/shard_map/ppermute | solution.py:45
  455.6 48.2 %collective-permute-start.32 = (bf16[1024,512]{1,0:T(8,128)(2,1)}, bf16[1024,512]{1,0:T(8,128)(2,1)}, u32[]{:S(2)}, u32[]{:S(2)}) collective-permute-start(bf16[1024,512]{1,0:T(8,128)(2,1)} %add_convert_fusion.6), channel_id=1, source_target_pairs={{0,4},{4,0},{1,5},{5,1},{2,6},{6,2},{3,7},{7,3},{8,12},{12,8},{9,1... | collective-permute-start | bytes 3145736 | tf_op jit(solution)/shard_map/ppermute | solution.py:45
  457.2 46.6 %collective-permute-start.33 = (bf16[1024,512]{1,0:T(8,128)(2,1)}, bf16[1024,512]{1,0:T(8,128)(2,1)}, u32[]{:S(2)}, u32[]{:S(2)}) collective-permute-start(bf16[1024,512]{1,0:T(8,128)(2,1)} %convolution_convert_fusion.1), channel_id=1, source_target_pairs={{0,2},{2,0},{1,3},{3,1},{4,6},{6,4},{5,7},{7,5},{8,10},{10,8},{9,1... | collective-permute-start | bytes 3145736 | tf_op jit(solution)/shard_map/ppermute | solution.py:45
  507.9 31.0 %all-to-all-start.5 = ((bf16[4,4,128,256]{3,2,1,0:T(8,128)(2,1)}), bf16[4,4,128,256]{3,2,1,0:T(8,128)(2,1)}, u32[]{:S(2)}, u32[]{:S(2)}) async-start(bf16[4,4,128,256]{3,2,1,0:T(8,128)(2,1)} %bitcast.216), calls=%async_computation.7 | async-start | bytes 2097152 | tf_op jit(solution)/shard_map/all_to_all | solution.py:67
  544.1 27.7 %all-to-all-start.6 = ((bf16[4,256,512]{2,1,0:T(8,128)(2,1)}), bf16[4,256,512]{2,1,0:T(8,128)(2,1)}, u32[]{:S(2)}, u32[]{:S(2)}) async-start(bf16[4,256,512]{2,1,0:T(8,128)(2,1)} %bitcast.194), calls=%async_computation.9 | async-start | bytes 2097152 | tf_op jit(solution)/shard_map/all_to_all | solution.py:67
  548.8 77.1 %reduce-scatter.11.cloned.1.call-start = ((), (), s32[]{:S(2)}) async-start(), calls=%async_computation.18 | async-start | bytes 1310720 | tf_op jit(solution)/shard_map/reduce_scatter | solution.py:1006
  (94 other events, 1357.7 us)
Sparse Core Ops, SparseCore 0:
  21.9 28.4 all-gather.5
  56.6 45.6 all-gather.11
  175.7 69.8 all-gather.7
  247.6 44.3 all-gather.9
  304.0 48.7 reduce-scatter.6
  355.0 48.1 reduce-scatter.4
  483.2 27.1 reduce-scatter.8
  578.0 35.8 reduce-scatter.10

commit v6 on v5

--- a/solution.py
+++ b/solution.py
@@ -11,7 +11,7 @@
 SEG = 256
 MAX_STEPS = 9
 LANES = 2 * HEAD_SIZE
-KERNEL_VMEM = 56 * 2**20
+KERNEL_VMEM = 32 * 2**20
 SMALL_COST = pl.CostEstimate(flops=2**28, bytes_accessed=2**18, transcendentals=0)
 
 
@@ -387,7 +387,7 @@
             jax.ShapeDtypeStruct((seg_total, LANES, SEG), sum_type),
         ],
         scratch_shapes=[pltpu.VMEM((seg_total, LANES, SEG), jnp.float32)],
-        compiler_params=pltpu.CompilerParams(vmem_limit_bytes=KERNEL_VMEM),
+        compiler_params=pltpu.CompilerParams(vmem_limit_bytes=56 * 2**20),
         cost_estimate=SMALL_COST,
     )(
         parents, segs, queries, grads, attended, stats, cosine, sine, keys_values,
@@ -914,14 +914,13 @@
     down_near = summed_pieces([turned_matmul(a, acts[0]) for a in grad_parts], "y")
     down_far = [rotated(v, "x", -1 - i) for i, v in enumerate(down_far)]
     down_near, down_far, mlp_mine = together(down_near, down_far, mlp_mine)
-    mixed = natural_columns((middle + branch_scale * mlp_mine.astype(jnp.float32)).astype(low))
     grad_down_z = sum([v.astype(jnp.float32) for v in down_far], down_near).astype(low)
     gate_near = summed_pieces([turned_matmul(a, gate_parts[0]) for a in rows_parts], "y")
     gate_far = [rotated(v, "x", -1 - i) for i, v in enumerate(gate_far)]
     up_near = [turned_matmul(rows_parts[0], b) for b in up_parts]
     up_near[1:] = [v.astype(low) for v in up_near[1:]]
-    grad_rows_two, mixed, up_far, up_near, grad_down_z = together(
-        grad_rows_two, mixed, up_far, up_near, grad_down_z
+    grad_rows_two, mlp_mine, up_far, up_near, grad_down_z = together(
+        grad_rows_two, mlp_mine, up_far, up_near, grad_down_z
     )
     grad_rows_two = grad_rows_two.astype(jnp.float32)
     gain_two_part = jnp.sum(grad_rows_two * normed_two, axis=0)
@@ -1006,8 +1005,9 @@
     grad_q = lax.psum_scatter(grad_q_y, "z", scatter_dimension=0, tiled=True)
     input_x = x_blocks(input_core)
     input_sent = [rotated(v, "x", -1 - i) for i, v in enumerate(input_x[1:])]
-    input_x[0], input_sent, kv_sent, kv_dots, wide_z, grad_up, grad_o = together(
-        input_x[0], input_sent, kv_sent, kv_dots, wide_z, grad_up, grad_o
+    grad_gate, grad_down, grad_up = finished(wide_z, grad_up)
+    input_x[0], input_sent, kv_sent, kv_dots, grad_gate, grad_down, grad_up, grad_o = together(
+        input_x[0], input_sent, kv_sent, kv_dots, grad_gate, grad_down, grad_up, grad_o
     )
     grad_rows_one = sum([v.astype(jnp.float32) for v in input_sent], input_x[0].astype(jnp.float32))
     kv_blocks = own_first(total(kv_dots[0], kv_sent).reshape(z_size, own_width, -1), "z")
@@ -1020,15 +1020,15 @@
         gain_parts, (2, z_size * y_size, tensor_size, own_width)
     ).reshape(2, -1, own_width).transpose(1, 0, 2)
     gain_parts = exchanged(gain_parts, ("z", "y", "x", "c"))
+    mlp_mine = after(mlp_mine, grad_inputs)
+    mixed = natural_columns((middle + branch_scale * mlp_mine.astype(jnp.float32)).astype(low))
     grad_tokens = natural_columns(grad_inputs.astype(low))
-    gain_parts, kv_sent, kv_blocks, wide_z, grad_up, grad_o, grad_tokens = together(
-        gain_parts, kv_sent, kv_blocks, wide_z, grad_up, grad_o, grad_tokens
+    grad_o = after(grad_o, grad_inputs).astype(jnp.float32).T
+    gain_parts, kv_sent, kv_blocks, grad_q, grad_o, grad_tokens, mixed = together(
+        gain_parts, kv_sent, kv_blocks, grad_q.astype(jnp.float32), grad_o, grad_tokens, mixed
     )
     gain_sums = jnp.sum(gain_parts, axis=0)
-    grad_gate, grad_down, grad_up = finished(wide_z, grad_up)
-    grad_o = grad_o.astype(jnp.float32).T
     grad_kv_weight = sum([v.astype(jnp.float32) for v in kv_sent], kv_blocks[0].astype(jnp.float32))
-    grad_q = grad_q.astype(jnp.float32)
     grad_heads = halves(grad_kv_weight, 2 * kv_local)
     return (
         mixed,

time: 645 us -> 633 us (0.981)
  local copies, waits for them, and re-layouts: 43.7 us -> 81.6 us
  waiting for transfers between devices: 268 us -> 240 us
  Pallas kernels: 128 us -> 112 us
    unnamed x128 -> x220, local copies, waits for them, and re-layouts: 11.8 us -> 51.7 us
    ppermute x42, waiting for transfers between devices: 214 us -> 193 us  [rotated(): lax.ppermute(value, axis, [(i, (i + step) % size) for i in range(size)])]
    pallas_call x4, Pallas kernels: 52.8 us -> 40.6 us  [wide_call(): pl.pallas_call(functools.partial(kernel, per, parts, pieces), grid=(count...]
    all_to_all x7, waiting for transfers between devices: 45.5 us -> 36.9 us  [exchanged(): return lax.all_to_all(blocks, axis, 0, 0, tiled=True)]
    pallas_call x2, Pallas kernels: 22.8 us -> 29.9 us  [attend_back(): pl.pallas_call(attend_back_kernel, grid=(count // SEG,), in_specs=[scalar...]
  transfers between devices with their start and end apart: 58 -> 58, of which waited for: 37 -> 34; matrix products, arithmetic and copies ran while one was open for 20% -> 18% of each run, Pallas kernels for 18% -> 17%
where the time goes in v6:
time: 633 us; the launch traced here: 623 us
  waiting for transfers between devices  240 us (38%)
  Pallas kernels  112 us (18%)
  local copies, waits for them, and re-layouts  81.6 us (13%)
  starting transfers between devices  80.2 us (13%)
  other arithmetic  46.7 us (7%)
  matrix products  46.5 us (7%)
  between operations  16.1 us (3%)
    ppermute x42, waiting for transfers between devices, rotated(): lax.ppermute(value, axis, [(i, (i + step) % size) for i in range(size)])  193 us
    unnamed x220, local copies, waits for them, and re-layouts  51.7 us
    ppermute x42, starting transfers between devices, rotated(): lax.ppermute(value, axis, [(i, (i + step) % size) for i in range(size)])  42.5 us
    pallas_call x4, Pallas kernels, wide_call(): pl.pallas_call(functools.partial(kernel, per, parts, pieces), grid=(count...  40.6 us
    dot_general x18, matrix products, turned_matmul(): lax.dot_general(left, right, (((0,), (0,)), ((), ())), preferred_element_...  40.3 us
    all_to_all x7, waiting for transfers between devices, exchanged(): return lax.all_to_all(blocks, axis, 0, 0, tiled=True)  36.9 us
    all_to_all x7, starting transfers between devices, exchanged(): return lax.all_to_all(blocks, axis, 0, 0, tiled=True)  32.8 us
    pallas_call x2, Pallas kernels, attend_back(): pl.pallas_call(attend_back_kernel, grid=(count // SEG,), in_specs=[scalar...  29.9 us
  transfers between devices with their start and end apart: 58, of which 34 were waited for; matrix products, arithmetic and copies ran while one was open for 18% of the time, Pallas kernels for 17%

profile of v6, /device:TPU:0, one launch (start us, length us, event | category | flops | bytes accessed | tf_op | source)
XLA Modules:
  0.0 623.1 jit_solution(4491272676245304252)
XLA Ops:
  25.2 6.9 %all-to-all-done = bf16[4,258,256]{2,1,0:T(8,128)(2,1)S(1)} async-done(((bf16[4,258,256]{2,1,0:T(8,128)(2,1)}), bf16[4,258,256]{2,1,0:T(8,128)(2,1)S(1)}, u32[]{:S(2)}, u32[]{:S(2)}) %all-to-all-start) | async-done | bytes 528416 | tf_op jit(solution)/shard_map/all_to_all | solution.py:67
  36.3 9.0 %collective-permute-done.2 = bf16[4,258,256]{2,0,1:T(4,128)(2,1)S(1)} collective-permute-done((bf16[4,258,256]{2,0,1:T(4,128)(2,1)S(1)}, bf16[4,258,256]{2,0,1:T(4,128)(2,1)S(1)}, u32[]{:S(2)}, u32[]{:S(2)}) %collective-permute-start.2) | collective-permute-done | bytes 528416 | tf_op jit(solution)/shard_map/ppermute | solution.py:45
  68.3 18.9 %collective-permute-done.4.refs_1_ = bf16[1024,512]{1,0:T(8,128)(2,1)} collective-permute-done((bf16[1024,512]{1,0:T(8,128)(2,1)}, bf16[1024,512]{1,0:T(8,128)(2,1)}, u32[]{:S(2)}, u32[]{:S(2)}) %collective-permute-start.4) | collective-permute-done | bytes 1048608 | tf_op jit(solution)/shard_map/ppermute | solution.py:45
  92.5 6.9 %all-gather.12.cloned.1.call-done = bf16[2048,256]{1,0:T(8,128)(2,1)} async-done(((bf16[512,256]{1,0:T(8,128)(2,1)}), bf16[2048,256]{1,0:T(8,128)(2,1)}) %all-gather.12.cloned.1.call-update) | async-done | bytes 1048592 | tf_op jit(solution)/shard_map/all_gather | solution.py:802
  109.2 16.3 %shard_map.207 = (f32[512,256]{1,0:T(8,128)S(1)}, f32[2,1024,1]{2,1,0:T(8,128)S(1)}, bf16[512,256]{1,0:T(8,128)(2,1)}) custom-call(s32[16]{0:T(128)S(1)} %copy-done.59, s32[2]{0:T(128)S(1)} %iota_add_fusion.segs, bf16[512,256]{1,0:T(8,128)(2,1)} %collective-permute-done.5.queries, bf16[16,256,128]{2,1,0:T(8,128)(2,1)S(1)} %bitcast.171), custom_call_target="tpu_custom_call" | custom-call | flops 268435456 | bytes 262144 | tf_op jit(solution)/shard_map/pallas_call | solution.py:351
  161.3 8.8 %collective-permute-done.9 = bf16[128,2048]{1,0:T(8,128)(2,1)} collective-permute-done((bf16[128,2048]{1,0:T(8,128)(2,1)}, bf16[128,2048]{1,0:T(8,128)(2,1)}, u32[]{:S(2)}, u32[]{:S(2)}) %collective-permute-start.9) | collective-permute-done | bytes 524320 | tf_op jit(solution)/shard_map/ppermute | solution.py:45
  182.8 14.8 %collective-permute-done.10.refs_1_.refs_3_ = bf16[1024,512]{1,0:T(8,128)(2,1)} collective-permute-done((bf16[1024,512]{1,0:T(8,128)(2,1)}, bf16[1024,512]{1,0:T(8,128)(2,1)}, u32[]{:S(2)}, u32[]{:S(2)}) %collective-permute-start.10) | collective-permute-done | bytes 1048608 | tf_op jit(solution)/shard_map/ppermute | solution.py:45
  210.1 13.6 %collective-permute-done.14.refs_6_.refs_8_ = bf16[1024,512]{1,0:T(8,128)(2,1)} collective-permute-done((bf16[1024,512]{1,0:T(8,128)(2,1)}, bf16[1024,512]{1,0:T(8,128)(2,1)}, u32[]{:S(2)}, u32[]{:S(2)}) %collective-permute-start.14) | collective-permute-done | bytes 1048608 | tf_op jit(solution)/shard_map/ppermute | solution.py:45
  225.1 7.7 %all-to-all-done.3.refs_0_ = bf16[4,512,256]{2,1,0:T(8,128)(2,1)S(1)} async-done(((bf16[4,512,256]{2,1,0:T(8,128)(2,1)}), bf16[4,512,256]{2,1,0:T(8,128)(2,1)S(1)}, u32[]{:S(2)}, u32[]{:S(2)}) %all-to-all-start.3) | async-done | bytes 1048608 | tf_op jit(solution)/shard_map/all_to_all | solution.py:67
  233.5 20.9 %collective-permute-done.12.refs_3_.refs_5_ = bf16[1024,512]{1,0:T(8,128)(2,1)S(1)} collective-permute-done((bf16[1024,512]{1,0:T(8,128)(2,1)}, bf16[1024,512]{1,0:T(8,128)(2,1)S(1)}, u32[]{:S(2)}, u32[]{:S(2)}) %collective-permute-start.12) | collective-permute-done | bytes 1048608 | tf_op jit(solution)/shard_map/ppermute | solution.py:45
  261.3 14.7 %shard_map.210 = (bf16[1024,1024]{1,0:T(8,128)(2,1)S(1)}, f32[1024,1024]{1,0:T(8,128)S(1)}, f32[1024,1024]{1,0:T(8,128)S(1)}) custom-call(bf16[1024,2048]{1,0:T(8,128)(2,1)} %all-gather.8.cloned.1.call-done.rows, bf16[1024,512]{1,0:T(8,128)(2,1)} %bitcast.33.refs_0_.refs_2_, bf16[1024,512]{1,0:T(8,128)(2,1)} %collective-permute-done.10.refs_1_.refs_3_, ...), custom_call_target="tpu_custom_call" | custom-call | flops 268435456 | bytes 262144 | tf_op jit(solution)/shard_map/pallas_call | solution.py:494
  291.1 6.4 %shard_map.211 = bf16[1024,2048]{1,0:T(8,128)(2,1)S(1)} custom-call(bf16[1024,1024]{1,0:T(8,128)(2,1)S(1)} %get-tuple-element.220.acts, bf16[4,512,256]{2,1,0:T(8,128)(2,1)S(1)} %all-to-all-done.3.refs_0_, bf16[4,512,256]{2,1,0:T(8,128)(2,1)S(1)} %collective-permute-done.17.refs_1_, bf16[4,512,256]{2,1,0:T(8,128)(2,1)S(1)} %collective-permute-done.16.refs_2_, ...), custom_call_target="tpu_custom_call" | custom-call | flops 268435456 | bytes 262144 | tf_op jit(solution)/shard_map/pallas_call | solution.py:494
  311.7 6.8 %shard_map.212 = (bf16[1024,1024]{1,0:T(8,128)(2,1)S(1)}, bf16[1024,1024]{1,0:T(8,128)(2,1)S(1)}) custom-call(bf16[1024,2048]{1,0:T(8,128)(2,1)S(1)} %copy-done.33, bf16[4,512,256]{2,1,0:T(8,128)(2,1)S(1)} %all-to-all-done.3.refs_0_, bf16[4,512,256]{2,1,0:T(8,128)(2,1)S(1)} %copy-done.16, bf16[4,512,256]{2,1,0:T(8,128)(2,1)S(1)} %copy-done.14, ...), custom_call_target="tpu_custom_call" | custom-call | flops 268435456 | bytes 262144 | tf_op jit(solution)/shard_map/pallas_call | solution.py:494
  332.4 12.7 %shard_map.213 = bf16[1024,2048]{1,0:T(8,128)(2,1)S(1)} custom-call(bf16[1024,1024]{1,0:T(8,128)(2,1)S(1)} %get-tuple-element.232.refs_0_, bf16[1024,1024]{1,0:T(8,128)(2,1)S(1)} %get-tuple-element.231.refs_1_, bf16[1024,512]{1,0:T(8,128)(2,1)} %bitcast.33.refs_0_.refs_2_, bf16[1024,512]{1,0:T(8,128)(2,1)} %collective-permute-done.10.refs_1_.refs_3_, ...), custom_call_target="tpu_custom_call" | custom-call | flops 268435456 | bytes 262144 | tf_op jit(solution)/shard_map/pallas_call | solution.py:494
  354.1 14.7 %collective-permute-done.22 = bf16[1024,512]{1,0:T(8,128)(2,1)S(1)} collective-permute-done((bf16[1024,512]{1,0:T(8,128)(2,1)}, bf16[1024,512]{1,0:T(8,128)(2,1)S(1)}, u32[]{:S(2)}, u32[]{:S(2)}) %collective-permute-start.22) | collective-permute-done | bytes 1048608 | tf_op jit(solution)/shard_map/ppermute | solution.py:45
  386.1 14.1 %collective-permute-done.23 = bf16[1024,512]{1,0:T(8,128)(2,1)S(1)} collective-permute-done((bf16[1024,512]{1,0:T(8,128)(2,1)S(1)}, bf16[1024,512]{1,0:T(8,128)(2,1)S(1)}, u32[]{:S(2)}, u32[]{:S(2)}) %collective-permute-start.23) | collective-permute-done | bytes 1048608 | tf_op jit(solution)/shard_map/ppermute | solution.py:45
  416.1 7.0 %collective-permute-done.27 = bf16[1024,512]{1,0:T(8,128)(2,1)} collective-permute-done((bf16[1024,512]{1,0:T(8,128)(2,1)}, bf16[1024,512]{1,0:T(8,128)(2,1)}, u32[]{:S(2)}, u32[]{:S(2)}) %collective-permute-start.27) | collective-permute-done | bytes 1048608 | tf_op jit(solution)/shard_map/ppermute | solution.py:45
  445.7 6.4 %collective-permute-done.29.grads = bf16[512,256]{1,0:T(8,128)(2,1)S(1)} collective-permute-done((bf16[512,256]{1,0:T(8,128)(2,1)S(1)}, bf16[512,256]{1,0:T(8,128)(2,1)S(1)}, u32[]{:S(2)}, u32[]{:S(2)}) %collective-permute-start.29) | collective-permute-done | bytes 262176 | tf_op jit(solution)/shard_map/ppermute | solution.py:45
  455.8 19.9 %shard_map.215 = (bf16[512,256]{1,0:T(8,128)(2,1)}, f32[16,128,256]{2,1,0:T(8,128)}) custom-call(s32[16]{0:T(128)} %parents.7, s32[2]{0:T(128)} %copy-done.60, bf16[512,256]{1,0:T(8,128)(2,1)} %collective-permute-done.5.queries, bf16[512,256]{1,0:T(8,128)(2,1)} %copy-done.94, f32[512,256]{1,0:T(8,128)} %copy-done.53, f32[2,1024,1]{2,1,0:T(8,128)} %copy-done.45, ...), custom_call_target="tpu_custom_call" | custom-call | flops 268435456 | bytes 262144 | tf_op jit(solution)/shard_map/pallas_call | solution.py:377
  482.6 9.9 %shard_map.216 = (bf16[512,256]{1,0:T(8,128)(2,1)}, bf16[16,128,256]{2,1,0:T(8,128)(2,1)}) custom-call(s32[16]{0:T(128)} %parents.7, s32[2]{0:T(128)} %copy-done.61, bf16[512,256]{1,0:T(8,128)(2,1)} %copy-done.39, bf16[512,256]{1,0:T(8,128)(2,1)} %get-tuple-element.259.grads, f32[512,256]{1,0:T(8,128)} %copy-done.58, f32[2,1024,1]{2,1,0:T(8,128)} %copy-done.52, ...), custom_call_target="tpu_custom_call" | custom-call | flops 268435456 | bytes 262144 | tf_op jit(solution)/shard_map/pallas_call | solution.py:377
  492.5 8.1 %collective-permute-done.32 = bf16[1024,512]{1,0:T(8,128)(2,1)S(1)} collective-permute-done((bf16[1024,512]{1,0:T(8,128)(2,1)}, bf16[1024,512]{1,0:T(8,128)(2,1)S(1)}, u32[]{:S(2)}, u32[]{:S(2)}) %collective-permute-start.32) | collective-permute-done | bytes 1048608 | tf_op jit(solution)/shard_map/ppermute | solution.py:45
  522.6 13.0 %collective-permute-done.34 = bf16[1024,512]{1,0:T(8,128)(2,1)} collective-permute-done((bf16[1024,512]{1,0:T(8,128)(2,1)}, bf16[1024,512]{1,0:T(8,128)(2,1)}, u32[]{:S(2)}, u32[]{:S(2)}) %collective-permute-start.34) | collective-permute-done | bytes 1048608 | tf_op jit(solution)/shard_map/ppermute | solution.py:45
  560.9 8.5 %all-to-all-done.6.single = bf16[4,256,512]{2,1,0:T(8,128)(2,1)} async-done(((bf16[4,256,512]{2,1,0:T(8,128)(2,1)}), bf16[4,256,512]{2,1,0:T(8,128)(2,1)}, u32[]{:S(2)}, u32[]{:S(2)}) %all-to-all-start.6) | async-done | bytes 1048608 | tf_op jit(solution)/shard_map/all_to_all | solution.py:67
  604.6 7.9 %all-to-all-done.7 = f32[32,2,256]{2,1,0:T(2,128)S(1)} async-done(((f32[32,2,256]{2,1,0:T(2,128)}), f32[32,2,256]{2,1,0:T(2,128)S(1)}, u32[]{:S(2)}, u32[]{:S(2)}) %all-to-all-start.7) | async-done | bytes 65568 | tf_op jit(solution)/shard_map/all_to_all | solution.py:67
  (485 shorter events, 332.9 us)
Async XLA Ops:
  17.2 32.1 %all-gather.6.cloned.1.call-start = ((), (), s32[]{:S(2)}) async-start(), calls=%async_computation.12 | async-start | bytes 1310720 | tf_op jit(solution)/shard_map/all_gather | solution.py:799
  20.3 79.1 %all-gather.12.cloned.1.call-start = ((), (), s32[]{:S(2)}) async-start(), calls=%async_computation.19 | async-start | bytes 1310720 | tf_op jit(solution)/shard_map/all_gather | solution.py:802
  59.1 43.9 %all-to-all-start.1 = ((bf16[4,2,512,128]{3,2,1,0:T(8,128)(2,1)}), bf16[4,2,512,128]{3,2,1,0:T(8,128)(2,1)S(1)}, u32[]{:S(2)}, u32[]{:S(2)}) async-start(bf16[4,2,512,128]{3,2,1,0:T(8,128)(2,1)} %broadcast_in_dim.23), calls=%async_computation.1 | async-start | bytes 2097152 | tf_op jit(solution)/shard_map/all_to_all | solution.py:63
  103.0 53.0 %all-to-all-start.2 = ((bf16[4,2,256,512]{3,2,1,0:T(8,128)(2,1)}), bf16[4,2,256,512]{3,2,1,0:T(8,128)(2,1)}, u32[]{:S(2)}, u32[]{:S(2)}) async-start(bf16[4,2,256,512]{3,2,1,0:T(8,128)(2,1)} %copy-done.6), calls=%async_computation.2 | async-start | bytes 4194304 | tf_op jit(solution)/shard_map/all_to_all | solution.py:67
  107.4 148.9 %all-gather.8.cloned.1.call-start = ((), (), s32[]{:S(2)}) async-start(), calls=%async_computation.13 | async-start | bytes 4718592 | tf_op jit(solution)/shard_map/all_gather | solution.py:872
  107.7 30.9 %collective-permute-start.7 = (bf16[4,512,256]{2,1,0:T(8,128)(2,1)}, bf16[4,512,256]{2,1,0:T(8,128)(2,1)}, u32[]{:S(2)}, u32[]{:S(2)}) collective-permute-start(bf16[4,512,256]{2,1,0:T(8,128)(2,1)} %bitcast.188), channel_id=1, source_target_pairs={{0,4},{4,0},{1,5},{5,1},{2,6},{6,2},{3,7},{7,3},{8,12},{12,8},{9,1... | collective-permute-start | bytes 3145736 | tf_op jit(solution)/shard_map/ppermute | solution.py:45
  175.6 27.5 %collective-permute-start.11 = (bf16[1024,512]{1,0:T(8,128)(2,1)}, bf16[1024,512]{1,0:T(8,128)(2,1)}, u32[]{:S(2)}, u32[]{:S(2)}) collective-permute-start(bf16[1024,512]{1,0:T(8,128)(2,1)} %bitcast.33.refs_0_.refs_2_), channel_id=1, source_target_pairs={{0,4},{4,0},{1,5},{5,1},{2,6},{6,2},{3,7},{7,3},{8,12},{12,8},{9,1... | collective-permute-start | bytes 3145736 | tf_op jit(solution)/shard_map/ppermute | solution.py:45
  178.6 54.2 %all-to-all-start.3 = ((bf16[4,512,256]{2,1,0:T(8,128)(2,1)}), bf16[4,512,256]{2,1,0:T(8,128)(2,1)S(1)}, u32[]{:S(2)}, u32[]{:S(2)}) async-start(bf16[4,512,256]{2,1,0:T(8,128)(2,1)} %bitcast.211), calls=%async_computation.3 | async-start | bytes 2097152 | tf_op jit(solution)/shard_map/all_to_all | solution.py:67
  182.1 118.4 %all-gather.10.cloned.1.call-start = ((), (), s32[]{:S(2)}) async-start(), calls=%async_computation.14 | async-start | bytes 4718592 | tf_op jit(solution)/shard_map/all_gather | solution.py:879
  182.2 41.6 %collective-permute-start.14 = (bf16[1024,512]{1,0:T(8,128)(2,1)}, bf16[1024,512]{1,0:T(8,128)(2,1)}, u32[]{:S(2)}, u32[]{:S(2)}) collective-permute-start(bf16[1024,512]{1,0:T(8,128)(2,1)} %bitcast.175), channel_id=1, source_target_pairs={{0,4},{4,0},{1,5},{5,1},{2,6},{6,2},{3,7},{7,3},{8,12},{12,8},{9,1... | collective-permute-start | bytes 3145736 | tf_op jit(solution)/shard_map/ppermute | solution.py:45
  232.8 172.7 %reduce-scatter.7.cloned.1.call-start = ((), (), s32[]{:S(2)}) async-start(), calls=%async_computation.16 | async-start | bytes 4718592 | tf_op jit(solution)/shard_map/reduce_scatter | solution.py:894
  300.6 108.0 %reduce-scatter.5.cloned.1.call-start = ((), (), s32[]{:S(2)}) async-start(), calls=%async_computation.15 | async-start | bytes 4718592 | tf_op jit(solution)/shard_map/reduce_scatter | solution.py:912
  320.8 26.3 %collective-permute-start.20 = (bf16[1024,512]{1,0:T(8,128)(2,1)}, bf16[1024,512]{1,0:T(8,128)(2,1)S(1)}, u32[]{:S(2)}, u32[]{:S(2)}) collective-permute-start(bf16[1024,512]{1,0:T(8,128)(2,1)} %fusion.18), channel_id=1, source_target_pairs={{0,4},{4,0},{1,5},{5,1},{2,6},{6,2},{3,7},{7,3},{8,12},{12,8},{9,1... | collective-permute-start | bytes 3145736 | tf_op jit(solution)/shard_map/ppermute | solution.py:45
  378.0 38.1 %collective-permute-start.26 = (bf16[1024,512]{1,0:T(8,128)(2,1)}, bf16[1024,512]{1,0:T(8,128)(2,1)}, u32[]{:S(2)}, u32[]{:S(2)}) collective-permute-start(bf16[1024,512]{1,0:T(8,128)(2,1)} %convolution_convert_fusion), channel_id=1, source_target_pairs={{0,4},{4,0},{1,5},{5,1},{2,6},{6,2},{3,7},{7,3},{8,12},{12,8},{9,1... | collective-permute-start | bytes 3145736 | tf_op jit(solution)/shard_map/ppermute | solution.py:45
  379.2 26.2 %collective-permute-start.24 = (bf16[1024,512]{1,0:T(8,128)(2,1)S(1)}, bf16[1024,512]{1,0:T(8,128)(2,1)}, u32[]{:S(2)}, u32[]{:S(2)}) collective-permute-start(bf16[1024,512]{1,0:T(8,128)(2,1)S(1)} %copy-done.105), channel_id=1, source_target_pairs={{0,2},{2,0},{1,3},{3,1},{4,6},{6,4},{5,7},{7,5},{8,10},{10,8},{9,1... | collective-permute-start | bytes 3145736 | tf_op jit(solution)/shard_map/ppermute | solution.py:45
  384.9 38.2 %collective-permute-start.27 = (bf16[1024,512]{1,0:T(8,128)(2,1)}, bf16[1024,512]{1,0:T(8,128)(2,1)}, u32[]{:S(2)}, u32[]{:S(2)}) collective-permute-start(bf16[1024,512]{1,0:T(8,128)(2,1)} %add_convert_fusion.7), channel_id=1, source_target_pairs={{0,2},{2,0},{1,3},{3,1},{4,6},{6,4},{5,7},{7,5},{8,10},{10,8},{9,1... | collective-permute-start | bytes 3145736 | tf_op jit(solution)/shard_map/ppermute | solution.py:45
  436.9 55.6 %all-to-all-start.4 = ((bf16[4,2,256,512]{3,2,1,0:T(8,128)(2,1)}), bf16[4,2,256,512]{3,2,1,0:T(8,128)(2,1)}, u32[]{:S(2)}, u32[]{:S(2)}) async-start(bf16[4,2,256,512]{3,2,1,0:T(8,128)(2,1)} %pad_maximum_fusion), calls=%async_computation.6 | async-start | bytes 4194304 | tf_op jit(solution)/shard_map/all_to_all | solution.py:67
  441.5 81.1 %reduce-scatter.9.cloned.1.call-start = ((), (), s32[]{:S(2)}) async-start(), calls=%async_computation.17 | async-start | bytes 1310720 | tf_op jit(solution)/shard_map/reduce_scatter | solution.py:958
  452.1 26.2 %collective-permute-start.30 = (bf16[1024,512]{1,0:T(8,128)(2,1)S(1)}, bf16[1024,512]{1,0:T(8,128)(2,1)}, u32[]{:S(2)}, u32[]{:S(2)}) collective-permute-start(bf16[1024,512]{1,0:T(8,128)(2,1)S(1)} %convolution_convert_fusion.5), channel_id=1, source_target_pairs={{0,4},{4,0},{1,5},{5,1},{2,6},{6,2},{3,7},{7,3},{8,12},{12,8},{9,1... | collective-permute-start | bytes 3145736 | tf_op jit(solution)/shard_map/ppermute | solution.py:45
  453.3 47.4 %collective-permute-start.32 = (bf16[1024,512]{1,0:T(8,128)(2,1)}, bf16[1024,512]{1,0:T(8,128)(2,1)S(1)}, u32[]{:S(2)}, u32[]{:S(2)}) collective-permute-start(bf16[1024,512]{1,0:T(8,128)(2,1)} %add_convert_fusion.6), channel_id=1, source_target_pairs={{0,4},{4,0},{1,5},{5,1},{2,6},{6,2},{3,7},{7,3},{8,12},{12,8},{9,1... | collective-permute-start | bytes 3145736 | tf_op jit(solution)/shard_map/ppermute | solution.py:45
  454.1 46.5 %collective-permute-start.33 = (bf16[1024,512]{1,0:T(8,128)(2,1)}, bf16[1024,512]{1,0:T(8,128)(2,1)}, u32[]{:S(2)}, u32[]{:S(2)}) collective-permute-start(bf16[1024,512]{1,0:T(8,128)(2,1)} %convolution_convert_fusion.1), channel_id=1, source_target_pairs={{0,2},{2,0},{1,3},{3,1},{4,6},{6,4},{5,7},{7,5},{8,10},{10,8},{9,1... | collective-permute-start | bytes 3145736 | tf_op jit(solution)/shard_map/ppermute | solution.py:45
  504.6 31.0 %all-to-all-start.5 = ((bf16[4,4,128,256]{3,2,1,0:T(8,128)(2,1)}), bf16[4,4,128,256]{3,2,1,0:T(8,128)(2,1)}, u32[]{:S(2)}, u32[]{:S(2)}) async-start(bf16[4,4,128,256]{3,2,1,0:T(8,128)(2,1)} %bitcast.212), calls=%async_computation.7 | async-start | bytes 2097152 | tf_op jit(solution)/shard_map/all_to_all | solution.py:67
  541.7 27.8 %all-to-all-start.6 = ((bf16[4,256,512]{2,1,0:T(8,128)(2,1)}), bf16[4,256,512]{2,1,0:T(8,128)(2,1)}, u32[]{:S(2)}, u32[]{:S(2)}) async-start(bf16[4,256,512]{2,1,0:T(8,128)(2,1)} %bitcast.195), calls=%async_computation.9 | async-start | bytes 2097152 | tf_op jit(solution)/shard_map/all_to_all | solution.py:67
  546.4 56.3 %reduce-scatter.11.cloned.1.call-start = ((), (), s32[]{:S(2)}) async-start(), calls=%async_computation.18 | async-start | bytes 1310720 | tf_op jit(solution)/shard_map/reduce_scatter | solution.py:1005
  (140 other events, 1811.9 us)
Sparse Core Ops, SparseCore 0:
  20.5 28.7 all-gather.5
  54.1 45.3 all-gather.11
  174.1 68.2 all-gather.7
  243.8 44.5 all-gather.9
  300.7 48.9 reduce-scatter.6
  351.9 48.2 reduce-scatter.4
  481.4 27.5 reduce-scatter.8
  573.9 28.3 reduce-scatter.10
